TPU v7x, 32 devices: a whole 2x2x4 slice. The times are simulated.
32 devices in a mesh: freq: 1, tile: 32 (over z, y, x, core).
Axes of the slice: x: 2, y: 2, z: 4, core: 2. Of those that a mesh axis runs over, the one named last changes fastest.
Arguments:
- voltages: bfloat16 [4, 4096, 2, 2048], P(None, ('freq', 'tile')), may hold values from -4 to 4
- scales: int32 [4, 4096, 8], P(None, ('freq', 'tile')), may hold values from 1 to 3
- owner_half: int32 [4, 8], replicated, may hold values from 0 to 1, as said below
Outputs:
- visibilities: float32 [1, 32, 5, 512, 1024], P(None, ('freq', 'tile'))
Inputs may be any that keep to these rules, and one draw needn't show every extreme that they name: owner_half[c, b] + owner_half[c, (b + 4) mod 8] = 1 for every channel c and block b.
All inputs are finite; a program needn't handle non-finite values.
Results may differ from a plain program's by a relative error of at most 0.0026.
Values may be sent and summed in bfloat16 or wider, within the bound.
No kernel may reach another device: no remote copies, remote signals or barrier semaphores. Data moves between devices by JAX's collectives and lax.ppermute only.
A program may use at most 192 MiB of HBM per device.

v0:
```python
import jax
import jax.numpy as jnp
from jax import lax
from jax.sharding import PartitionSpec as P

CHANNELS_PER_BIN = 4
NB = 8


def from_behind(value, axis, by):
    count = lax.axis_size(axis)
    return lax.ppermute(value, axis, [(i, (i + by) % count) for i in range(count)])


def dequantize(voltages, scales):
    chan_count, in_count, re_im, time_len = voltages.shape
    group_count = scales.shape[2]
    shaped = voltages.astype(jnp.float32).reshape(
        chan_count, in_count, re_im, group_count, time_len // group_count
    )
    factor = scales.astype(jnp.float32)[:, :, None, :, None]
    return (shaped * factor).astype(jnp.bfloat16).reshape(chan_count, in_count, re_im, time_len)


def send_buffer(local_x, freq_count, blk_stride):
    chan_count, in_count, re_im, time_len = local_x.shape
    per_block = in_count // NB
    per_chan = chan_count // freq_count
    baseline_count = NB // blk_stride
    blocks = local_x.reshape(freq_count, per_chan, per_block, NB, re_im, time_len)
    blocks = blocks.reshape(
        freq_count, per_chan, per_block, baseline_count, blk_stride, re_im, time_len
    )
    blocks = blocks.transpose(0, 4, 1, 3, 2, 5, 6)
    return blocks.reshape(
        freq_count * blk_stride * per_chan, baseline_count, per_block, re_im, time_len
    )


def unpack(received):
    sender_count, baseline_count, per_block, re_im, time_len = received.shape
    return received.transpose(1, 0, 2, 3, 4).reshape(
        baseline_count, sender_count * per_block, re_im, time_len
    )


def right_side(own_blocks):
    swapped = jnp.stack([own_blocks[:, :, 1], -own_blocks[:, :, 0]], axis=2)
    return jnp.concatenate([own_blocks, swapped], axis=1)


def tile_product(rows_blk, right_blk):
    return jnp.einsum("rmkt,rnkt->rmn", rows_blk, right_blk, preferred_element_type=jnp.float32)


def roll_fix(received, base, wrap_cut, tile_pos):
    return jnp.where(
        tile_pos < wrap_cut, jnp.roll(received, base + 1, axis=0), jnp.roll(received, base, axis=0)
    )


def shards(voltages, scales, owner_half):
    time_len = voltages.shape[3]
    freq_count = lax.axis_size("freq")
    tile_count = lax.axis_size("tile")
    blk_stride = tile_count // CHANNELS_PER_BIN
    half_span = NB // 2
    inverse_map = 1.0 / time_len
    tile_pos = lax.axis_index("tile")
    chan_idx = lax.axis_index("freq") * CHANNELS_PER_BIN + tile_pos % CHANNELS_PER_BIN
    own_row = lax.dynamic_slice_in_dim(owner_half, chan_idx, 1, 0)
    flags = lax.dynamic_slice_in_dim(own_row, tile_pos // CHANNELS_PER_BIN, 1, 1)[:, 0]
    local_x = dequantize(voltages, scales)
    received = lax.all_to_all(
        send_buffer(local_x, freq_count, blk_stride),
        ("freq", "tile"),
        split_axis=0,
        concat_axis=0,
        tiled=True,
    )
    own_blocks = unpack(received)
    held = [own_blocks]
    rows_blk = own_blocks
    for distance in range(1, half_span + 1):
        moved = from_behind(rows_blk, "tile", CHANNELS_PER_BIN)
        rows_blk = roll_fix(moved, 0, CHANNELS_PER_BIN, tile_pos)
        held.append(rows_blk)
    right_blk = right_side(own_blocks)
    tiles = []
    for distance in range(half_span):
        tiles.append(tile_product(held[distance], right_blk) * inverse_map)
    last_tile = tile_product(held[half_span], right_blk) * inverse_map
    last_tile = jnp.where(flags[:, None, None] == 1, last_tile, jnp.zeros_like(last_tile))
    tiles.append(last_tile)
    return jnp.stack(tiles, axis=1)[:, None]


def solution(mesh):
    in_specs = (P(None, ("freq", "tile"), None, None), P(None, ("freq", "tile"), None), P())
    out_specs = P(None, ("freq", "tile"), None, None, None)
    return jax.shard_map(shards, mesh=mesh, in_specs=in_specs, out_specs=out_specs, check_vma=False)
```

profile of v0, /device:TPU:0, one launch (start us, length us, event | category | flops | bytes accessed | tf_op | source)
XLA Modules:
  0.0 520.9 jit_solution(8718707958596883026)
XLA Ops:
  0.0 0.7 convert_element_type.14
  0.7 0.1 copy.10
  0.9 2.6 mul.40
  3.5 4.9 mul.41
  8.3 6.6 %copy.11 = f32[4,16,8,2048]{3,1,0,2:T(8,128)} copy(f32[4,16,8,2048]{3,2,1,0:T(8,128)} %mul.41) | data formatting | bytes 8388608 | tf_op jit(solution)/shard_map/mul | solution.py:22
  14.9 10.2 %convert.1 = f32[1,4,16,1,8,2,2048]{6,5,4,2,1,3,0:T(2,128)} convert(bf16[1,4,16,1,8,2,2048]{6,5,4,2,1,3,0:T(2,128)(2,1)} %bitcast.80) | non-fusion elementwise | flops 2097152 | bytes 12582912 | tf_op jit(solution)/shard_map/reshape | solution.py:18
  25.1 9.5 %fusion = bf16[1,4,16,1,8,2,2048]{6,2,5,1,4,3,0:T(8,128)(2,1)S(1)} fusion(f32[1,4,16,1,8,2,2048]{6,5,4,2,1,3,0:T(2,128)} %convert.1, f32[4,16,8,2048]{3,1,0,2:T(8,128)} %copy.11), kind=kLoop, calls=%fused_computation.2 | loop fusion | flops 4194304 | bytes 16777216 | tf_op jit(solution)/shard_map/convert_element_type | solution.py:22
  34.6 100.8 %all_to_all.5 = bf16[32,1,16,2,2048]{4,2,3,1,0:T(8,128)(2,1)S(1)} all-to-all(bf16[32,1,16,2,2048]{4,2,3,1,0:T(8,128)(2,1)S(1)} %bitcast.79), channel_id=1, replica_groups=mesh['freq'=1,'tile'=32] {'freq','tile'}, dimensions={0} | all-to-all | bytes 8388608 | tf_op jit(solution)/shard_map/all_to_all | solution.py:74
  135.3 0.6 copy.13
  135.9 0.0 copy-start
  135.9 2.0 copy-done
  137.9 1.5 collective-permute-start
  139.4 93.0 %collective-permute-done = bf16[1,512,2,2048]{3,1,2,0:T(8,128)(2,1)S(1)} collective-permute-done((bf16[1,512,2,2048]{3,1,2,0:T(8,128)(2,1)S(1)}, bf16[1,512,2,2048]{3,1,2,0:T(8,128)(2,1)S(1)}, u32[]{:S(2)}, u32[]{:S(2)}) %collective-permute-start) | collective-permute-done | bytes 4194336 | tf_op jit(solution)/shard_map/ppermute | solution.py:12
  232.5 0.0 copy-start.2
  232.5 1.9 copy-done.2
  234.4 0.0 collective-permute-start.1
  234.4 93.7 %collective-permute-done.1 = bf16[1,512,2,2048]{3,1,2,0:T(8,128)(2,1)} collective-permute-done((bf16[1,512,2,2048]{3,1,2,0:T(8,128)(2,1)S(1)}, bf16[1,512,2,2048]{3,1,2,0:T(8,128)(2,1)}, u32[]{:S(2)}, u32[]{:S(2)}) %collective-permute-start.1) | collective-permute-done | bytes 4194336 | tf_op jit(solution)/shard_map/ppermute | solution.py:12
  328.1 0.0 collective-permute-start.2
  328.1 1.3 dynamic_slice.4
  330.0 0.0 copy-start.1
  330.0 2.6 fusion.18
  332.7 88.4 %collective-permute-done.2 = bf16[1,512,2,2048]{3,1,2,0:T(8,128)(2,1)} collective-permute-done((bf16[1,512,2,2048]{3,1,2,0:T(8,128)(2,1)}, bf16[1,512,2,2048]{3,1,2,0:T(8,128)(2,1)}, u32[]{:S(2)}, u32[]{:S(2)}) %collective-permute-start.2) | collective-permute-done | bytes 4194336 | tf_op jit(solution)/shard_map/ppermute | solution.py:12
  421.1 0.0 collective-permute-start.3
  421.1 0.0 copy-done.1
  421.1 0.0 copy-start.3
  421.1 8.0 %bitcast_dynamic-update-slice_fusion.4 = f32[1,5,512,1024]{3,2,1,0:T(8,128)} fusion(bf16[512,2,2048]{2,0,1:T(8,128)(2,1)S(1)} %bitcast.73, bf16[1,512,1,2048]{3,1,2,0:T(8,128)(2,1)S(1)} %get-tuple-element.6, bf16[1,512,1,2048]{3,1,2,0:T(8,128)(2,1)S(1)} %get-tuple-element.5, bf16[1,512,2,2048]{3,1,2,0:T(8,128)(2,1)S(1)} %bitcast.74), kind=kOutput, calls=%fused_computation.21 | convolution fusion | flops 4320657408 | bytes 14680064 | tf_op jit(solution)/shard_map/rmkt,rnkt->rmn/dot_general | solution.py:53
  429.1 0.0 copy-done.3
  429.1 8.0 %bitcast_dynamic-update-slice_fusion.3 = f32[1,5,512,1024]{3,2,1,0:T(8,128)} fusion(f32[1,5,512,1024]{3,2,1,0:T(8,128)} %bitcast_dynamic-update-slice_fusion.4, bf16[1,512,2,2048]{3,1,2,0:T(8,128)(2,1)S(1)} %copy-done.3, bf16[1,512,1,2048]{3,1,2,0:T(8,128)(2,1)S(1)} %get-tuple-element.6, bf16[1,512,1,2048]{3,1,2,0:T(8,128)(2,1)S(1)} %get-tuple-element.5, ...), kind=kOutput, calls=%fused_computation.19 | convolution fusion | flops 4320657408 | bytes 14680064 | tf_op jit(solution)/shard_map/rmkt,rnkt->rmn/dot_general | solution.py:53
  437.1 8.1 %bitcast_dynamic-update-slice_fusion.2 = f32[1,5,512,1024]{3,2,1,0:T(8,128)} fusion(f32[1,5,512,1024]{3,2,1,0:T(8,128)} %bitcast_dynamic-update-slice_fusion.3, bf16[1,512,2,2048]{3,1,2,0:T(8,128)(2,1)} %collective-permute-done.1, bf16[1,512,1,2048]{3,1,2,0:T(8,128)(2,1)S(1)} %get-tuple-element.6, bf16[1,512,1,2048]{3,1,2,0:T(8,128)(2,1)S(1)} %get-tuple-element.5, ...), kind=kOutput, calls=%fused_computation.17 | convolution fusion | flops 4320657408 | bytes 14680064 | tf_op jit(solution)/shard_map/rmkt,rnkt->rmn/dot_general | solution.py:53
  445.2 8.1 %bitcast_dynamic-update-slice_fusion.1 = f32[1,5,512,1024]{3,2,1,0:T(8,128)} fusion(f32[1,5,512,1024]{3,2,1,0:T(8,128)} %bitcast_dynamic-update-slice_fusion.2, bf16[1,512,2,2048]{3,1,2,0:T(8,128)(2,1)} %collective-permute-done.2, bf16[1,512,1,2048]{3,1,2,0:T(8,128)(2,1)S(1)} %get-tuple-element.6, bf16[1,512,1,2048]{3,1,2,0:T(8,128)(2,1)S(1)} %get-tuple-element.5, ...), kind=kOutput, calls=%fused_computation.15 | convolution fusion | flops 4320657408 | bytes 14680064 | tf_op jit(solution)/shard_map/rmkt,rnkt->rmn/dot_general | solution.py:53
  453.2 59.8 %collective-permute-done.3 = bf16[1,512,2,2048]{3,1,2,0:T(8,128)(2,1)S(1)} collective-permute-done((bf16[1,512,2,2048]{3,1,2,0:T(8,128)(2,1)}, bf16[1,512,2,2048]{3,1,2,0:T(8,128)(2,1)S(1)}, u32[]{:S(2)}, u32[]{:S(2)}) %collective-permute-start.3) | collective-permute-done | bytes 4194336 | tf_op jit(solution)/shard_map/ppermute | solution.py:12
  513.0 7.9 %bitcast_dynamic-update-slice_fusion = f32[1,5,512,1024]{3,2,1,0:T(8,128)} fusion(f32[1,5,512,1024]{3,2,1,0:T(8,128)} %bitcast_dynamic-update-slice_fusion.1, bf16[1,512,2,2048]{3,1,2,0:T(8,128)(2,1)S(1)} %collective-permute-done.3, pred[]{:T(512)} %bitcast.17, bf16[1,512,1,2048]{3,1,2,0:T(8,128)(2,1)S(1)} %get-tuple-element.6, ...), kind=kOutput, calls=%fused_computation.12 | convolution fusion | flops 4321181696 | bytes 14680576 | tf_op jit(solution)/shard_map/rmkt,rnkt->rmn/dot_general | solution.py:53
Async XLA Ops:
  135.9 2.0 copy-start
  137.9 94.5 %collective-permute-start = (bf16[1,512,2,2048]{3,1,2,0:T(8,128)(2,1)S(1)}, bf16[1,512,2,2048]{3,1,2,0:T(8,128)(2,1)S(1)}, u32[]{:S(2)}, u32[]{:S(2)}) collective-permute-start(bf16[1,512,2,2048]{3,1,2,0:T(8,128)(2,1)S(1)} %bitcast.71), channel_id=1, source_target_pairs={{0,4},{1,5},{2,6},{3,7},{4,8},{5,9},{6,10},{7,11},{8,12},{9,13},{1... | collective-permute-start | bytes 12582920 | tf_op jit(solution)/shard_map/ppermute | solution.py:12
  232.5 1.9 copy-start.2
  234.4 93.7 %collective-permute-start.1 = (bf16[1,512,2,2048]{3,1,2,0:T(8,128)(2,1)S(1)}, bf16[1,512,2,2048]{3,1,2,0:T(8,128)(2,1)}, u32[]{:S(2)}, u32[]{:S(2)}) collective-permute-start(bf16[1,512,2,2048]{3,1,2,0:T(8,128)(2,1)S(1)} %collective-permute-done), channel_id=1, source_target_pairs={{0,4},{1,5},{2,6},{3,7},{4,8},{5,9},{6,10},{7,11},{8,12},{9,13},{1... | collective-permute-start | bytes 12582920 | tf_op jit(solution)/shard_map/ppermute | solution.py:12
  328.1 93.0 %collective-permute-start.2 = (bf16[1,512,2,2048]{3,1,2,0:T(8,128)(2,1)}, bf16[1,512,2,2048]{3,1,2,0:T(8,128)(2,1)}, u32[]{:S(2)}, u32[]{:S(2)}) collective-permute-start(bf16[1,512,2,2048]{3,1,2,0:T(8,128)(2,1)} %collective-permute-done.1), channel_id=1, source_target_pairs={{0,4},{1,5},{2,6},{3,7},{4,8},{5,9},{6,10},{7,11},{8,12},{9,13},{1... | collective-permute-start | bytes 12582920 | tf_op jit(solution)/shard_map/ppermute | solution.py:12
  330.0 91.1 %copy-start.1 = (bf16[32,1,16,2,2048]{4,2,0,3,1:T(8,128)(2,1)S(1)}, bf16[32,1,16,2,2048]{4,2,0,3,1:T(8,128)(2,1)}, u32[]{:S(2)}) copy-start(bf16[32,1,16,2,2048]{4,2,0,3,1:T(8,128)(2,1)} %copy-done) | copy-start | bytes 12582916
  421.1 92.0 %collective-permute-start.3 = (bf16[1,512,2,2048]{3,1,2,0:T(8,128)(2,1)}, bf16[1,512,2,2048]{3,1,2,0:T(8,128)(2,1)S(1)}, u32[]{:S(2)}, u32[]{:S(2)}) collective-permute-start(bf16[1,512,2,2048]{3,1,2,0:T(8,128)(2,1)} %collective-permute-done.2), channel_id=1, source_target_pairs={{0,4},{1,5},{2,6},{3,7},{4,8},{5,9},{6,10},{7,11},{8,12},{9,13},{1... | collective-permute-start | bytes 12582920 | tf_op jit(solution)/shard_map/ppermute | solution.py:12
  421.1 8.0 %copy-start.3 = (bf16[1,512,2,2048]{3,1,2,0:T(8,128)(2,1)S(1)}, bf16[1,512,2,2048]{3,1,2,0:T(8,128)(2,1)}, u32[]{:S(2)}) copy-start(bf16[1,512,2,2048]{3,1,2,0:T(8,128)(2,1)} %copy-done.2) | copy-start | bytes 12582916
where the time goes:
time: 522 us; the launch traced here: 521 us
  waiting for transfers between devices  335 us (64%)
  blocking collectives  101 us (19%)
  matrix products  40 us (8%)
  other arithmetic  23 us (4%)
  local copies, waits for them, and re-layouts  20 us (4%)
    ppermute x4, waiting for transfers between devices, from_behind(): lax.ppermute(value, axis, [(i, (i + by) % count) for i in range(count)])  335 us
    all_to_all x1, blocking collectives, shards(): lax.all_to_all(send_buffer(local_x, freq_count, blk_stride), ('freq', 'ti...  101 us
    dot_general x5, matrix products, tile_product(): jnp.einsum('rmkt,rnkt->rmn', rows_blk, right_blk, preferred_element_type=...  40 us
    mul x3, local copies, waits for them, and re-layouts, dequantize(): shaped * factor  14.1 us
  transfers between devices with their start and end apart: 4, of which 4 were waited for; matrix products, arithmetic and copies ran while one was open for 7% of the time, Pallas kernels for 0%

commit v1 on v0

v1 whole, which is shorter than its diff:
```python
import functools

import jax
import jax.numpy as jnp
from jax import lax
from jax.experimental import pallas as pl
from jax.experimental.pallas import tpu as pltpu
from jax.sharding import PartitionSpec as P

CHANNELS_PER_BIN = 4
NB = 8
LINES = 2
DEPTH = NB // LINES
HALF = NB // 2
UP = (2, 3, 4, 5, 6, 7)
DOWN = (4, 5, 6, 7, 0, 1)
SHORT_UP = (0, 1)
SHORT_DOWN = (2, 3)
PARTS = 4
EXCHANGES = ((0, 1), (1, 4))
STEPS = ((0, 0), (0, 1), (1, 0), (0, 2), (1, 1), (2, 0), (1, 2), (3, 0), (2, 1), (3, 1), (2, 2), (3, 2))
GATHERS = {0: (0,), 2: (1,), 4: (2,), 5: (3,)}
TILES = {7: (0,), 9: (1,), 13: (2, 3)}
SIDE = 6
VMEM_BYTES = 56 * 1024 * 1024
STEP_BYTES = 4_000_000

KINDS = range(2 * NB)


def place(kind):
    return kind // 4, kind // 2 % 2, kind % 2


def along(name, kind):
    z, y, parity = place(kind)
    step = 1 if (name == "a") == (parity == 0) else -1
    if 0 <= z + step < DEPTH:
        return 4 * (z + step) + 2 * y + parity, True
    return 4 * z + 2 * y + 1 - parity, False


def upward(parity):
    return "a" if parity == 0 else "b"


def downward(parity):
    return "b" if parity == 0 else "a"


def my_kind(lanes):
    me = lax.axis_index("tile")
    return me // lanes * 2 + me % 2


def needed(u):
    return [(u - s) % NB for s in range(HALF + 1)]


def device_pairs(step, positions, lanes):
    pairs = []
    for g in range(positions):
        kind = step(g // lanes * 2 + g % 2)
        pairs.append((g, kind // 2 * lanes + g % lanes // 2 * 2 + kind % 2))
    return pairs


class Plan:
    def __init__(self):
        self.held = {}

    def own(self, name, part, blocks):
        self.held[name] = [[(part,) + place(k)[:2] + (b,) for b in blocks(place(k)[2])] for k in KINDS]

    def move(self, source, target, step):
        got = [None] * len(KINDS)
        for kind in KINDS:
            goal, useful = step(kind)
            items = self.held[source][kind]
            got[goal] = list(items) if useful else [None] * len(items)
        self.held[target] = got

    def find(self, kind, item, names):
        for name in names:
            if item in self.held[name][kind]:
                return name, self.held[name][kind].index(item)
        return None


def runs(picks):
    out = []
    for dst, name, src in picks:
        if out and out[-1][1] == name and out[-1][0] + out[-1][3] == dst and out[-1][2] + out[-1][3] == src:
            out[-1][3] += 1
        else:
            out.append([dst, name, src, 1])
    return [tuple(r) for r in out]


def copies_kernel(names, after, plan, patched, outs, lanes, *refs):
    ins = dict(zip(names, refs[: len(names)]))
    targets = dict(zip(list(patched) + list(outs), refs[len(names) + 1 + after : -3]))
    through, sems = refs[-2:]
    me = my_kind(lanes)
    for kind, todo in plan.items():

        @pl.when(me == kind)
        def _(todo=todo):
            started, onward, at = [], [], 0
            for i, (target, dst, name, src, length) in enumerate(todo):
                goal = targets[target].at[pl.ds(dst, length)]
                if target in patched:
                    onward.append((i, through.at[pl.ds(at, length)], goal))
                    goal = through.at[pl.ds(at, length)]
                    at += length
                copy = pltpu.make_async_copy(ins[name].at[pl.ds(src, length)], goal, sems.at[0, i])
                copy.start()
                started.append(copy)
            for copy in started:
                copy.wait()
            started = [pltpu.make_async_copy(src, goal, sems.at[1, i]) for i, src, goal in onward]
            for copy in started:
                copy.start()
            for copy in started:
                copy.wait()


def run_copies(arrays, names, after, plan, patched, outs, lanes):
    shape = arrays["a0.0"].shape[1:]
    dtype = arrays["a0.0"].dtype
    any_spec = pl.BlockSpec(memory_space=pl.ANY)
    out_shape = [jax.ShapeDtypeStruct(arrays[n].shape, dtype) for n in patched]
    out_shape += [jax.ShapeDtypeStruct((slots,) + shape, dtype) for slots in outs.values()]
    most = max(1, max(len(todo) for todo in plan.values()))
    token = arrays["token"]
    aliases = {names.index(n): i for i, n in enumerate(patched)}
    aliases[len(names)] = len(out_shape)
    got = pl.pallas_call(
        functools.partial(copies_kernel, names, len(after), plan, patched, list(outs), lanes),
        out_shape=out_shape + [jax.ShapeDtypeStruct(token.shape, token.dtype)],
        in_specs=[any_spec] * (len(names) + 1 + len(after)),
        out_specs=[any_spec] * len(patched) + [pl.BlockSpec(memory_space=pltpu.VMEM)] * len(outs) + [any_spec],
        scratch_shapes=[pltpu.VMEM((4,) + shape, dtype), pltpu.SemaphoreType.DMA((2, most))],
        input_output_aliases=aliases,
        compiler_params=pltpu.CompilerParams(vmem_limit_bytes=VMEM_BYTES),
        cost_estimate=pl.CostEstimate(flops=0, bytes_accessed=STEP_BYTES, transcendentals=0),
        name="pick",
    )(*[arrays[n] for n in names], token, *[arrays[n] for n in after])
    for n, value in zip(list(patched) + list(outs) + ["token"], got):
        arrays[n] = value


def gather_kernel(plan, lanes, start, own, token, a, b, token_out, sems):
    senders, rows = own.shape[0], own.shape[4]
    targets = {"a": a, "b": b}
    me = my_kind(lanes)
    for kind, todo in plan.items():

        @pl.when(me == kind)
        def _(todo=todo):
            started = []
            for lane in range(senders):
                at = pl.ds(lane * rows, rows)
                for i, (target, dst, src, length) in enumerate(todo):
                    copy = pltpu.make_async_copy(
                        own.at[lane, pl.ds(src, length), :, :, :, pl.ds(start, a.shape[-1])],
                        targets[target].at[pl.ds(dst, length), :, :, at],
                        sems.at[lane, i],
                    )
                    copy.start()
                    started.append(copy)
            for copy in started:
                copy.wait()


def run_gather(arrays, part, own, start, samples, plan, lanes):
    senders, _, two, split, rows, _ = own.shape
    shape = (two, split, senders * rows, samples)
    token = arrays["token"]
    any_spec = pl.BlockSpec(memory_space=pl.ANY)
    vmem_spec = pl.BlockSpec(memory_space=pltpu.VMEM)
    most = max(len(todo) for todo in plan.values())
    arrays["a0.%d" % part], arrays["b0.%d" % part], arrays["token"] = pl.pallas_call(
        functools.partial(gather_kernel, plan, lanes, start),
        out_shape=[jax.ShapeDtypeStruct((n,) + shape, own.dtype) for n in (len(UP), len(DOWN))]
        + [jax.ShapeDtypeStruct(token.shape, token.dtype)],
        in_specs=[any_spec] * 2,
        out_specs=[vmem_spec] * 2 + [any_spec],
        scratch_shapes=[pltpu.SemaphoreType.DMA((senders, most))],
        input_output_aliases={1: 2},
        compiler_params=pltpu.CompilerParams(vmem_limit_bytes=VMEM_BYTES),
        cost_estimate=pl.CostEstimate(flops=0, bytes_accessed=0, transcendentals=0),
        name="gather",
    )(own, token)


def tiles_kernel(names, plan, lanes, scale, first, last, *refs):
    ins = dict(zip(names, refs[: len(names)]))
    refs = refs[len(names) :]
    flag = acc = None
    if last:
        flag, refs = refs[0], refs[1:]
    if not first:
        acc, refs = refs[0], refs[1:]
    _, out, _, held, sems = refs
    me = my_kind(lanes)
    s = pl.program_id(0)

    @pl.when(s == 0)
    def _():
        for kind, todo in plan.items():

            @pl.when(me == kind)
            def _(todo=todo):
                for slot, row, name, src in todo:
                    pltpu.make_async_copy(ins[name].at[src], held.at[slot, :, :, row], sems.at[slot, row]).start()

    for row in range(NB):
        pltpu.make_async_copy(held.at[s, :, :, row], held.at[s, :, :, row], sems.at[s, row]).wait()
    rows = held.shape[2] * held.shape[3] * held.shape[4]
    samples = held.shape[5]

    def mul(a, b):
        return lax.dot_general(a, b, (((1,), (1,)), ((), ())), preferred_element_type=jnp.float32)

    ar = held[s, 0].reshape(rows, samples)
    ai = held[s, 1].reshape(rows, samples)
    br = held[0, 0].reshape(rows, samples)
    bi = held[0, 1].reshape(rows, samples)
    real = (mul(ar, br) + mul(ai, bi)) * scale
    imag = (mul(ar, bi) - mul(ai, br)) * scale
    if not first:
        real = real + acc[0, :, :rows]
        imag = imag + acc[0, :, rows:]
    if last:
        keep = jnp.logical_or(s < HALF, flag[0] == 1)
        real = jnp.where(keep, real, 0.0)
        imag = jnp.where(keep, imag, 0.0)
    out[0, :, :rows] = real
    out[0, :, rows:] = imag


def run_tiles(arrays, names, plan, lanes, scale, acc, flag):
    token = arrays["token"]
    shape = arrays[names[0]].shape[1:]
    rows = shape[1] * shape[2] * NB
    samples = shape[3]
    any_spec = pl.BlockSpec(memory_space=pl.ANY)
    tile_spec = pl.BlockSpec((1, rows, 2 * rows), lambda s: (s, 0, 0))
    operands = [arrays[n] for n in names]
    in_specs = [any_spec] * len(names)
    aliases = {}
    if flag is not None:
        operands.append(flag)
        in_specs.append(pl.BlockSpec(memory_space=pltpu.SMEM))
    if acc is not None:
        aliases = {len(operands): 0}
        operands.append(acc)
        in_specs.append(tile_spec)
    aliases[len(operands)] = 1
    operands.append(token)
    in_specs.append(any_spec)
    held = (HALF + 1, 2, shape[1], NB, shape[2], samples)
    result, arrays["token"] = pl.pallas_call(
        functools.partial(tiles_kernel, names, plan, lanes, scale, acc is None, flag is not None),
        grid=(HALF + 1,),
        out_shape=[
            jax.ShapeDtypeStruct((HALF + 1, rows, 2 * rows), jnp.float32),
            jax.ShapeDtypeStruct(token.shape, token.dtype),
        ],
        in_specs=in_specs,
        out_specs=[tile_spec, any_spec],
        scratch_shapes=[pltpu.VMEM(held, jnp.bfloat16), pltpu.SemaphoreType.DMA((HALF + 1, NB))],
        input_output_aliases=aliases,
        compiler_params=pltpu.CompilerParams(vmem_limit_bytes=VMEM_BYTES),
        cost_estimate=pl.CostEstimate(flops=0, bytes_accessed=0, transcendentals=0),
        name="tiles",
    )(*operands)
    return result


def dequantize(voltages, scales):
    groups = scales.shape[-1]
    shaped = voltages.reshape(voltages.shape[:-1] + (groups, voltages.shape[-1] // groups))
    product = shaped.astype(jnp.float32) * scales.astype(jnp.float32)[..., None]
    return product.astype(jnp.bfloat16).reshape(voltages.shape)


def exchange(voltages, scales, freq_count, lanes):
    samples = voltages.shape[3]
    rows = voltages.shape[1] // NB
    split = (freq_count, lanes, rows, NB)
    x = dequantize(voltages.reshape(split + (2, samples)), scales.reshape(split + (1, scales.shape[2])))
    x = x.transpose(1, 3, 4, 0, 2, 5)
    if freq_count > 1:
        x = lax.all_to_all(x, "freq", 3, 3, tiled=True)
    positions = lax.axis_size("tile")
    groups = [list(range(g, g + lanes)) for g in range(0, positions, lanes)]
    x = lax.all_to_all(x, "tile", 0, 0, axis_index_groups=groups, tiled=True)
    if freq_count > 1:
        x = x.transpose(1, 2, 3, 0, 4, 5)
        x = x.reshape((1,) + x.shape[:3] + (lanes * rows, samples))
    return x


class Turn:
    def __init__(self, owns, lanes):
        self.owns, self.lanes = owns, lanes
        self.positions = lax.axis_size("tile")
        self.plan = Plan()
        self.arrays = {"token": jnp.zeros((8, 128), jnp.int32)}
        for part in range(len(owns)):
            self.plan.own("blocks.%d" % part, part, lambda parity: range(NB))
            self.plan.own("a0.%d" % part, part, lambda parity: DOWN if parity else UP)
            self.plan.own("b0.%d" % part, part, lambda parity: UP if parity else DOWN)
        self.sent = [set() for _ in KINDS]
        self.here = []
        self.crossed = []

    def move(self, source, target, step):
        self.plan.move(source, target, step)
        pairs = device_pairs(lambda kind: step(kind)[0], self.positions, self.lanes)
        self.arrays[target] = lax.ppermute(self.arrays[source], "tile", pairs)

    def gather(self, part):
        todo = {}
        for kind in KINDS:
            todo[kind] = []
            for name in "ab":
                blocks = [item[3] for item in self.plan.held["%s0.%d" % (name, part)][kind]]
                for d, _, src, length in runs([(i, "", b) for i, b in enumerate(blocks)]):
                    todo[kind].append((name, d, src, length))
        run_gather(self.arrays, part, *self.owns[part], todo, self.lanes)
        self.here += ["a0.%d" % part, "b0.%d" % part]

    def along(self, part, stage):
        for name in "ab":
            self.move("%s%d.%d" % (name, stage, part), "%s%d.%d" % (name, stage + 1, part), functools.partial(along, name))

    def arrived(self, part, stage):
        names = ["%s%d.%d" % (name, stage, part) for name in "ab"]
        self.here += names
        return names

    def choose(self, kind, most, parts):
        wanted = []
        y = place(kind)[1]
        for part in parts:
            for source in range(DEPTH):
                for b in needed(kind // 2 ^ 1):
                    item = (part, source, y, b)
                    where = self.plan.find(kind, item, self.here)
                    if item not in self.sent[kind] and where and len(wanted) < most:
                        wanted.append((item, where))
        wanted.sort(key=lambda w: w[1])
        self.sent[kind].update(w[0] for w in wanted)
        return wanted

    def prepare(self, part=None, stage=None, side=None, after=(), parts=None):
        todo = {kind: [] for kind in KINDS}
        patched, outs = [], {}
        if part is not None:
            patched = ["%s%d.%d" % (name, stage, part) for name in "ab"]
        if stage:
            for kind in KINDS:
                z, y, parity = place(kind)
                for low, way, blocks in ((z, upward, SHORT_UP), (DEPTH - 1 - z, downward, SHORT_DOWN)):
                    if low == stage - 1:
                        target, dst = "%s%d.%d" % (way(parity), stage, part), 2 * (stage - 1)
                        items = [(part, z, y, b) for b in blocks]
                        found = [self.plan.find(kind, item, ["a0.%d" % part, "b0.%d" % part]) for item in items]
                        for d, name, src, length in runs([(dst + i, n, k) for i, (n, k) in enumerate(found)]):
                            todo[kind].append((target, d, name, src, length))
                        self.plan.held[target][kind][dst : dst + len(items)] = items
        if side is not None:
            name, most = side
            chosen = [self.choose(kind, most, range(len(self.owns)) if parts is None else parts) for kind in KINDS]
            slots = max(len(c) for c in chosen)
            outs = {"side" + name: slots}
            for kind in KINDS:
                self.plan.held.setdefault("side" + name, []).append(
                    [w[0] for w in chosen[kind]] + [None] * (slots - len(chosen[kind]))
                )
                picks = [(i, n, k) for i, (_, (n, k)) in enumerate(chosen[kind])]
                todo[kind] += [("side" + name,) + r for r in runs(picks)]
        used = {t[2] for kind in KINDS for t in todo[kind]}
        names = [n for n in self.here if n in used or n in patched]
        after = [n for n in after if n not in names]
        run_copies(self.arrays, names, after, todo, patched, outs, self.lanes)
        if side is not None:
            self.move("side" + name, "got" + name, lambda kind: (kind ^ 2, True))
            self.crossed.append("got" + name)

    def tiles(self, part, scale, result, flag):
        names = [n for n in self.here if n.endswith(".%d" % part)] + self.crossed
        todo = {}
        for kind in KINDS:
            todo[kind] = []
            for s, b in enumerate(needed(kind // 2)):
                for row in range(NB):
                    where = self.plan.find(kind, (part, row // 2, row % 2, b), names)
                    assert where is not None
                    todo[kind].append((s, row) + where)
        used = {t[2] for kind in KINDS for t in todo[kind]}
        return run_tiles(self.arrays, [n for n in names if n in used], todo, self.lanes, scale, result, flag)


def shards(voltages, scales, owner_half):
    time_len = voltages.shape[3]
    group_len = time_len // scales.shape[2]
    freq_count = lax.axis_size("freq")
    lanes = CHANNELS_PER_BIN
    tile_pos = lax.axis_index("tile")
    chan_idx = lax.axis_index("freq") * lanes + tile_pos % lanes
    flag = lax.dynamic_slice(owner_half, (chan_idx, tile_pos // lanes), (1, 1)).reshape(1)
    samples = time_len // PARTS
    owns = []
    for first, last in EXCHANGES:
        start, stop = first * samples, last * samples
        own = exchange(
            voltages[..., start:stop], scales[..., start // group_len : stop // group_len], freq_count, lanes
        )
        owns += [(own, (part - first) * samples, samples) for part in range(first, last)]
    scale = 1.0 / time_len
    turn = Turn(owns, lanes)
    result = None
    known = 0
    for n, (part, stage) in enumerate(STEPS):
        for fresh in GATHERS.get(n, ()):
            turn.gather(fresh)
        done = []
        while known < n and (known <= n - 2 or STEPS[known][0] == part):
            done += turn.arrived(STEPS[known][0], STEPS[known][1] + 1)
            known += 1
        if n >= 2:
            done = done + ["got%d" % (n - 2)]
        turn.prepare(part, stage, side=(str(n), SIDE), after=done)
        turn.along(part, stage)
        for ready in TILES.get(n, ()):
            result = turn.tiles(ready, scale, result, None)
    for n in (len(STEPS), len(STEPS) + 1):
        done = ["got%d" % (n - 2)]
        while known < n - 1:
            done += turn.arrived(STEPS[known][0], STEPS[known][1] + 1)
            known += 1
        turn.prepare(side=(str(n), SIDE if n == len(STEPS) else 99), after=done)
    for ready in TILES.get(n, ()):
        result = turn.tiles(ready, scale, result, flag if ready == PARTS - 1 else None)
    return result[None, None]


def solution(mesh):
    in_specs = (P(None, ("freq", "tile"), None, None), P(None, ("freq", "tile"), None), P())
    out_specs = P(None, ("freq", "tile"), None, None, None)
    return jax.shard_map(shards, mesh=mesh, in_specs=in_specs, out_specs=out_specs, check_vma=False)
```

time: 522 us -> 318 us (0.61)
  waiting for transfers between devices: 335 us -> 135 us
  blocking collectives: 101 us -> 0 us
  Pallas kernels: 0 us -> 93.8 us
  starting transfers between devices: 1.48 us -> 47.4 us
  matrix products: 40 us -> 0 us
  other arithmetic: 23 us -> 12.8 us
  local copies, waits for them, and re-layouts: 20 us -> 27.7 us
    ppermute x4 -> x38, waiting for transfers between devices: 335 us -> 131 us  [move(): self.arrays[target] = lax.ppermute(self.arrays[source], 'tile', pairs)]
    all_to_all x1 -> x0, blocking collectives: 101 us -> none  [shards(): lax.all_to_all(send_buffer(local_x, freq_count, blk_stride), ('freq', 'ti...]
    pallas_call x0 -> x22, Pallas kernels: none -> 93.8 us  [the longest x4 50.3 us: run_tiles(): pl.pallas_call(functools.partial(tiles_kernel, names, plan, lanes, scale,...]
    dot_general x5 -> x0, matrix products: 40 us -> none  [tile_product(): jnp.einsum('rmkt,rnkt->rmn', rows_blk, right_blk, preferred_element_type=...]
    ppermute x4 -> x38, starting transfers between devices: 1.48 us -> 39.3 us  [move(): self.arrays[target] = lax.ppermute(self.arrays[source], 'tile', pairs)]
    unnamed x8 -> x76, local copies, waits for them, and re-layouts: 3.96 us -> 16.5 us
    reshape x1 -> x0, other arithmetic: 10.2 us -> none  [dequantize(): voltages.astype(jnp.float32)]
    mul x3 -> x4, local copies, waits for them, and re-layouts: 14.1 us -> 4.7 us  [dequantize(): product = shaped.astype(jnp.float32) * scales.astype(jnp.float32)[..., None]]
  transfers between devices with their start and end apart: 4 -> 40, of which waited for: 4 -> 23; matrix products, arithmetic and copies ran while one was open for 7% -> 4% of each run, Pallas kernels for 0% -> 25%
where the time goes in v1:
time: 318 us; the launch traced here: 317 us
  waiting for transfers between devices  135 us (42%)
  Pallas kernels  93.8 us (29%)
  starting transfers between devices  47.4 us (15%)
  local copies, waits for them, and re-layouts  27.7 us (9%)
  other arithmetic  12.8 us (4%)
    ppermute x38, waiting for transfers between devices, move(): self.arrays[target] = lax.ppermute(self.arrays[source], 'tile', pairs)  131 us
    pallas_call x4, Pallas kernels, run_tiles(): pl.pallas_call(functools.partial(tiles_kernel, names, plan, lanes, scale,...  50.3 us
    ppermute x38, starting transfers between devices, move(): self.arrays[target] = lax.ppermute(self.arrays[source], 'tile', pairs)  39.3 us
    pallas_call x14, Pallas kernels, run_copies(): pl.pallas_call(functools.partial(copies_kernel, names, len(after), plan,...  32.5 us
    unnamed x76, local copies, waits for them, and re-layouts  16.5 us
    pallas_call x4, Pallas kernels, run_gather(): pl.pallas_call(functools.partial(gather_kernel, plan, lanes, start), out_...  10.9 us
    transpose x2, other arithmetic, exchange(): x = x.transpose(1, 3, 4, 0, 2, 5)  8.74 us
    all_to_all x2, starting transfers between devices, exchange(): x = lax.all_to_all(x, 'tile', 0, 0, axis_index_groups=groups, tiled=True)  8.09 us
  transfers between devices with their start and end apart: 40, of which 23 were waited for; matrix products, arithmetic and copies ran while one was open for 4% of the time, Pallas kernels for 25%

profile of v1, /device:TPU:0, one launch (start us, length us, event | category | flops | bytes accessed | tf_op | source)
XLA Modules:
  0.0 317.2 jit_solution(4449722215635400879)
XLA Ops:
  0.0 2.0 slice.14
  5.3 3.4 %fusion.4 = bf16[4,8,2,1,16,512]{5,4,3,2,1,0:T(8,128)(2,1)} fusion(f32[1,4,16,8,2,512]{5,3,2,4,1,0:T(8,128)S(1)} %fusion.5, f32[4,16,8,512]{3,1,2,0:T(8,128)} %mul.48), kind=kLoop, calls=%fused_computation.7 | loop fusion | flops 1048576 | bytes 4194304 | tf_op jit(solution)/shard_map/transpose | solution.py:294
  8.7 4.2 %all-to-all-start.1 = ((bf16[4,8,2,1,16,512]{5,4,3,2,1,0:T(8,128)(2,1)}), bf16[4,8,2,1,16,512]{5,4,3,2,1,0:T(8,128)(2,1)S(1)}, u32[]{:S(2)}, u32[]{:S(2)}) async-start(bf16[4,8,2,1,16,512]{5,4,3,2,1,0:T(8,128)(2,1)} %fusion.4), calls=%async_computation.1 | async-start | bytes 2097152 | tf_op jit(solution)/shard_map/all_to_all | solution.py:299
  12.9 1.9 slice-done
  14.8 3.8 %fusion.2 = f32[1,4,16,8,2,1536]{5,3,2,4,1,0:T(8,128)} fusion(bf16[4,128,2,1536]{3,2,1,0:T(2,128)(2,1)S(1)} %slice-done), kind=kLoop, calls=%fused_computation.4 | loop fusion | flops 1572864 | bytes 9437184 | tf_op jit(solution)/shard_map/convert_element_type | solution.py:285
  22.0 5.3 %fusion.1 = bf16[4,8,2,1,16,1536]{5,4,3,2,1,0:T(8,128)(2,1)} fusion(f32[1,4,16,8,2,1536]{5,3,2,4,1,0:T(8,128)S(1)} %copy-done.3, f32[4,16,8,1536]{3,1,2,0:T(8,128)S(1)} %copy.58), kind=kLoop, calls=%fused_computation.2 | loop fusion | flops 3145728 | bytes 12582912 | tf_op jit(solution)/shard_map/transpose | solution.py:294
  28.3 3.9 %all-to-all-start = ((bf16[4,8,2,1,16,1536]{5,4,3,2,1,0:T(8,128)(2,1)}), bf16[4,8,2,1,16,1536]{5,4,3,2,1,0:T(8,128)(2,1)S(1)}, u32[]{:S(2)}, u32[]{:S(2)}) async-start(bf16[4,8,2,1,16,1536]{5,4,3,2,1,0:T(8,128)(2,1)} %fusion.1), calls=%async_computation | async-start | bytes 6291456 | tf_op jit(solution)/shard_map/all_to_all | solution.py:299
  32.8 2.7 gather.4
  35.5 2.0 pick.14
  37.5 2.4 collective-permute-start
  39.9 17.8 %collective-permute-done.refs_2_ = bf16[6,2,1,64,512]{4,3,2,1,0:T(8,128)(2,1)S(1)} collective-permute-done((bf16[6,2,1,64,512]{4,3,2,1,0:T(8,128)(2,1)}, bf16[6,2,1,64,512]{4,3,2,1,0:T(8,128)(2,1)S(1)}, u32[]{:S(2)}, u32[]{:S(2)}) %collective-permute-start) | collective-permute-done | bytes 786464 | tf_op jit(solution)/shard_map/ppermute | solution.py:323
  59.2 2.8 pick.15
  65.4 3.7 %all-to-all-done.own = bf16[4,8,2,1,16,1536]{5,4,3,2,1,0:T(8,128)(2,1)S(1)} async-done(((bf16[4,8,2,1,16,1536]{5,4,3,2,1,0:T(8,128)(2,1)}), bf16[4,8,2,1,16,1536]{5,4,3,2,1,0:T(8,128)(2,1)S(1)}, u32[]{:S(2)}, u32[]{:S(2)}) %all-to-all-start) | async-done | bytes 3145760 | tf_op jit(solution)/shard_map/all_to_all | solution.py:299
  70.8 2.7 gather.5
  73.5 7.9 %collective-permute-done.4.refs_5_.refs_8_ = bf16[5,2,1,64,512]{4,3,2,1,0:T(8,128)(2,1)} collective-permute-done((bf16[5,2,1,64,512]{4,3,2,1,0:T(8,128)(2,1)}, bf16[5,2,1,64,512]{4,3,2,1,0:T(8,128)(2,1)}, u32[]{:S(2)}, u32[]{:S(2)}) %collective-permute-start.4) | collective-permute-done | bytes 655392 | tf_op jit(solution)/shard_map/ppermute | solution.py:323
  81.3 2.1 pick.16
  86.7 11.5 %collective-permute-done.5.refs_5_.refs_9_ = bf16[6,2,1,64,512]{4,3,2,1,0:T(8,128)(2,1)} collective-permute-done((bf16[6,2,1,64,512]{4,3,2,1,0:T(8,128)(2,1)}, bf16[6,2,1,64,512]{4,3,2,1,0:T(8,128)(2,1)}, u32[]{:S(2)}, u32[]{:S(2)}) %collective-permute-start.5) | collective-permute-done | bytes 786464 | tf_op jit(solution)/shard_map/ppermute | solution.py:323
  98.2 2.0 pick.17
  102.0 2.7 gather.6
  104.8 2.4 collective-permute-start.9
  107.2 7.8 %collective-permute-done.8.refs_7_.refs_10_.refs_8_ = bf16[6,2,1,64,512]{4,3,2,1,0:T(8,128)(2,1)S(1)} collective-permute-done((bf16[6,2,1,64,512]{4,3,2,1,0:T(8,128)(2,1)}, bf16[6,2,1,64,512]{4,3,2,1,0:T(8,128)(2,1)S(1)}, u32[]{:S(2)}, u32[]{:S(2)}) %collective-permute-start.8) | collective-permute-done | bytes 786464 | tf_op jit(solution)/shard_map/ppermute | solution.py:323
  115.8 2.9 pick.18
  122.1 2.8 gather.7
  124.9 6.9 %collective-permute-done.11.refs_7_.refs_11_ = bf16[6,2,1,64,512]{4,3,2,1,0:T(8,128)(2,1)S(1)} collective-permute-done((bf16[6,2,1,64,512]{4,3,2,1,0:T(8,128)(2,1)}, bf16[6,2,1,64,512]{4,3,2,1,0:T(8,128)(2,1)S(1)}, u32[]{:S(2)}, u32[]{:S(2)}) %collective-permute-start.11) | collective-permute-done | bytes 786464 | tf_op jit(solution)/shard_map/ppermute | solution.py:323
  132.9 2.1 pick.19
  140.5 8.2 %collective-permute-done.16.refs_7_.refs_9_.refs_8_ = bf16[6,2,1,64,512]{4,3,2,1,0:T(8,128)(2,1)S(1)} collective-permute-done((bf16[6,2,1,64,512]{4,3,2,1,0:T(8,128)(2,1)}, bf16[6,2,1,64,512]{4,3,2,1,0:T(8,128)(2,1)S(1)}, u32[]{:S(2)}, u32[]{:S(2)}) %collective-permute-start.16) | collective-permute-done | bytes 786464 | tf_op jit(solution)/shard_map/ppermute | solution.py:323
  149.5 2.2 pick.20
  151.7 2.4 collective-permute-start.20
  157.5 8.0 %collective-permute-done.17.refs_7_.refs_12_.refs_10_.refs_9_ = bf16[6,2,1,64,512]{4,3,2,1,0:T(8,128)(2,1)S(1)} collective-permute-done((bf16[6,2,1,64,512]{4,3,2,1,0:T(8,128)(2,1)}, bf16[6,2,1,64,512]{4,3,2,1,0:T(8,128)(2,1)S(1)}, u32[]{:S(2)}, u32[]{:S(2)}) %collective-permute-start.17) | collective-permute-done | bytes 786464 | tf_op jit(solution)/shard_map/ppermute | solution.py:323
  166.4 2.2 pick.21
  172.8 9.6 %tiles.4 = (f32[5,512,1024]{2,1,0:T(8,128)}, s32[8,128]{1,0:T(8,128)}) custom-call(bf16[6,2,1,64,512]{4,3,2,1,0:T(8,128)(2,1)} %get-tuple-element.79.refs_0_, bf16[6,2,1,64,512]{4,3,2,1,0:T(8,128)(2,1)} %get-tuple-element.80.refs_1_, bf16[6,2,1,64,512]{4,3,2,1,0:T(8,128)(2,1)} %get-tuple-element.82.refs_0_.refs_2_, ...), custom_call_target="tpu_custom_call", output_to_operand_aliasing={{1}: (13, {})} | custom-call | tf_op jit(solution)/shard_map/tiles/pallas_call | solution.py:264
  183.6 2.9 pick.22
  188.7 10.5 %collective-permute-done.23.refs_5_.refs_11_ = bf16[6,2,1,64,512]{4,3,2,1,0:T(8,128)(2,1)S(1)} collective-permute-done((bf16[6,2,1,64,512]{4,3,2,1,0:T(8,128)(2,1)}, bf16[6,2,1,64,512]{4,3,2,1,0:T(8,128)(2,1)S(1)}, u32[]{:S(2)}, u32[]{:S(2)}) %collective-permute-start.23) | collective-permute-done | bytes 786464 | tf_op jit(solution)/shard_map/ppermute | solution.py:323
  200.1 2.9 pick.23
  203.9 10.3 %collective-permute-done.28.refs_12_.refs_9_.refs_8_ = bf16[6,2,1,64,512]{4,3,2,1,0:T(8,128)(2,1)S(1)} collective-permute-done((bf16[6,2,1,64,512]{4,3,2,1,0:T(8,128)(2,1)}, bf16[6,2,1,64,512]{4,3,2,1,0:T(8,128)(2,1)S(1)}, u32[]{:S(2)}, u32[]{:S(2)}) %collective-permute-start.28) | collective-permute-done | bytes 786464 | tf_op jit(solution)/shard_map/ppermute | solution.py:323
  215.9 13.3 %tiles.5 = (f32[5,512,1024]{2,1,0:T(8,128)}, s32[8,128]{1,0:T(8,128)}) custom-call(bf16[6,2,1,64,512]{4,3,2,1,0:T(8,128)(2,1)} %get-tuple-element.94.refs_0_, bf16[6,2,1,64,512]{4,3,2,1,0:T(8,128)(2,1)} %get-tuple-element.95.refs_1_, bf16[6,2,1,64,512]{4,3,2,1,0:T(8,128)(2,1)} %get-tuple-element.98.refs_2_, ...), custom_call_target="tpu_custom_call", output_to_operand_aliasing={{0}: (13, {}), {1}: (14, {})} | custom-call | tf_op jit(solution)/shard_map/tiles/pallas_call | solution.py:264
  230.4 2.1 pick.24
  236.1 2.2 pick.25
  238.2 3.1 collective-permute-start.30
  241.3 8.9 %collective-permute-done.32.refs_9_.refs_13_.refs_10_ = bf16[6,2,1,64,512]{4,3,2,1,0:T(8,128)(2,1)S(1)} collective-permute-done((bf16[6,2,1,64,512]{4,3,2,1,0:T(8,128)(2,1)}, bf16[6,2,1,64,512]{4,3,2,1,0:T(8,128)(2,1)S(1)}, u32[]{:S(2)}, u32[]{:S(2)}) %collective-permute-start.32) | collective-permute-done | bytes 786464 | tf_op jit(solution)/shard_map/ppermute | solution.py:323
  253.0 2.7 collective-permute-done.35.refs_7_
  256.6 2.1 pick.26
  259.9 8.5 %collective-permute-done.30.refs_6_ = bf16[6,2,1,64,512]{4,3,2,1,0:T(8,128)(2,1)S(1)} collective-permute-done((bf16[6,2,1,64,512]{4,3,2,1,0:T(8,128)(2,1)}, bf16[6,2,1,64,512]{4,3,2,1,0:T(8,128)(2,1)S(1)}, u32[]{:S(2)}, u32[]{:S(2)}) %collective-permute-start.30) | collective-permute-done | bytes 786464 | tf_op jit(solution)/shard_map/ppermute | solution.py:323
  268.4 2.6 collective-permute-done.33.refs_9_.refs_11_
  271.9 2.1 pick.27
  276.5 11.3 %collective-permute-done.36.refs_14_.refs_12_ = bf16[6,2,1,64,512]{4,3,2,1,0:T(8,128)(2,1)S(1)} collective-permute-done((bf16[6,2,1,64,512]{4,3,2,1,0:T(8,128)(2,1)}, bf16[6,2,1,64,512]{4,3,2,1,0:T(8,128)(2,1)S(1)}, u32[]{:S(2)}, u32[]{:S(2)}) %collective-permute-start.36) | collective-permute-done | bytes 786464 | tf_op jit(solution)/shard_map/ppermute | solution.py:323
  288.7 13.3 %tiles.6 = (f32[5,512,1024]{2,1,0:T(8,128)}, s32[8,128]{1,0:T(8,128)}) custom-call(bf16[6,2,1,64,512]{4,3,2,1,0:T(8,128)(2,1)} %get-tuple-element.105.refs_2_.refs_0_, bf16[6,2,1,64,512]{4,3,2,1,0:T(8,128)(2,1)} %get-tuple-element.106.refs_3_.refs_1_, ...), custom_call_target="tpu_custom_call", output_to_operand_aliasing={{0}: (15, {}), {1}: (16, {})} | custom-call | tf_op jit(solution)/shard_map/tiles/pallas_call | solution.py:264
  303.0 14.0 %tiles.7 = (f32[5,512,1024]{2,1,0:T(8,128)}, s32[8,128]{1,0:T(8,128)}) custom-call(bf16[6,2,1,64,512]{4,3,2,1,0:T(8,128)(2,1)} %get-tuple-element.113.refs_2_.refs_0_, bf16[6,2,1,64,512]{4,3,2,1,0:T(8,128)(2,1)} %get-tuple-element.114.refs_3_.refs_1_, ...), custom_call_target="tpu_custom_call", output_to_operand_aliasing={{0}: (15, {}), {1}: (16, {})} | custom-call | tf_op jit(solution)/shard_map/tiles/pallas_call | solution.py:264
  (149 shorter events, 61.6 us)
Async XLA Ops:
  8.7 18.7 %all-to-all-start.1 = ((bf16[4,8,2,1,16,512]{5,4,3,2,1,0:T(8,128)(2,1)}), bf16[4,8,2,1,16,512]{5,4,3,2,1,0:T(8,128)(2,1)S(1)}, u32[]{:S(2)}, u32[]{:S(2)}) async-start(bf16[4,8,2,1,16,512]{5,4,3,2,1,0:T(8,128)(2,1)} %fusion.4), calls=%async_computation.1 | async-start | bytes 2097152 | tf_op jit(solution)/shard_map/all_to_all | solution.py:299
  28.3 40.8 %all-to-all-start = ((bf16[4,8,2,1,16,1536]{5,4,3,2,1,0:T(8,128)(2,1)}), bf16[4,8,2,1,16,1536]{5,4,3,2,1,0:T(8,128)(2,1)S(1)}, u32[]{:S(2)}, u32[]{:S(2)}) async-start(bf16[4,8,2,1,16,1536]{5,4,3,2,1,0:T(8,128)(2,1)} %fusion.1), calls=%async_computation | async-start | bytes 6291456 | tf_op jit(solution)/shard_map/all_to_all | solution.py:299
  37.5 20.1 %collective-permute-start = (bf16[6,2,1,64,512]{4,3,2,1,0:T(8,128)(2,1)}, bf16[6,2,1,64,512]{4,3,2,1,0:T(8,128)(2,1)S(1)}, u32[]{:S(2)}, u32[]{:S(2)}) collective-permute-start(bf16[6,2,1,64,512]{4,3,2,1,0:T(8,128)(2,1)} %get-tuple-element.79.refs_0_), channel_id=1, source_target_pairs={{0,8},{1,0},{2,10},{3,2},{4,12},{5,4},{6,14},{7,6},{8,16},{9,1},{1... | collective-permute-start | bytes 2359304 | tf_op jit(solution)/shard_map/ppermute | solution.py:323
  39.9 18.4 %collective-permute-start.1 = (bf16[6,2,1,64,512]{4,3,2,1,0:T(8,128)(2,1)}, bf16[6,2,1,64,512]{4,3,2,1,0:T(8,128)(2,1)S(1)}, u32[]{:S(2)}, u32[]{:S(2)}) collective-permute-start(bf16[6,2,1,64,512]{4,3,2,1,0:T(8,128)(2,1)} %get-tuple-element.80.refs_1_), channel_id=1, source_target_pairs={{0,1},{1,9},{2,3},{3,11},{4,5},{5,13},{6,7},{7,15},{8,0},{9,17},{1... | collective-permute-start | bytes 2359304 | tf_op jit(solution)/shard_map/ppermute | solution.py:323
  62.0 23.1 %collective-permute-start.2 = (bf16[6,2,1,64,512]{4,3,2,1,0:T(8,128)(2,1)}, bf16[6,2,1,64,512]{4,3,2,1,0:T(8,128)(2,1)}, u32[]{:S(2)}, u32[]{:S(2)}) collective-permute-start(bf16[6,2,1,64,512]{4,3,2,1,0:T(8,128)(2,1)} %get-tuple-element.82.refs_0_.refs_2_), channel_id=1, source_target_pairs={{0,8},{1,0},{2,10},{3,2},{4,12},{5,4},{6,14},{7,6},{8,16},{9,1},{1... | collective-permute-start | bytes 2359304 | tf_op jit(solution)/shard_map/ppermute | solution.py:323
  63.4 18.0 %collective-permute-start.4 = (bf16[5,2,1,64,512]{4,3,2,1,0:T(8,128)(2,1)}, bf16[5,2,1,64,512]{4,3,2,1,0:T(8,128)(2,1)}, u32[]{:S(2)}, u32[]{:S(2)}) collective-permute-start(bf16[5,2,1,64,512]{4,3,2,1,0:T(8,128)(2,1)} %get-tuple-element.88), channel_id=1, source_target_pairs={{0,4},{1,5},{2,6},{3,7},{4,0},{5,1},{6,2},{7,3},{8,12},{9,13},{10,... | collective-permute-start | bytes 1966088 | tf_op jit(solution)/shard_map/ppermute | solution.py:323
  65.0 21.7 %collective-permute-start.3 = (bf16[6,2,1,64,512]{4,3,2,1,0:T(8,128)(2,1)}, bf16[6,2,1,64,512]{4,3,2,1,0:T(8,128)(2,1)}, u32[]{:S(2)}, u32[]{:S(2)}) collective-permute-start(bf16[6,2,1,64,512]{4,3,2,1,0:T(8,128)(2,1)} %get-tuple-element.83.refs_1_.refs_3_), channel_id=1, source_target_pairs={{0,1},{1,9},{2,3},{3,11},{4,5},{5,13},{6,7},{7,15},{8,0},{9,17},{1... | collective-permute-start | bytes 2359304 | tf_op jit(solution)/shard_map/ppermute | solution.py:323
  65.0 33.2 %collective-permute-start.5 = (bf16[6,2,1,64,512]{4,3,2,1,0:T(8,128)(2,1)}, bf16[6,2,1,64,512]{4,3,2,1,0:T(8,128)(2,1)}, u32[]{:S(2)}, u32[]{:S(2)}) collective-permute-start(bf16[6,2,1,64,512]{4,3,2,1,0:T(8,128)(2,1)} %get-tuple-element.90), channel_id=1, source_target_pairs={{0,4},{1,5},{2,6},{3,7},{4,0},{5,1},{6,2},{7,3},{8,12},{9,13},{10,... | collective-permute-start | bytes 2359304 | tf_op jit(solution)/shard_map/ppermute | solution.py:323
  83.4 21.3 %collective-permute-start.6 = (bf16[6,2,1,64,512]{4,3,2,1,0:T(8,128)(2,1)}, bf16[6,2,1,64,512]{4,3,2,1,0:T(8,128)(2,1)S(1)}, u32[]{:S(2)}, u32[]{:S(2)}) collective-permute-start(bf16[6,2,1,64,512]{4,3,2,1,0:T(8,128)(2,1)} %get-tuple-element.94.refs_0_), channel_id=1, source_target_pairs={{0,8},{1,0},{2,10},{3,2},{4,12},{5,4},{6,14},{7,6},{8,16},{9,1},{1... | collective-permute-start | bytes 2359304 | tf_op jit(solution)/shard_map/ppermute | solution.py:323
  85.1 22.0 %collective-permute-start.7 = (bf16[6,2,1,64,512]{4,3,2,1,0:T(8,128)(2,1)}, bf16[6,2,1,64,512]{4,3,2,1,0:T(8,128)(2,1)S(1)}, u32[]{:S(2)}, u32[]{:S(2)}) collective-permute-start(bf16[6,2,1,64,512]{4,3,2,1,0:T(8,128)(2,1)} %get-tuple-element.95.refs_1_), channel_id=1, source_target_pairs={{0,1},{1,9},{2,3},{3,11},{4,5},{5,13},{6,7},{7,15},{8,0},{9,17},{1... | collective-permute-start | bytes 2359304 | tf_op jit(solution)/shard_map/ppermute | solution.py:323
  85.1 29.8 %collective-permute-start.8 = (bf16[6,2,1,64,512]{4,3,2,1,0:T(8,128)(2,1)}, bf16[6,2,1,64,512]{4,3,2,1,0:T(8,128)(2,1)S(1)}, u32[]{:S(2)}, u32[]{:S(2)}) collective-permute-start(bf16[6,2,1,64,512]{4,3,2,1,0:T(8,128)(2,1)} %get-tuple-element.97), channel_id=1, source_target_pairs={{0,4},{1,5},{2,6},{3,7},{4,0},{5,1},{6,2},{7,3},{8,12},{9,13},{10,... | collective-permute-start | bytes 2359304 | tf_op jit(solution)/shard_map/ppermute | solution.py:323
  100.2 21.0 %collective-permute-start.10 = (bf16[6,2,1,64,512]{4,3,2,1,0:T(8,128)(2,1)}, bf16[6,2,1,64,512]{4,3,2,1,0:T(8,128)(2,1)S(1)}, u32[]{:S(2)}, u32[]{:S(2)}) collective-permute-start(bf16[6,2,1,64,512]{4,3,2,1,0:T(8,128)(2,1)} %get-tuple-element.101.refs_5_), channel_id=1, source_target_pairs={{0,1},{1,9},{2,3},{3,11},{4,5},{5,13},{6,7},{7,15},{8,0},{9,17},{1... | collective-permute-start | bytes 2359304 | tf_op jit(solution)/shard_map/ppermute | solution.py:323
  100.3 31.5 %collective-permute-start.11 = (bf16[6,2,1,64,512]{4,3,2,1,0:T(8,128)(2,1)}, bf16[6,2,1,64,512]{4,3,2,1,0:T(8,128)(2,1)S(1)}, u32[]{:S(2)}, u32[]{:S(2)}) collective-permute-start(bf16[6,2,1,64,512]{4,3,2,1,0:T(8,128)(2,1)} %get-tuple-element.104), channel_id=1, source_target_pairs={{0,4},{1,5},{2,6},{3,7},{4,0},{5,1},{6,2},{7,3},{8,12},{9,13},{10,... | collective-permute-start | bytes 2359304 | tf_op jit(solution)/shard_map/ppermute | solution.py:323
  104.8 10.2 %copy-start.14 = (bf16[6,2,1,64,512]{4,3,2,1,0:T(8,128)(2,1)}, bf16[6,2,1,64,512]{4,3,2,1,0:T(8,128)(2,1)S(1)}, u32[]{:S(2)}) copy-start(bf16[6,2,1,64,512]{4,3,2,1,0:T(8,128)(2,1)S(1)} %collective-permute-done.6.refs_4_) | copy-start | bytes 2359300
  104.8 27.0 %collective-permute-start.9 = (bf16[6,2,1,64,512]{4,3,2,1,0:T(8,128)(2,1)}, bf16[6,2,1,64,512]{4,3,2,1,0:T(8,128)(2,1)S(1)}, u32[]{:S(2)}, u32[]{:S(2)}) collective-permute-start(bf16[6,2,1,64,512]{4,3,2,1,0:T(8,128)(2,1)} %get-tuple-element.100.refs_4_), channel_id=1, source_target_pairs={{0,8},{1,0},{2,10},{3,2},{4,12},{5,4},{6,14},{7,6},{8,16},{9,1},{1... | collective-permute-start | bytes 2359304 | tf_op jit(solution)/shard_map/ppermute | solution.py:323
  118.7 18.5 %collective-permute-start.14 = (bf16[6,2,1,64,512]{4,3,2,1,0:T(8,128)(2,1)}, bf16[6,2,1,64,512]{4,3,2,1,0:T(8,128)(2,1)S(1)}, u32[]{:S(2)}, u32[]{:S(2)}) collective-permute-start(bf16[6,2,1,64,512]{4,3,2,1,0:T(8,128)(2,1)} %get-tuple-element.98.refs_2_), channel_id=1, source_target_pairs={{0,8},{1,0},{2,10},{3,2},{4,12},{5,4},{6,14},{7,6},{8,16},{9,1},{1... | collective-permute-start | bytes 2359304 | tf_op jit(solution)/shard_map/ppermute | solution.py:323
  119.6 20.9 %collective-permute-start.15 = (bf16[6,2,1,64,512]{4,3,2,1,0:T(8,128)(2,1)}, bf16[6,2,1,64,512]{4,3,2,1,0:T(8,128)(2,1)S(1)}, u32[]{:S(2)}, u32[]{:S(2)}) collective-permute-start(bf16[6,2,1,64,512]{4,3,2,1,0:T(8,128)(2,1)} %get-tuple-element.99.refs_3_), channel_id=1, source_target_pairs={{0,1},{1,9},{2,3},{3,11},{4,5},{5,13},{6,7},{7,15},{8,0},{9,17},{1... | collective-permute-start | bytes 2359304 | tf_op jit(solution)/shard_map/ppermute | solution.py:323
  121.3 10.5 %copy-start.33 = (bf16[6,2,1,64,512]{4,3,2,1,0:T(8,128)(2,1)}, bf16[6,2,1,64,512]{4,3,2,1,0:T(8,128)(2,1)S(1)}, u32[]{:S(2)}) copy-start(bf16[6,2,1,64,512]{4,3,2,1,0:T(8,128)(2,1)S(1)} %collective-permute-done.10.refs_5_.refs_7_) | copy-start | bytes 2359300
  121.3 27.4 %collective-permute-start.16 = (bf16[6,2,1,64,512]{4,3,2,1,0:T(8,128)(2,1)}, bf16[6,2,1,64,512]{4,3,2,1,0:T(8,128)(2,1)S(1)}, u32[]{:S(2)}, u32[]{:S(2)}) collective-permute-start(bf16[6,2,1,64,512]{4,3,2,1,0:T(8,128)(2,1)} %get-tuple-element.110), channel_id=1, source_target_pairs={{0,4},{1,5},{2,6},{3,7},{4,0},{5,1},{6,2},{7,3},{8,12},{9,13},{10,... | collective-permute-start | bytes 2359304 | tf_op jit(solution)/shard_map/ppermute | solution.py:323
  135.1 19.2 %collective-permute-start.12 = (bf16[6,2,1,64,512]{4,3,2,1,0:T(8,128)(2,1)}, bf16[6,2,1,64,512]{4,3,2,1,0:T(8,128)(2,1)S(1)}, u32[]{:S(2)}, u32[]{:S(2)}) collective-permute-start(bf16[6,2,1,64,512]{4,3,2,1,0:T(8,128)(2,1)} %get-tuple-element.105.refs_2_.refs_0_), channel_id=1, source_target_pairs={{0,8},{1,0},{2,10},{3,2},{4,12},{5,4},{6,14},{7,6},{8,16},{9,1},{1... | collective-permute-start | bytes 2359304 | tf_op jit(solution)/shard_map/ppermute | solution.py:323
  136.7 20.8 %collective-permute-start.13 = (bf16[6,2,1,64,512]{4,3,2,1,0:T(8,128)(2,1)}, bf16[6,2,1,64,512]{4,3,2,1,0:T(8,128)(2,1)S(1)}, u32[]{:S(2)}, u32[]{:S(2)}) collective-permute-start(bf16[6,2,1,64,512]{4,3,2,1,0:T(8,128)(2,1)} %get-tuple-element.106.refs_3_.refs_1_), channel_id=1, source_target_pairs={{0,1},{1,9},{2,3},{3,11},{4,5},{5,13},{6,7},{7,15},{8,0},{9,17},{1... | collective-permute-start | bytes 2359304 | tf_op jit(solution)/shard_map/ppermute | solution.py:323
  137.2 11.4 %copy-start.29 = (bf16[6,2,1,64,512]{4,3,2,1,0:T(8,128)(2,1)}, bf16[6,2,1,64,512]{4,3,2,1,0:T(8,128)(2,1)S(1)}, u32[]{:S(2)}) copy-start(bf16[6,2,1,64,512]{4,3,2,1,0:T(8,128)(2,1)S(1)} %collective-permute-done.14.refs_4_) | copy-start | bytes 2359300
  137.2 28.3 %collective-permute-start.17 = (bf16[6,2,1,64,512]{4,3,2,1,0:T(8,128)(2,1)}, bf16[6,2,1,64,512]{4,3,2,1,0:T(8,128)(2,1)S(1)}, u32[]{:S(2)}, u32[]{:S(2)}) collective-permute-start(bf16[6,2,1,64,512]{4,3,2,1,0:T(8,128)(2,1)} %get-tuple-element.112), channel_id=1, source_target_pairs={{0,4},{1,5},{2,6},{3,7},{4,0},{5,1},{6,2},{7,3},{8,12},{9,13},{10,... | collective-permute-start | bytes 2359304 | tf_op jit(solution)/shard_map/ppermute | solution.py:323
  140.5 8.2 %copy-start.31 = (bf16[6,2,1,64,512]{4,3,2,1,0:T(8,128)(2,1)}, bf16[6,2,1,64,512]{4,3,2,1,0:T(8,128)(2,1)S(1)}, u32[]{:S(2)}) copy-start(bf16[6,2,1,64,512]{4,3,2,1,0:T(8,128)(2,1)S(1)} %collective-permute-done.15.refs_5_) | copy-start | bytes 2359300
  151.7 19.4 %collective-permute-start.20 = (bf16[6,2,1,64,512]{4,3,2,1,0:T(8,128)(2,1)}, bf16[6,2,1,64,512]{4,3,2,1,0:T(8,128)(2,1)S(1)}, u32[]{:S(2)}, u32[]{:S(2)}) collective-permute-start(bf16[6,2,1,64,512]{4,3,2,1,0:T(8,128)(2,1)} %get-tuple-element.115.refs_4_), channel_id=1, source_target_pairs={{0,8},{1,0},{2,10},{3,2},{4,12},{5,4},{6,14},{7,6},{8,16},{9,1},{1... | collective-permute-start | bytes 2359304 | tf_op jit(solution)/shard_map/ppermute | solution.py:323
  154.1 28.3 %collective-permute-start.21 = (bf16[6,2,1,64,512]{4,3,2,1,0:T(8,128)(2,1)}, bf16[6,2,1,64,512]{4,3,2,1,0:T(8,128)(2,1)S(1)}, u32[]{:S(2)}, u32[]{:S(2)}) collective-permute-start(bf16[6,2,1,64,512]{4,3,2,1,0:T(8,128)(2,1)} %get-tuple-element.116.refs_5_), channel_id=1, source_target_pairs={{0,1},{1,9},{2,3},{3,11},{4,5},{5,13},{6,7},{7,15},{8,0},{9,17},{1... | collective-permute-start | bytes 2359304 | tf_op jit(solution)/shard_map/ppermute | solution.py:323
  154.3 11.2 %copy-start.12 = (bf16[6,2,1,64,512]{4,3,2,1,0:T(8,128)(2,1)}, bf16[6,2,1,64,512]{4,3,2,1,0:T(8,128)(2,1)S(1)}, u32[]{:S(2)}) copy-start(bf16[6,2,1,64,512]{4,3,2,1,0:T(8,128)(2,1)S(1)} %collective-permute-done.12.refs_4_) | copy-start | bytes 2359300
  154.3 28.2 %collective-permute-start.22 = (bf16[6,2,1,64,512]{4,3,2,1,0:T(8,128)(2,1)}, bf16[6,2,1,64,512]{4,3,2,1,0:T(8,128)(2,1)S(1)}, u32[]{:S(2)}, u32[]{:S(2)}) collective-permute-start(bf16[6,2,1,64,512]{4,3,2,1,0:T(8,128)(2,1)} %get-tuple-element.119), channel_id=1, source_target_pairs={{0,4},{1,5},{2,6},{3,7},{4,0},{5,1},{6,2},{7,3},{8,12},{9,13},{10,... | collective-permute-start | bytes 2359304 | tf_op jit(solution)/shard_map/ppermute | solution.py:323
  168.6 20.1 %collective-permute-start.18 = (bf16[6,2,1,64,512]{4,3,2,1,0:T(8,128)(2,1)}, bf16[6,2,1,64,512]{4,3,2,1,0:T(8,128)(2,1)S(1)}, u32[]{:S(2)}, u32[]{:S(2)}) collective-permute-start(bf16[6,2,1,64,512]{4,3,2,1,0:T(8,128)(2,1)} %get-tuple-element.113.refs_2_.refs_0_), channel_id=1, source_target_pairs={{0,8},{1,0},{2,10},{3,2},{4,12},{5,4},{6,14},{7,6},{8,16},{9,1},{1... | collective-permute-start | bytes 2359304 | tf_op jit(solution)/shard_map/ppermute | solution.py:323
  170.3 18.4 %collective-permute-start.19 = (bf16[6,2,1,64,512]{4,3,2,1,0:T(8,128)(2,1)}, bf16[6,2,1,64,512]{4,3,2,1,0:T(8,128)(2,1)S(1)}, u32[]{:S(2)}, u32[]{:S(2)}) collective-permute-start(bf16[6,2,1,64,512]{4,3,2,1,0:T(8,128)(2,1)} %get-tuple-element.114.refs_3_.refs_1_), channel_id=1, source_target_pairs={{0,1},{1,9},{2,3},{3,11},{4,5},{5,13},{6,7},{7,15},{8,0},{9,17},{1... | collective-permute-start | bytes 2359304 | tf_op jit(solution)/shard_map/ppermute | solution.py:323
  171.1 11.3 %copy-start.26 = (bf16[6,2,1,64,512]{4,3,2,1,0:T(8,128)(2,1)}, bf16[6,2,1,64,512]{4,3,2,1,0:T(8,128)(2,1)S(1)}, u32[]{:S(2)}) copy-start(bf16[6,2,1,64,512]{4,3,2,1,0:T(8,128)(2,1)S(1)} %collective-permute-done.20.refs_6_) | copy-start | bytes 2359300
  171.1 28.1 %collective-permute-start.23 = (bf16[6,2,1,64,512]{4,3,2,1,0:T(8,128)(2,1)}, bf16[6,2,1,64,512]{4,3,2,1,0:T(8,128)(2,1)S(1)}, u32[]{:S(2)}, u32[]{:S(2)}) collective-permute-start(bf16[6,2,1,64,512]{4,3,2,1,0:T(8,128)(2,1)} %get-tuple-element.121), channel_id=1, source_target_pairs={{0,4},{1,5},{2,6},{3,7},{4,0},{5,1},{6,2},{7,3},{8,12},{9,13},{10,... | collective-permute-start | bytes 2359304 | tf_op jit(solution)/shard_map/ppermute | solution.py:323
  186.5 27.7 %collective-permute-start.28 = (bf16[6,2,1,64,512]{4,3,2,1,0:T(8,128)(2,1)}, bf16[6,2,1,64,512]{4,3,2,1,0:T(8,128)(2,1)S(1)}, u32[]{:S(2)}, u32[]{:S(2)}) collective-permute-start(bf16[6,2,1,64,512]{4,3,2,1,0:T(8,128)(2,1)} %get-tuple-element.126), channel_id=1, source_target_pairs={{0,4},{1,5},{2,6},{3,7},{4,0},{5,1},{6,2},{7,3},{8,12},{9,13},{10,... | collective-permute-start | bytes 2359304 | tf_op jit(solution)/shard_map/ppermute | solution.py:323
  187.9 41.3 %collective-permute-start.26 = (bf16[6,2,1,64,512]{4,3,2,1,0:T(8,128)(2,1)}, bf16[6,2,1,64,512]{4,3,2,1,0:T(8,128)(2,1)S(1)}, u32[]{:S(2)}, u32[]{:S(2)}) collective-permute-start(bf16[6,2,1,64,512]{4,3,2,1,0:T(8,128)(2,1)} %get-tuple-element.124.refs_2_), channel_id=1, source_target_pairs={{0,8},{1,0},{2,10},{3,2},{4,12},{5,4},{6,14},{7,6},{8,16},{9,1},{1... | collective-permute-start | bytes 2359304 | tf_op jit(solution)/shard_map/ppermute | solution.py:323
  188.7 10.5 %copy-start.1 = (bf16[6,2,1,64,512]{4,3,2,1,0:T(8,128)(2,1)}, bf16[6,2,1,64,512]{4,3,2,1,0:T(8,128)(2,1)S(1)}, u32[]{:S(2)}) copy-start(bf16[6,2,1,64,512]{4,3,2,1,0:T(8,128)(2,1)S(1)} %collective-permute-done.18.refs_2_) | copy-start | bytes 2359300
  188.7 40.6 %collective-permute-start.27 = (bf16[6,2,1,64,512]{4,3,2,1,0:T(8,128)(2,1)}, bf16[6,2,1,64,512]{4,3,2,1,0:T(8,128)(2,1)S(1)}, u32[]{:S(2)}, u32[]{:S(2)}) collective-permute-start(bf16[6,2,1,64,512]{4,3,2,1,0:T(8,128)(2,1)} %get-tuple-element.125.refs_3_), channel_id=1, source_target_pairs={{0,1},{1,9},{2,3},{3,11},{4,5},{5,13},{6,7},{7,15},{8,0},{9,17},{1... | collective-permute-start | bytes 2359304 | tf_op jit(solution)/shard_map/ppermute | solution.py:323
  188.7 10.5 %copy-start.2 = (bf16[6,2,1,64,512]{4,3,2,1,0:T(8,128)(2,1)}, bf16[6,2,1,64,512]{4,3,2,1,0:T(8,128)(2,1)S(1)}, u32[]{:S(2)}) copy-start(bf16[6,2,1,64,512]{4,3,2,1,0:T(8,128)(2,1)S(1)} %collective-permute-done.19.refs_3_) | copy-start | bytes 2359300
  203.0 31.7 %collective-permute-start.24 = (bf16[6,2,1,64,512]{4,3,2,1,0:T(8,128)(2,1)}, bf16[6,2,1,64,512]{4,3,2,1,0:T(8,128)(2,1)S(1)}, u32[]{:S(2)}, u32[]{:S(2)}) collective-permute-start(bf16[6,2,1,64,512]{4,3,2,1,0:T(8,128)(2,1)} %get-tuple-element.122.refs_4_.refs_2_), channel_id=1, source_target_pairs={{0,8},{1,0},{2,10},{3,2},{4,12},{5,4},{6,14},{7,6},{8,16},{9,1},{1... | collective-permute-start | bytes 2359304 | tf_op jit(solution)/shard_map/ppermute | solution.py:323
  203.9 30.8 %collective-permute-start.25 = (bf16[6,2,1,64,512]{4,3,2,1,0:T(8,128)(2,1)}, bf16[6,2,1,64,512]{4,3,2,1,0:T(8,128)(2,1)S(1)}, u32[]{:S(2)}, u32[]{:S(2)}) collective-permute-start(bf16[6,2,1,64,512]{4,3,2,1,0:T(8,128)(2,1)} %get-tuple-element.123.refs_5_.refs_3_), channel_id=1, source_target_pairs={{0,1},{1,9},{2,3},{3,11},{4,5},{5,13},{6,7},{7,15},{8,0},{9,17},{1... | collective-permute-start | bytes 2359304 | tf_op jit(solution)/shard_map/ppermute | solution.py:323
  214.2 20.5 %collective-permute-start.29 = (bf16[6,2,1,64,512]{4,3,2,1,0:T(8,128)(2,1)}, bf16[6,2,1,64,512]{4,3,2,1,0:T(8,128)(2,1)S(1)}, u32[]{:S(2)}, u32[]{:S(2)}) collective-permute-start(bf16[6,2,1,64,512]{4,3,2,1,0:T(8,128)(2,1)} %get-tuple-element.131), channel_id=1, source_target_pairs={{0,4},{1,5},{2,6},{3,7},{4,0},{5,1},{6,2},{7,3},{8,12},{9,13},{10,... | collective-permute-start | bytes 2359304 | tf_op jit(solution)/shard_map/ppermute | solution.py:323
  232.5 17.8 %collective-permute-start.32 = (bf16[6,2,1,64,512]{4,3,2,1,0:T(8,128)(2,1)}, bf16[6,2,1,64,512]{4,3,2,1,0:T(8,128)(2,1)S(1)}, u32[]{:S(2)}, u32[]{:S(2)}) collective-permute-start(bf16[6,2,1,64,512]{4,3,2,1,0:T(8,128)(2,1)} %get-tuple-element.134), channel_id=1, source_target_pairs={{0,4},{1,5},{2,6},{3,7},{4,0},{5,1},{6,2},{7,3},{8,12},{9,13},{10,... | collective-permute-start | bytes 2359304 | tf_op jit(solution)/shard_map/ppermute | solution.py:323
  233.5 19.5 %collective-permute-start.34 = (bf16[6,2,1,64,512]{4,3,2,1,0:T(8,128)(2,1)}, bf16[6,2,1,64,512]{4,3,2,1,0:T(8,128)(2,1)S(1)}, u32[]{:S(2)}, u32[]{:S(2)}) collective-permute-start(bf16[6,2,1,64,512]{4,3,2,1,0:T(8,128)(2,1)} %get-tuple-element.136.refs_4_), channel_id=1, source_target_pairs={{0,8},{1,0},{2,10},{3,2},{4,12},{5,4},{6,14},{7,6},{8,16},{9,1},{1... | collective-permute-start | bytes 2359304 | tf_op jit(solution)/shard_map/ppermute | solution.py:323
  234.7 21.0 %collective-permute-start.35 = (bf16[6,2,1,64,512]{4,3,2,1,0:T(8,128)(2,1)}, bf16[6,2,1,64,512]{4,3,2,1,0:T(8,128)(2,1)S(1)}, u32[]{:S(2)}, u32[]{:S(2)}) collective-permute-start(bf16[6,2,1,64,512]{4,3,2,1,0:T(8,128)(2,1)} %get-tuple-element.137.refs_5_), channel_id=1, source_target_pairs={{0,1},{1,9},{2,3},{3,11},{4,5},{5,13},{6,7},{7,15},{8,0},{9,17},{1... | collective-permute-start | bytes 2359304 | tf_op jit(solution)/shard_map/ppermute | solution.py:323
  238.2 30.2 %collective-permute-start.30 = (bf16[6,2,1,64,512]{4,3,2,1,0:T(8,128)(2,1)}, bf16[6,2,1,64,512]{4,3,2,1,0:T(8,128)(2,1)S(1)}, u32[]{:S(2)}, u32[]{:S(2)}) collective-permute-start(bf16[6,2,1,64,512]{4,3,2,1,0:T(8,128)(2,1)} %get-tuple-element.132.refs_4_), channel_id=1, source_target_pairs={{0,8},{1,0},{2,10},{3,2},{4,12},{5,4},{6,14},{7,6},{8,16},{9,1},{1... | collective-permute-start | bytes 2359304 | tf_op jit(solution)/shard_map/ppermute | solution.py:323
  241.3 27.1 %collective-permute-start.31 = (bf16[6,2,1,64,512]{4,3,2,1,0:T(8,128)(2,1)}, bf16[6,2,1,64,512]{4,3,2,1,0:T(8,128)(2,1)S(1)}, u32[]{:S(2)}, u32[]{:S(2)}) collective-permute-start(bf16[6,2,1,64,512]{4,3,2,1,0:T(8,128)(2,1)} %get-tuple-element.133.refs_5_), channel_id=1, source_target_pairs={{0,1},{1,9},{2,3},{3,11},{4,5},{5,13},{6,7},{7,15},{8,0},{9,17},{1... | collective-permute-start | bytes 2359304 | tf_op jit(solution)/shard_map/ppermute | solution.py:323
  250.3 20.7 %collective-permute-start.33 = (bf16[6,2,1,64,512]{4,3,2,1,0:T(8,128)(2,1)}, bf16[6,2,1,64,512]{4,3,2,1,0:T(8,128)(2,1)S(1)}, u32[]{:S(2)}, u32[]{:S(2)}) collective-permute-start(bf16[6,2,1,64,512]{4,3,2,1,0:T(8,128)(2,1)} %get-tuple-element.135), channel_id=1, source_target_pairs={{0,4},{1,5},{2,6},{3,7},{4,0},{5,1},{6,2},{7,3},{8,12},{9,13},{10,... | collective-permute-start | bytes 2359304 | tf_op jit(solution)/shard_map/ppermute | solution.py:323
  258.7 29.1 %collective-permute-start.36 = (bf16[6,2,1,64,512]{4,3,2,1,0:T(8,128)(2,1)}, bf16[6,2,1,64,512]{4,3,2,1,0:T(8,128)(2,1)S(1)}, u32[]{:S(2)}, u32[]{:S(2)}) collective-permute-start(bf16[6,2,1,64,512]{4,3,2,1,0:T(8,128)(2,1)} %get-tuple-element.139), channel_id=1, source_target_pairs={{0,4},{1,5},{2,6},{3,7},{4,0},{5,1},{6,2},{7,3},{8,12},{9,13},{10,... | collective-permute-start | bytes 2359304 | tf_op jit(solution)/shard_map/ppermute | solution.py:323
  274.0 28.0 %collective-permute-start.37 = (bf16[6,2,1,64,512]{4,3,2,1,0:T(8,128)(2,1)}, bf16[6,2,1,64,512]{4,3,2,1,0:T(8,128)(2,1)S(1)}, u32[]{:S(2)}, u32[]{:S(2)}) collective-permute-start(bf16[6,2,1,64,512]{4,3,2,1,0:T(8,128)(2,1)} %get-tuple-element.141), channel_id=1, source_target_pairs={{0,4},{1,5},{2,6},{3,7},{4,0},{5,1},{6,2},{7,3},{8,12},{9,13},{10,... | collective-permute-start | bytes 2359304 | tf_op jit(solution)/shard_map/ppermute | solution.py:323
  (31 other events, 58.7 us)

commit v2 on v1

--- a/solution.py
+++ b/solution.py
@@ -19,7 +19,7 @@
 PARTS = 4
 EXCHANGES = ((0, 1), (1, 4))
 STEPS = ((0, 0), (0, 1), (1, 0), (0, 2), (1, 1), (2, 0), (1, 2), (3, 0), (2, 1), (3, 1), (2, 2), (3, 2))
-GATHERS = {0: (0,), 2: (1,), 4: (2,), 5: (3,)}
+GATHERS = {0: (0,), 2: (1,), 3: (2,), 4: (3,)}
 TILES = {7: (0,), 9: (1,), 13: (2, 3)}
 SIDE = 6
 VMEM_BYTES = 56 * 1024 * 1024
@@ -279,19 +279,14 @@
     return result
 
 
-def dequantize(voltages, scales):
-    groups = scales.shape[-1]
-    shaped = voltages.reshape(voltages.shape[:-1] + (groups, voltages.shape[-1] // groups))
-    product = shaped.astype(jnp.float32) * scales.astype(jnp.float32)[..., None]
-    return product.astype(jnp.bfloat16).reshape(voltages.shape)
-
-
 def exchange(voltages, scales, freq_count, lanes):
     samples = voltages.shape[3]
     rows = voltages.shape[1] // NB
+    groups = scales.shape[2]
     split = (freq_count, lanes, rows, NB)
-    x = dequantize(voltages.reshape(split + (2, samples)), scales.reshape(split + (1, scales.shape[2])))
-    x = x.transpose(1, 3, 4, 0, 2, 5)
+    factor = scales.astype(jnp.bfloat16).reshape(split + (1, groups, 1))
+    x = voltages.reshape(split + (2, groups, samples // groups)) * factor
+    x = x.reshape(split + (2, samples)).transpose(1, 3, 4, 0, 2, 5)
     if freq_count > 1:
         x = lax.all_to_all(x, "freq", 3, 3, tiled=True)
     positions = lax.axis_size("tile")
@@ -432,8 +427,8 @@
         while known < n and (known <= n - 2 or STEPS[known][0] == part):
             done += turn.arrived(STEPS[known][0], STEPS[known][1] + 1)
             known += 1
-        if n >= 2:
-            done = done + ["got%d" % (n - 2)]
+        if n >= 1:
+            done = done + ["got%d" % max(n - 2, 0)]
         turn.prepare(part, stage, side=(str(n), SIDE), after=done)
         turn.along(part, stage)
         for ready in TILES.get(n, ()):

time: 318 us -> 302 us (0.950)
  other arithmetic: 12.8 us -> 4.79 us
  waiting for transfers between devices: 135 us -> 127 us
  local copies, waits for them, and re-layouts: 27.7 us -> 21.2 us
  starting transfers between devices: 47.4 us -> 53.1 us
    ppermute x38, waiting for transfers between devices: 131 us -> 113 us  [move(): self.arrays[target] = lax.ppermute(self.arrays[source], 'tile', pairs)]
    all_to_all x2, waiting for transfers between devices: 3.76 us -> 14.2 us  [exchange(): x = lax.all_to_all(x, 'tile', 0, 0, axis_index_groups=groups, tiled=True)]
    ppermute x38, starting transfers between devices: 39.3 us -> 45.2 us  [move(): self.arrays[target] = lax.ppermute(self.arrays[source], 'tile', pairs)]
    transpose x2, other arithmetic: 8.74 us -> 3.98 us  [exchange(): x = x.reshape(split + (2, samples)).transpose(1, 3, 4, 0, 2, 5)]
    convert_element_type x4 -> x0, other arithmetic: 4.08 us -> none  [dequantize(): product = shaped.astype(jnp.float32) * scales.astype(jnp.float32)[..., None]]
    unnamed x76 -> x74, local copies, waits for them, and re-layouts: 16.5 us -> 15.9 us
  transfers between devices with their start and end apart: 40 -> 40, of which waited for: 23 -> 20; matrix products, arithmetic and copies ran while one was open for 4% -> 2% of each run, Pallas kernels for 25% -> 26%
where the time goes in v2:
time: 302 us; the launch traced here: 301 us
  waiting for transfers between devices  127 us (42%)
  Pallas kernels  93.5 us (31%)
  starting transfers between devices  53.1 us (18%)
  local copies, waits for them, and re-layouts  21.2 us (7%)
  other arithmetic  4.79 us (2%)
    ppermute x38, waiting for transfers between devices, move(): self.arrays[target] = lax.ppermute(self.arrays[source], 'tile', pairs)  113 us
    pallas_call x4, Pallas kernels, run_tiles(): pl.pallas_call(functools.partial(tiles_kernel, names, plan, lanes, scale,...  50.3 us
    ppermute x38, starting transfers between devices, move(): self.arrays[target] = lax.ppermute(self.arrays[source], 'tile', pairs)  45.2 us
    pallas_call x14, Pallas kernels, run_copies(): pl.pallas_call(functools.partial(copies_kernel, names, len(after), plan,...  32.2 us
    unnamed x74, local copies, waits for them, and re-layouts  15.9 us
    all_to_all x2, waiting for transfers between devices, exchange(): x = lax.all_to_all(x, 'tile', 0, 0, axis_index_groups=groups, tiled=True)  14.2 us
    pallas_call x4, Pallas kernels, run_gather(): pl.pallas_call(functools.partial(gather_kernel, plan, lanes, start), out_...  11 us
    all_to_all x2, starting transfers between devices, exchange(): x = lax.all_to_all(x, 'tile', 0, 0, axis_index_groups=groups, tiled=True)  7.93 us
  transfers between devices with their start and end apart: 40, of which 20 were waited for; matrix products, arithmetic and copies ran while one was open for 2% of the time, Pallas kernels for 26%

profile of v2, /device:TPU:0, one launch (start us, length us, event | category | flops | bytes accessed | tf_op | source)
XLA Modules:
  0.0 300.5 jit_solution(3264599014719902588)
XLA Ops:
  4.0 4.2 %all-to-all-start.1 = ((bf16[4,8,2,1,16,512]{5,4,3,2,1,0:T(8,128)(2,1)}), bf16[4,8,2,1,16,512]{5,4,3,2,1,0:T(8,128)(2,1)}, u32[]{:S(2)}, u32[]{:S(2)}) async-start(bf16[4,8,2,1,16,512]{5,4,3,2,1,0:T(8,128)(2,1)} %fusion.1), calls=%async_computation.1 | async-start | bytes 2097152 | tf_op jit(solution)/shard_map/all_to_all | solution.py:294
  10.7 2.6 fusion
  13.3 10.1 %all-to-all-done.1.own = bf16[4,8,2,1,16,512]{5,4,3,2,1,0:T(8,128)(2,1)} async-done(((bf16[4,8,2,1,16,512]{5,4,3,2,1,0:T(8,128)(2,1)}), bf16[4,8,2,1,16,512]{5,4,3,2,1,0:T(8,128)(2,1)}, u32[]{:S(2)}, u32[]{:S(2)}) %all-to-all-start.1) | async-done | bytes 1048608 | tf_op jit(solution)/shard_map/all_to_all | solution.py:294
  23.4 3.7 %all-to-all-start = ((bf16[4,8,2,1,16,1536]{5,4,3,2,1,0:T(8,128)(2,1)}), bf16[4,8,2,1,16,1536]{5,4,3,2,1,0:T(8,128)(2,1)S(1)}, u32[]{:S(2)}, u32[]{:S(2)}) async-start(bf16[4,8,2,1,16,1536]{5,4,3,2,1,0:T(8,128)(2,1)} %fusion), calls=%async_computation | async-start | bytes 6291456 | tf_op jit(solution)/shard_map/all_to_all | solution.py:294
  27.7 2.7 gather.4
  32.4 2.4 collective-permute-start
  36.4 15.5 %collective-permute-done.2.refs_5_.refs_8_ = bf16[5,2,1,64,512]{4,3,2,1,0:T(8,128)(2,1)S(1)} collective-permute-done((bf16[5,2,1,64,512]{4,3,2,1,0:T(8,128)(2,1)}, bf16[5,2,1,64,512]{4,3,2,1,0:T(8,128)(2,1)S(1)}, u32[]{:S(2)}, u32[]{:S(2)}) %collective-permute-start.2) | collective-permute-done | bytes 655392 | tf_op jit(solution)/shard_map/ppermute | solution.py:318
  54.1 2.8 pick.15
  59.9 4.1 %all-to-all-done.own = bf16[4,8,2,1,16,1536]{5,4,3,2,1,0:T(8,128)(2,1)S(1)} async-done(((bf16[4,8,2,1,16,1536]{5,4,3,2,1,0:T(8,128)(2,1)}), bf16[4,8,2,1,16,1536]{5,4,3,2,1,0:T(8,128)(2,1)S(1)}, u32[]{:S(2)}, u32[]{:S(2)}) %all-to-all-start) | async-done | bytes 3145760 | tf_op jit(solution)/shard_map/all_to_all | solution.py:294
  65.7 2.7 gather.5
  68.4 2.0 pick.16
  70.4 2.4 collective-permute-start.3
  72.9 3.7 %collective-permute-done.5.refs_4_ = bf16[6,2,1,64,512]{4,3,2,1,0:T(8,128)(2,1)} collective-permute-done((bf16[6,2,1,64,512]{4,3,2,1,0:T(8,128)(2,1)}, bf16[6,2,1,64,512]{4,3,2,1,0:T(8,128)(2,1)}, u32[]{:S(2)}, u32[]{:S(2)}) %collective-permute-start.5) | collective-permute-done | bytes 786464 | tf_op jit(solution)/shard_map/ppermute | solution.py:318
  78.2 2.8 gather.6
  81.0 2.1 pick.17
  83.6 9.7 %collective-permute-done.3.refs_4_ = bf16[6,2,1,64,512]{4,3,2,1,0:T(8,128)(2,1)S(1)} collective-permute-done((bf16[6,2,1,64,512]{4,3,2,1,0:T(8,128)(2,1)}, bf16[6,2,1,64,512]{4,3,2,1,0:T(8,128)(2,1)S(1)}, u32[]{:S(2)}, u32[]{:S(2)}) %collective-permute-start.3) | collective-permute-done | bytes 786464 | tf_op jit(solution)/shard_map/ppermute | solution.py:318
  93.4 2.4 collective-permute-start.9
  95.8 2.8 gather.7
  99.7 2.9 pick.18
  103.5 4.9 %collective-permute-done.10.refs_5_.refs_7_ = bf16[6,2,1,64,512]{4,3,2,1,0:T(8,128)(2,1)S(1)} collective-permute-done((bf16[6,2,1,64,512]{4,3,2,1,0:T(8,128)(2,1)}, bf16[6,2,1,64,512]{4,3,2,1,0:T(8,128)(2,1)S(1)}, u32[]{:S(2)}, u32[]{:S(2)}) %collective-permute-start.10) | collective-permute-done | bytes 786464 | tf_op jit(solution)/shard_map/ppermute | solution.py:318
  110.3 3.7 %collective-permute-done.11.refs_7_.refs_11_.refs_8_ = bf16[6,2,1,64,512]{4,3,2,1,0:T(8,128)(2,1)S(1)} collective-permute-done((bf16[6,2,1,64,512]{4,3,2,1,0:T(8,128)(2,1)}, bf16[6,2,1,64,512]{4,3,2,1,0:T(8,128)(2,1)S(1)}, u32[]{:S(2)}, u32[]{:S(2)}) %collective-permute-start.11) | collective-permute-done | bytes 786464 | tf_op jit(solution)/shard_map/ppermute | solution.py:318
  115.2 2.1 pick.19
  117.3 2.1 collective-permute-start.12
  119.4 11.1 %collective-permute-done.14.refs_4_ = bf16[6,2,1,64,512]{4,3,2,1,0:T(8,128)(2,1)S(1)} collective-permute-done((bf16[6,2,1,64,512]{4,3,2,1,0:T(8,128)(2,1)}, bf16[6,2,1,64,512]{4,3,2,1,0:T(8,128)(2,1)S(1)}, u32[]{:S(2)}, u32[]{:S(2)}) %collective-permute-start.14) | collective-permute-done | bytes 786464 | tf_op jit(solution)/shard_map/ppermute | solution.py:318
  133.6 2.1 pick.20
  135.8 3.1 %collective-permute-start.20 = (bf16[6,2,1,64,512]{4,3,2,1,0:T(8,128)(2,1)}, bf16[6,2,1,64,512]{4,3,2,1,0:T(8,128)(2,1)S(1)}, u32[]{:S(2)}, u32[]{:S(2)}) collective-permute-start(bf16[6,2,1,64,512]{4,3,2,1,0:T(8,128)(2,1)} %get-tuple-element.115.refs_4_), channel_id=1, source_target_pairs={{0,8},{1,0},{2,10},{3,2},{4,12},{5,4},{6,14},{7,6},{8,16},{9,1},{1... | collective-permute-start | bytes 2359304 | tf_op jit(solution)/shard_map/ppermute | solution.py:318
  138.9 8.4 %collective-permute-done.12.refs_4_ = bf16[6,2,1,64,512]{4,3,2,1,0:T(8,128)(2,1)S(1)} collective-permute-done((bf16[6,2,1,64,512]{4,3,2,1,0:T(8,128)(2,1)}, bf16[6,2,1,64,512]{4,3,2,1,0:T(8,128)(2,1)S(1)}, u32[]{:S(2)}, u32[]{:S(2)}) %collective-permute-start.12) | collective-permute-done | bytes 786464 | tf_op jit(solution)/shard_map/ppermute | solution.py:318
  150.5 2.1 pick.21
  152.7 2.4 collective-permute-start.18
  155.1 9.1 %collective-permute-done.20.refs_6_ = bf16[6,2,1,64,512]{4,3,2,1,0:T(8,128)(2,1)S(1)} collective-permute-done((bf16[6,2,1,64,512]{4,3,2,1,0:T(8,128)(2,1)}, bf16[6,2,1,64,512]{4,3,2,1,0:T(8,128)(2,1)S(1)}, u32[]{:S(2)}, u32[]{:S(2)}) %collective-permute-start.20) | collective-permute-done | bytes 786464 | tf_op jit(solution)/shard_map/ppermute | solution.py:318
  166.2 9.6 %tiles.4 = (f32[5,512,1024]{2,1,0:T(8,128)}, s32[8,128]{1,0:T(8,128)}) custom-call(bf16[6,2,1,64,512]{4,3,2,1,0:T(8,128)(2,1)} %get-tuple-element.79.refs_0_, bf16[6,2,1,64,512]{4,3,2,1,0:T(8,128)(2,1)} %get-tuple-element.80.refs_1_, bf16[6,2,1,64,512]{4,3,2,1,0:T(8,128)(2,1)} %get-tuple-element.83.refs_0_.refs_2_, ...), custom_call_target="tpu_custom_call", output_to_operand_aliasing={{1}: (13, {})} | custom-call | tf_op jit(solution)/shard_map/tiles/pallas_call | solution.py:264
  176.9 2.9 pick.22
  183.7 2.8 pick.23
  188.3 9.3 %collective-permute-done.28.refs_12_.refs_9_.refs_13_.refs_8_ = bf16[6,2,1,64,512]{4,3,2,1,0:T(8,128)(2,1)S(1)} collective-permute-done((bf16[6,2,1,64,512]{4,3,2,1,0:T(8,128)(2,1)}, bf16[6,2,1,64,512]{4,3,2,1,0:T(8,128)(2,1)S(1)}, u32[]{:S(2)}, u32[]{:S(2)}) %collective-permute-start.28) | collective-permute-done | bytes 786464 | tf_op jit(solution)/shard_map/ppermute | solution.py:318
  199.3 13.3 %tiles.5 = (f32[5,512,1024]{2,1,0:T(8,128)}, s32[8,128]{1,0:T(8,128)}) custom-call(bf16[6,2,1,64,512]{4,3,2,1,0:T(8,128)(2,1)} %get-tuple-element.92.refs_0_, bf16[6,2,1,64,512]{4,3,2,1,0:T(8,128)(2,1)} %get-tuple-element.93.refs_1_, bf16[6,2,1,64,512]{4,3,2,1,0:T(8,128)(2,1)} %get-tuple-element.99.refs_2_, ...), custom_call_target="tpu_custom_call", output_to_operand_aliasing={{0}: (13, {}), {1}: (14, {})} | custom-call | tf_op jit(solution)/shard_map/tiles/pallas_call | solution.py:264
  213.8 2.1 pick.24
  216.9 2.9 collective-permute-start.34
  221.2 2.1 pick.25
  223.3 2.6 collective-permute-start.30
  225.9 7.8 %collective-permute-done.32.refs_9_.refs_14_.refs_10_ = bf16[6,2,1,64,512]{4,3,2,1,0:T(8,128)(2,1)S(1)} collective-permute-done((bf16[6,2,1,64,512]{4,3,2,1,0:T(8,128)(2,1)}, bf16[6,2,1,64,512]{4,3,2,1,0:T(8,128)(2,1)S(1)}, u32[]{:S(2)}, u32[]{:S(2)}) %collective-permute-start.32) | collective-permute-done | bytes 786464 | tf_op jit(solution)/shard_map/ppermute | solution.py:318
  234.6 3.5 %collective-permute-done.34.refs_6_ = bf16[6,2,1,64,512]{4,3,2,1,0:T(8,128)(2,1)S(1)} collective-permute-done((bf16[6,2,1,64,512]{4,3,2,1,0:T(8,128)(2,1)}, bf16[6,2,1,64,512]{4,3,2,1,0:T(8,128)(2,1)S(1)}, u32[]{:S(2)}, u32[]{:S(2)}) %collective-permute-start.34) | collective-permute-done | bytes 786464 | tf_op jit(solution)/shard_map/ppermute | solution.py:318
  238.1 2.4 collective-permute-done.35.refs_7_
  241.4 2.1 pick.26
  244.7 7.1 %collective-permute-done.30.refs_4_.refs_6_ = bf16[6,2,1,64,512]{4,3,2,1,0:T(8,128)(2,1)S(1)} collective-permute-done((bf16[6,2,1,64,512]{4,3,2,1,0:T(8,128)(2,1)}, bf16[6,2,1,64,512]{4,3,2,1,0:T(8,128)(2,1)S(1)}, u32[]{:S(2)}, u32[]{:S(2)}) %collective-permute-start.30) | collective-permute-done | bytes 786464 | tf_op jit(solution)/shard_map/ppermute | solution.py:318
  251.8 2.6 collective-permute-done.33.refs_7_.refs_11_
  259.5 11.7 %collective-permute-done.36.refs_15_.refs_12_ = bf16[6,2,1,64,512]{4,3,2,1,0:T(8,128)(2,1)S(1)} collective-permute-done((bf16[6,2,1,64,512]{4,3,2,1,0:T(8,128)(2,1)}, bf16[6,2,1,64,512]{4,3,2,1,0:T(8,128)(2,1)S(1)}, u32[]{:S(2)}, u32[]{:S(2)}) %collective-permute-start.36) | collective-permute-done | bytes 786464 | tf_op jit(solution)/shard_map/ppermute | solution.py:318
  272.1 13.3 %tiles.6 = (f32[5,512,1024]{2,1,0:T(8,128)}, s32[8,128]{1,0:T(8,128)}) custom-call(bf16[6,2,1,64,512]{4,3,2,1,0:T(8,128)(2,1)} %get-tuple-element.105.refs_2_.refs_0_, bf16[6,2,1,64,512]{4,3,2,1,0:T(8,128)(2,1)} %get-tuple-element.106.refs_3_.refs_1_, ...), custom_call_target="tpu_custom_call", output_to_operand_aliasing={{0}: (16, {}), {1}: (17, {})} | custom-call | tf_op jit(solution)/shard_map/tiles/pallas_call | solution.py:264
  286.3 14.0 %tiles.7 = (f32[5,512,1024]{2,1,0:T(8,128)}, s32[8,128]{1,0:T(8,128)}) custom-call(bf16[6,2,1,64,512]{4,3,2,1,0:T(8,128)(2,1)} %get-tuple-element.113.refs_2_.refs_0_, bf16[6,2,1,64,512]{4,3,2,1,0:T(8,128)(2,1)} %get-tuple-element.114.refs_3_.refs_1_, ...), custom_call_target="tpu_custom_call", output_to_operand_aliasing={{0}: (15, {}), {1}: (16, {})} | custom-call | tf_op jit(solution)/shard_map/tiles/pallas_call | solution.py:264
  (147 shorter events, 54.6 us)
Async XLA Ops:
  0.0 2.4 slice-start
  4.0 19.4 %all-to-all-start.1 = ((bf16[4,8,2,1,16,512]{5,4,3,2,1,0:T(8,128)(2,1)}), bf16[4,8,2,1,16,512]{5,4,3,2,1,0:T(8,128)(2,1)}, u32[]{:S(2)}, u32[]{:S(2)}) async-start(bf16[4,8,2,1,16,512]{5,4,3,2,1,0:T(8,128)(2,1)} %fusion.1), calls=%async_computation.1 | async-start | bytes 2097152 | tf_op jit(solution)/shard_map/all_to_all | solution.py:294
  23.4 40.6 %all-to-all-start = ((bf16[4,8,2,1,16,1536]{5,4,3,2,1,0:T(8,128)(2,1)}), bf16[4,8,2,1,16,1536]{5,4,3,2,1,0:T(8,128)(2,1)S(1)}, u32[]{:S(2)}, u32[]{:S(2)}) async-start(bf16[4,8,2,1,16,1536]{5,4,3,2,1,0:T(8,128)(2,1)} %fusion), calls=%async_computation | async-start | bytes 6291456 | tf_op jit(solution)/shard_map/all_to_all | solution.py:294
  32.4 20.2 %collective-permute-start = (bf16[6,2,1,64,512]{4,3,2,1,0:T(8,128)(2,1)}, bf16[6,2,1,64,512]{4,3,2,1,0:T(8,128)(2,1)S(1)}, u32[]{:S(2)}, u32[]{:S(2)}) collective-permute-start(bf16[6,2,1,64,512]{4,3,2,1,0:T(8,128)(2,1)} %get-tuple-element.79.refs_0_), channel_id=1, source_target_pairs={{0,8},{1,0},{2,10},{3,2},{4,12},{5,4},{6,14},{7,6},{8,16},{9,1},{1... | collective-permute-start | bytes 2359304 | tf_op jit(solution)/shard_map/ppermute | solution.py:318
  34.8 18.4 %collective-permute-start.1 = (bf16[6,2,1,64,512]{4,3,2,1,0:T(8,128)(2,1)}, bf16[6,2,1,64,512]{4,3,2,1,0:T(8,128)(2,1)S(1)}, u32[]{:S(2)}, u32[]{:S(2)}) collective-permute-start(bf16[6,2,1,64,512]{4,3,2,1,0:T(8,128)(2,1)} %get-tuple-element.80.refs_1_), channel_id=1, source_target_pairs={{0,1},{1,9},{2,3},{3,11},{4,5},{5,13},{6,7},{7,15},{8,0},{9,17},{1... | collective-permute-start | bytes 2359304 | tf_op jit(solution)/shard_map/ppermute | solution.py:318
  34.8 17.1 %collective-permute-start.2 = (bf16[5,2,1,64,512]{4,3,2,1,0:T(8,128)(2,1)}, bf16[5,2,1,64,512]{4,3,2,1,0:T(8,128)(2,1)S(1)}, u32[]{:S(2)}, u32[]{:S(2)}) collective-permute-start(bf16[5,2,1,64,512]{4,3,2,1,0:T(8,128)(2,1)} %get-tuple-element.82), channel_id=1, source_target_pairs={{0,4},{1,5},{2,6},{3,7},{4,0},{5,1},{6,2},{7,3},{8,12},{9,13},{10,... | collective-permute-start | bytes 1966088 | tf_op jit(solution)/shard_map/ppermute | solution.py:318
  56.9 19.6 %collective-permute-start.5 = (bf16[6,2,1,64,512]{4,3,2,1,0:T(8,128)(2,1)}, bf16[6,2,1,64,512]{4,3,2,1,0:T(8,128)(2,1)}, u32[]{:S(2)}, u32[]{:S(2)}) collective-permute-start(bf16[6,2,1,64,512]{4,3,2,1,0:T(8,128)(2,1)} %get-tuple-element.83.refs_0_.refs_2_), channel_id=1, source_target_pairs={{0,8},{1,0},{2,10},{3,2},{4,12},{5,4},{6,14},{7,6},{8,16},{9,1},{1... | collective-permute-start | bytes 2359304 | tf_op jit(solution)/shard_map/ppermute | solution.py:318
  58.2 22.8 %collective-permute-start.6 = (bf16[6,2,1,64,512]{4,3,2,1,0:T(8,128)(2,1)}, bf16[6,2,1,64,512]{4,3,2,1,0:T(8,128)(2,1)}, u32[]{:S(2)}, u32[]{:S(2)}) collective-permute-start(bf16[6,2,1,64,512]{4,3,2,1,0:T(8,128)(2,1)} %get-tuple-element.84.refs_1_.refs_3_), channel_id=1, source_target_pairs={{0,1},{1,9},{2,3},{3,11},{4,5},{5,13},{6,7},{7,15},{8,0},{9,17},{1... | collective-permute-start | bytes 2359304 | tf_op jit(solution)/shard_map/ppermute | solution.py:318
  58.2 22.8 %collective-permute-start.7 = (bf16[6,2,1,64,512]{4,3,2,1,0:T(8,128)(2,1)}, bf16[6,2,1,64,512]{4,3,2,1,0:T(8,128)(2,1)}, u32[]{:S(2)}, u32[]{:S(2)}) collective-permute-start(bf16[6,2,1,64,512]{4,3,2,1,0:T(8,128)(2,1)} %get-tuple-element.95), channel_id=1, source_target_pairs={{0,4},{1,5},{2,6},{3,7},{4,0},{5,1},{6,2},{7,3},{8,12},{9,13},{10,... | collective-permute-start | bytes 2359304 | tf_op jit(solution)/shard_map/ppermute | solution.py:318
  70.4 23.0 %collective-permute-start.3 = (bf16[6,2,1,64,512]{4,3,2,1,0:T(8,128)(2,1)}, bf16[6,2,1,64,512]{4,3,2,1,0:T(8,128)(2,1)S(1)}, u32[]{:S(2)}, u32[]{:S(2)}) collective-permute-start(bf16[6,2,1,64,512]{4,3,2,1,0:T(8,128)(2,1)} %get-tuple-element.92.refs_0_), channel_id=1, source_target_pairs={{0,8},{1,0},{2,10},{3,2},{4,12},{5,4},{6,14},{7,6},{8,16},{9,1},{1... | collective-permute-start | bytes 2359304 | tf_op jit(solution)/shard_map/ppermute | solution.py:318
  72.9 25.7 %collective-permute-start.4 = (bf16[6,2,1,64,512]{4,3,2,1,0:T(8,128)(2,1)}, bf16[6,2,1,64,512]{4,3,2,1,0:T(8,128)(2,1)S(1)}, u32[]{:S(2)}, u32[]{:S(2)}) collective-permute-start(bf16[6,2,1,64,512]{4,3,2,1,0:T(8,128)(2,1)} %get-tuple-element.93.refs_1_), channel_id=1, source_target_pairs={{0,1},{1,9},{2,3},{3,11},{4,5},{5,13},{6,7},{7,15},{8,0},{9,17},{1... | collective-permute-start | bytes 2359304 | tf_op jit(solution)/shard_map/ppermute | solution.py:318
  76.5 22.0 %collective-permute-start.8 = (bf16[6,2,1,64,512]{4,3,2,1,0:T(8,128)(2,1)}, bf16[6,2,1,64,512]{4,3,2,1,0:T(8,128)(2,1)S(1)}, u32[]{:S(2)}, u32[]{:S(2)}) collective-permute-start(bf16[6,2,1,64,512]{4,3,2,1,0:T(8,128)(2,1)} %get-tuple-element.98), channel_id=1, source_target_pairs={{0,4},{1,5},{2,6},{3,7},{4,0},{5,1},{6,2},{7,3},{8,12},{9,13},{10,... | collective-permute-start | bytes 2359304 | tf_op jit(solution)/shard_map/ppermute | solution.py:318
  83.2 25.2 %collective-permute-start.10 = (bf16[6,2,1,64,512]{4,3,2,1,0:T(8,128)(2,1)}, bf16[6,2,1,64,512]{4,3,2,1,0:T(8,128)(2,1)S(1)}, u32[]{:S(2)}, u32[]{:S(2)}) collective-permute-start(bf16[6,2,1,64,512]{4,3,2,1,0:T(8,128)(2,1)} %get-tuple-element.102.refs_5_), channel_id=1, source_target_pairs={{0,1},{1,9},{2,3},{3,11},{4,5},{5,13},{6,7},{7,15},{8,0},{9,17},{1... | collective-permute-start | bytes 2359304 | tf_op jit(solution)/shard_map/ppermute | solution.py:318
  83.2 30.9 %collective-permute-start.11 = (bf16[6,2,1,64,512]{4,3,2,1,0:T(8,128)(2,1)}, bf16[6,2,1,64,512]{4,3,2,1,0:T(8,128)(2,1)S(1)}, u32[]{:S(2)}, u32[]{:S(2)}) collective-permute-start(bf16[6,2,1,64,512]{4,3,2,1,0:T(8,128)(2,1)} %get-tuple-element.104), channel_id=1, source_target_pairs={{0,4},{1,5},{2,6},{3,7},{4,0},{5,1},{6,2},{7,3},{8,12},{9,13},{10,... | collective-permute-start | bytes 2359304 | tf_op jit(solution)/shard_map/ppermute | solution.py:318
  93.4 5.2 %copy-start.14 = (bf16[6,2,1,64,512]{4,3,2,1,0:T(8,128)(2,1)}, bf16[6,2,1,64,512]{4,3,2,1,0:T(8,128)(2,1)S(1)}, u32[]{:S(2)}) copy-start(bf16[6,2,1,64,512]{4,3,2,1,0:T(8,128)(2,1)S(1)} %collective-permute-done.3.refs_4_) | copy-start | bytes 2359300
  93.4 20.7 %collective-permute-start.9 = (bf16[6,2,1,64,512]{4,3,2,1,0:T(8,128)(2,1)}, bf16[6,2,1,64,512]{4,3,2,1,0:T(8,128)(2,1)S(1)}, u32[]{:S(2)}, u32[]{:S(2)}) collective-permute-start(bf16[6,2,1,64,512]{4,3,2,1,0:T(8,128)(2,1)} %get-tuple-element.101.refs_4_), channel_id=1, source_target_pairs={{0,8},{1,0},{2,10},{3,2},{4,12},{5,4},{6,14},{7,6},{8,16},{9,1},{1... | collective-permute-start | bytes 2359304 | tf_op jit(solution)/shard_map/ppermute | solution.py:318
  102.6 27.9 %collective-permute-start.14 = (bf16[6,2,1,64,512]{4,3,2,1,0:T(8,128)(2,1)}, bf16[6,2,1,64,512]{4,3,2,1,0:T(8,128)(2,1)S(1)}, u32[]{:S(2)}, u32[]{:S(2)}) collective-permute-start(bf16[6,2,1,64,512]{4,3,2,1,0:T(8,128)(2,1)} %get-tuple-element.99.refs_2_), channel_id=1, source_target_pairs={{0,8},{1,0},{2,10},{3,2},{4,12},{5,4},{6,14},{7,6},{8,16},{9,1},{1... | collective-permute-start | bytes 2359304 | tf_op jit(solution)/shard_map/ppermute | solution.py:318
  103.5 28.9 %collective-permute-start.15 = (bf16[6,2,1,64,512]{4,3,2,1,0:T(8,128)(2,1)}, bf16[6,2,1,64,512]{4,3,2,1,0:T(8,128)(2,1)S(1)}, u32[]{:S(2)}, u32[]{:S(2)}) collective-permute-start(bf16[6,2,1,64,512]{4,3,2,1,0:T(8,128)(2,1)} %get-tuple-element.100.refs_3_), channel_id=1, source_target_pairs={{0,1},{1,9},{2,3},{3,11},{4,5},{5,13},{6,7},{7,15},{8,0},{9,17},{1... | collective-permute-start | bytes 2359304 | tf_op jit(solution)/shard_map/ppermute | solution.py:318
  108.4 5.7 %copy-start.33 = (bf16[6,2,1,64,512]{4,3,2,1,0:T(8,128)(2,1)}, bf16[6,2,1,64,512]{4,3,2,1,0:T(8,128)(2,1)S(1)}, u32[]{:S(2)}) copy-start(bf16[6,2,1,64,512]{4,3,2,1,0:T(8,128)(2,1)S(1)} %collective-permute-done.10.refs_5_.refs_7_) | copy-start | bytes 2359300
  108.4 24.1 %collective-permute-start.16 = (bf16[6,2,1,64,512]{4,3,2,1,0:T(8,128)(2,1)}, bf16[6,2,1,64,512]{4,3,2,1,0:T(8,128)(2,1)S(1)}, u32[]{:S(2)}, u32[]{:S(2)}) collective-permute-start(bf16[6,2,1,64,512]{4,3,2,1,0:T(8,128)(2,1)} %get-tuple-element.110), channel_id=1, source_target_pairs={{0,4},{1,5},{2,6},{3,7},{4,0},{5,1},{6,2},{7,3},{8,12},{9,13},{10,... | collective-permute-start | bytes 2359304 | tf_op jit(solution)/shard_map/ppermute | solution.py:318
  117.3 30.0 %collective-permute-start.12 = (bf16[6,2,1,64,512]{4,3,2,1,0:T(8,128)(2,1)}, bf16[6,2,1,64,512]{4,3,2,1,0:T(8,128)(2,1)S(1)}, u32[]{:S(2)}, u32[]{:S(2)}) collective-permute-start(bf16[6,2,1,64,512]{4,3,2,1,0:T(8,128)(2,1)} %get-tuple-element.105.refs_2_.refs_0_), channel_id=1, source_target_pairs={{0,8},{1,0},{2,10},{3,2},{4,12},{5,4},{6,14},{7,6},{8,16},{9,1},{1... | collective-permute-start | bytes 2359304 | tf_op jit(solution)/shard_map/ppermute | solution.py:318
  119.4 29.9 %collective-permute-start.13 = (bf16[6,2,1,64,512]{4,3,2,1,0:T(8,128)(2,1)}, bf16[6,2,1,64,512]{4,3,2,1,0:T(8,128)(2,1)S(1)}, u32[]{:S(2)}, u32[]{:S(2)}) collective-permute-start(bf16[6,2,1,64,512]{4,3,2,1,0:T(8,128)(2,1)} %get-tuple-element.106.refs_3_.refs_1_), channel_id=1, source_target_pairs={{0,1},{1,9},{2,3},{3,11},{4,5},{5,13},{6,7},{7,15},{8,0},{9,17},{1... | collective-permute-start | bytes 2359304 | tf_op jit(solution)/shard_map/ppermute | solution.py:318
  130.5 18.8 %collective-permute-start.17 = (bf16[6,2,1,64,512]{4,3,2,1,0:T(8,128)(2,1)}, bf16[6,2,1,64,512]{4,3,2,1,0:T(8,128)(2,1)S(1)}, u32[]{:S(2)}, u32[]{:S(2)}) collective-permute-start(bf16[6,2,1,64,512]{4,3,2,1,0:T(8,128)(2,1)} %get-tuple-element.112), channel_id=1, source_target_pairs={{0,4},{1,5},{2,6},{3,7},{4,0},{5,1},{6,2},{7,3},{8,12},{9,13},{10,... | collective-permute-start | bytes 2359304 | tf_op jit(solution)/shard_map/ppermute | solution.py:318
  135.8 28.4 %collective-permute-start.20 = (bf16[6,2,1,64,512]{4,3,2,1,0:T(8,128)(2,1)}, bf16[6,2,1,64,512]{4,3,2,1,0:T(8,128)(2,1)S(1)}, u32[]{:S(2)}, u32[]{:S(2)}) collective-permute-start(bf16[6,2,1,64,512]{4,3,2,1,0:T(8,128)(2,1)} %get-tuple-element.115.refs_4_), channel_id=1, source_target_pairs={{0,8},{1,0},{2,10},{3,2},{4,12},{5,4},{6,14},{7,6},{8,16},{9,1},{1... | collective-permute-start | bytes 2359304 | tf_op jit(solution)/shard_map/ppermute | solution.py:318
  138.9 36.9 %collective-permute-start.21 = (bf16[6,2,1,64,512]{4,3,2,1,0:T(8,128)(2,1)}, bf16[6,2,1,64,512]{4,3,2,1,0:T(8,128)(2,1)S(1)}, u32[]{:S(2)}, u32[]{:S(2)}) collective-permute-start(bf16[6,2,1,64,512]{4,3,2,1,0:T(8,128)(2,1)} %get-tuple-element.116.refs_5_), channel_id=1, source_target_pairs={{0,1},{1,9},{2,3},{3,11},{4,5},{5,13},{6,7},{7,15},{8,0},{9,17},{1... | collective-permute-start | bytes 2359304 | tf_op jit(solution)/shard_map/ppermute | solution.py:318
  147.3 28.5 %collective-permute-start.22 = (bf16[6,2,1,64,512]{4,3,2,1,0:T(8,128)(2,1)}, bf16[6,2,1,64,512]{4,3,2,1,0:T(8,128)(2,1)S(1)}, u32[]{:S(2)}, u32[]{:S(2)}) collective-permute-start(bf16[6,2,1,64,512]{4,3,2,1,0:T(8,128)(2,1)} %get-tuple-element.119), channel_id=1, source_target_pairs={{0,4},{1,5},{2,6},{3,7},{4,0},{5,1},{6,2},{7,3},{8,12},{9,13},{10,... | collective-permute-start | bytes 2359304 | tf_op jit(solution)/shard_map/ppermute | solution.py:318
  152.7 29.1 %collective-permute-start.18 = (bf16[6,2,1,64,512]{4,3,2,1,0:T(8,128)(2,1)}, bf16[6,2,1,64,512]{4,3,2,1,0:T(8,128)(2,1)S(1)}, u32[]{:S(2)}, u32[]{:S(2)}) collective-permute-start(bf16[6,2,1,64,512]{4,3,2,1,0:T(8,128)(2,1)} %get-tuple-element.113.refs_2_.refs_0_), channel_id=1, source_target_pairs={{0,8},{1,0},{2,10},{3,2},{4,12},{5,4},{6,14},{7,6},{8,16},{9,1},{1... | collective-permute-start | bytes 2359304 | tf_op jit(solution)/shard_map/ppermute | solution.py:318
  155.0 26.8 %collective-permute-start.19 = (bf16[6,2,1,64,512]{4,3,2,1,0:T(8,128)(2,1)}, bf16[6,2,1,64,512]{4,3,2,1,0:T(8,128)(2,1)S(1)}, u32[]{:S(2)}, u32[]{:S(2)}) collective-permute-start(bf16[6,2,1,64,512]{4,3,2,1,0:T(8,128)(2,1)} %get-tuple-element.114.refs_3_.refs_1_), channel_id=1, source_target_pairs={{0,1},{1,9},{2,3},{3,11},{4,5},{5,13},{6,7},{7,15},{8,0},{9,17},{1... | collective-permute-start | bytes 2359304 | tf_op jit(solution)/shard_map/ppermute | solution.py:318
  164.2 11.6 %copy-start.26 = (bf16[6,2,1,64,512]{4,3,2,1,0:T(8,128)(2,1)}, bf16[6,2,1,64,512]{4,3,2,1,0:T(8,128)(2,1)S(1)}, u32[]{:S(2)}) copy-start(bf16[6,2,1,64,512]{4,3,2,1,0:T(8,128)(2,1)S(1)} %collective-permute-done.20.refs_6_) | copy-start | bytes 2359300
  164.2 18.6 %collective-permute-start.23 = (bf16[6,2,1,64,512]{4,3,2,1,0:T(8,128)(2,1)}, bf16[6,2,1,64,512]{4,3,2,1,0:T(8,128)(2,1)S(1)}, u32[]{:S(2)}, u32[]{:S(2)}) collective-permute-start(bf16[6,2,1,64,512]{4,3,2,1,0:T(8,128)(2,1)} %get-tuple-element.121), channel_id=1, source_target_pairs={{0,4},{1,5},{2,6},{3,7},{4,0},{5,1},{6,2},{7,3},{8,12},{9,13},{10,... | collective-permute-start | bytes 2359304 | tf_op jit(solution)/shard_map/ppermute | solution.py:318
  179.8 17.8 %collective-permute-start.28 = (bf16[6,2,1,64,512]{4,3,2,1,0:T(8,128)(2,1)}, bf16[6,2,1,64,512]{4,3,2,1,0:T(8,128)(2,1)S(1)}, u32[]{:S(2)}, u32[]{:S(2)}) collective-permute-start(bf16[6,2,1,64,512]{4,3,2,1,0:T(8,128)(2,1)} %get-tuple-element.126), channel_id=1, source_target_pairs={{0,4},{1,5},{2,6},{3,7},{4,0},{5,1},{6,2},{7,3},{8,12},{9,13},{10,... | collective-permute-start | bytes 2359304 | tf_op jit(solution)/shard_map/ppermute | solution.py:318
  180.2 32.5 %collective-permute-start.26 = (bf16[6,2,1,64,512]{4,3,2,1,0:T(8,128)(2,1)}, bf16[6,2,1,64,512]{4,3,2,1,0:T(8,128)(2,1)S(1)}, u32[]{:S(2)}, u32[]{:S(2)}) collective-permute-start(bf16[6,2,1,64,512]{4,3,2,1,0:T(8,128)(2,1)} %get-tuple-element.124.refs_2_), channel_id=1, source_target_pairs={{0,8},{1,0},{2,10},{3,2},{4,12},{5,4},{6,14},{7,6},{8,16},{9,1},{1... | collective-permute-start | bytes 2359304 | tf_op jit(solution)/shard_map/ppermute | solution.py:318
  181.8 30.9 %collective-permute-start.27 = (bf16[6,2,1,64,512]{4,3,2,1,0:T(8,128)(2,1)}, bf16[6,2,1,64,512]{4,3,2,1,0:T(8,128)(2,1)S(1)}, u32[]{:S(2)}, u32[]{:S(2)}) collective-permute-start(bf16[6,2,1,64,512]{4,3,2,1,0:T(8,128)(2,1)} %get-tuple-element.125.refs_3_), channel_id=1, source_target_pairs={{0,1},{1,9},{2,3},{3,11},{4,5},{5,13},{6,7},{7,15},{8,0},{9,17},{1... | collective-permute-start | bytes 2359304 | tf_op jit(solution)/shard_map/ppermute | solution.py:318
  186.5 33.3 %collective-permute-start.24 = (bf16[6,2,1,64,512]{4,3,2,1,0:T(8,128)(2,1)}, bf16[6,2,1,64,512]{4,3,2,1,0:T(8,128)(2,1)S(1)}, u32[]{:S(2)}, u32[]{:S(2)}) collective-permute-start(bf16[6,2,1,64,512]{4,3,2,1,0:T(8,128)(2,1)} %get-tuple-element.122.refs_4_.refs_2_.refs_0_), channel_id=1, source_target_pairs={{0,8},{1,0},{2,10},{3,2},{4,12},{5,4},{6,14},{7,6},{8,16},{9,1},{1... | collective-permute-start | bytes 2359304 | tf_op jit(solution)/shard_map/ppermute | solution.py:318
  188.3 31.6 %collective-permute-start.25 = (bf16[6,2,1,64,512]{4,3,2,1,0:T(8,128)(2,1)}, bf16[6,2,1,64,512]{4,3,2,1,0:T(8,128)(2,1)S(1)}, u32[]{:S(2)}, u32[]{:S(2)}) collective-permute-start(bf16[6,2,1,64,512]{4,3,2,1,0:T(8,128)(2,1)} %get-tuple-element.123.refs_5_.refs_3_.refs_1_), channel_id=1, source_target_pairs={{0,1},{1,9},{2,3},{3,11},{4,5},{5,13},{6,7},{7,15},{8,0},{9,17},{1... | collective-permute-start | bytes 2359304 | tf_op jit(solution)/shard_map/ppermute | solution.py:318
  197.6 22.2 %collective-permute-start.29 = (bf16[6,2,1,64,512]{4,3,2,1,0:T(8,128)(2,1)}, bf16[6,2,1,64,512]{4,3,2,1,0:T(8,128)(2,1)S(1)}, u32[]{:S(2)}, u32[]{:S(2)}) collective-permute-start(bf16[6,2,1,64,512]{4,3,2,1,0:T(8,128)(2,1)} %get-tuple-element.131), channel_id=1, source_target_pairs={{0,4},{1,5},{2,6},{3,7},{4,0},{5,1},{6,2},{7,3},{8,12},{9,13},{10,... | collective-permute-start | bytes 2359304 | tf_op jit(solution)/shard_map/ppermute | solution.py:318
  215.9 17.8 %collective-permute-start.32 = (bf16[6,2,1,64,512]{4,3,2,1,0:T(8,128)(2,1)}, bf16[6,2,1,64,512]{4,3,2,1,0:T(8,128)(2,1)S(1)}, u32[]{:S(2)}, u32[]{:S(2)}) collective-permute-start(bf16[6,2,1,64,512]{4,3,2,1,0:T(8,128)(2,1)} %get-tuple-element.134), channel_id=1, source_target_pairs={{0,4},{1,5},{2,6},{3,7},{4,0},{5,1},{6,2},{7,3},{8,12},{9,13},{10,... | collective-permute-start | bytes 2359304 | tf_op jit(solution)/shard_map/ppermute | solution.py:318
  216.9 21.2 %collective-permute-start.34 = (bf16[6,2,1,64,512]{4,3,2,1,0:T(8,128)(2,1)}, bf16[6,2,1,64,512]{4,3,2,1,0:T(8,128)(2,1)S(1)}, u32[]{:S(2)}, u32[]{:S(2)}) collective-permute-start(bf16[6,2,1,64,512]{4,3,2,1,0:T(8,128)(2,1)} %get-tuple-element.136.refs_4_), channel_id=1, source_target_pairs={{0,8},{1,0},{2,10},{3,2},{4,12},{5,4},{6,14},{7,6},{8,16},{9,1},{1... | collective-permute-start | bytes 2359304 | tf_op jit(solution)/shard_map/ppermute | solution.py:318
  219.8 20.7 %collective-permute-start.35 = (bf16[6,2,1,64,512]{4,3,2,1,0:T(8,128)(2,1)}, bf16[6,2,1,64,512]{4,3,2,1,0:T(8,128)(2,1)S(1)}, u32[]{:S(2)}, u32[]{:S(2)}) collective-permute-start(bf16[6,2,1,64,512]{4,3,2,1,0:T(8,128)(2,1)} %get-tuple-element.137.refs_5_), channel_id=1, source_target_pairs={{0,1},{1,9},{2,3},{3,11},{4,5},{5,13},{6,7},{7,15},{8,0},{9,17},{1... | collective-permute-start | bytes 2359304 | tf_op jit(solution)/shard_map/ppermute | solution.py:318
  223.3 28.5 %collective-permute-start.30 = (bf16[6,2,1,64,512]{4,3,2,1,0:T(8,128)(2,1)}, bf16[6,2,1,64,512]{4,3,2,1,0:T(8,128)(2,1)S(1)}, u32[]{:S(2)}, u32[]{:S(2)}) collective-permute-start(bf16[6,2,1,64,512]{4,3,2,1,0:T(8,128)(2,1)} %get-tuple-element.132.refs_4_.refs_2_), channel_id=1, source_target_pairs={{0,8},{1,0},{2,10},{3,2},{4,12},{5,4},{6,14},{7,6},{8,16},{9,1},{1... | collective-permute-start | bytes 2359304 | tf_op jit(solution)/shard_map/ppermute | solution.py:318
  225.9 26.0 %collective-permute-start.31 = (bf16[6,2,1,64,512]{4,3,2,1,0:T(8,128)(2,1)}, bf16[6,2,1,64,512]{4,3,2,1,0:T(8,128)(2,1)S(1)}, u32[]{:S(2)}, u32[]{:S(2)}) collective-permute-start(bf16[6,2,1,64,512]{4,3,2,1,0:T(8,128)(2,1)} %get-tuple-element.133.refs_5_.refs_3_), channel_id=1, source_target_pairs={{0,1},{1,9},{2,3},{3,11},{4,5},{5,13},{6,7},{7,15},{8,0},{9,17},{1... | collective-permute-start | bytes 2359304 | tf_op jit(solution)/shard_map/ppermute | solution.py:318
  233.7 6.8 %copy-start.9 = (bf16[6,2,1,64,512]{4,3,2,1,0:T(8,128)(2,1)}, bf16[6,2,1,64,512]{4,3,2,1,0:T(8,128)(2,1)S(1)}, u32[]{:S(2)}) copy-start(bf16[6,2,1,64,512]{4,3,2,1,0:T(8,128)(2,1)S(1)} %collective-permute-done.32.refs_9_.refs_14_.refs_10_) | copy-start | bytes 2359300
  233.7 20.7 %collective-permute-start.33 = (bf16[6,2,1,64,512]{4,3,2,1,0:T(8,128)(2,1)}, bf16[6,2,1,64,512]{4,3,2,1,0:T(8,128)(2,1)S(1)}, u32[]{:S(2)}, u32[]{:S(2)}) collective-permute-start(bf16[6,2,1,64,512]{4,3,2,1,0:T(8,128)(2,1)} %get-tuple-element.135), channel_id=1, source_target_pairs={{0,4},{1,5},{2,6},{3,7},{4,0},{5,1},{6,2},{7,3},{8,12},{9,13},{10,... | collective-permute-start | bytes 2359304 | tf_op jit(solution)/shard_map/ppermute | solution.py:318
  238.1 2.4 copy-start.21
  243.5 27.8 %collective-permute-start.36 = (bf16[6,2,1,64,512]{4,3,2,1,0:T(8,128)(2,1)}, bf16[6,2,1,64,512]{4,3,2,1,0:T(8,128)(2,1)S(1)}, u32[]{:S(2)}, u32[]{:S(2)}) collective-permute-start(bf16[6,2,1,64,512]{4,3,2,1,0:T(8,128)(2,1)} %get-tuple-element.139), channel_id=1, source_target_pairs={{0,4},{1,5},{2,6},{3,7},{4,0},{5,1},{6,2},{7,3},{8,12},{9,13},{10,... | collective-permute-start | bytes 2359304 | tf_op jit(solution)/shard_map/ppermute | solution.py:318
  251.8 2.6 copy-start.23
  251.8 2.6 copy-start.24
  257.3 28.2 %collective-permute-start.37 = (bf16[5,2,1,64,512]{4,3,2,1,0:T(8,128)(2,1)}, bf16[5,2,1,64,512]{4,3,2,1,0:T(8,128)(2,1)S(1)}, u32[]{:S(2)}, u32[]{:S(2)}) collective-permute-start(bf16[5,2,1,64,512]{4,3,2,1,0:T(8,128)(2,1)} %get-tuple-element.141), channel_id=1, source_target_pairs={{0,4},{1,5},{2,6},{3,7},{4,0},{5,1},{6,2},{7,3},{8,12},{9,13},{10,... | collective-permute-start | bytes 1966088 | tf_op jit(solution)/shard_map/ppermute | solution.py:318
  (30 other events, 34.6 us)

commit v3 on v2

--- a/solution.py
+++ b/solution.py
@@ -150,9 +150,11 @@
         arrays[n] = value
 
 
-def gather_kernel(plan, lanes, start, own, token, a, b, token_out, sems):
+def gather_kernel(plan, lanes, start, named, own, *refs):
     senders, rows = own.shape[0], own.shape[4]
-    targets = {"a": a, "b": b}
+    sems = refs[-1]
+    targets = dict(zip(named, refs[-2 - len(named) : -2]))
+    samples = targets[named[0]].shape[-1]
     me = my_kind(lanes)
     for kind, todo in plan.items():
 
@@ -163,7 +165,7 @@
                 at = pl.ds(lane * rows, rows)
                 for i, (target, dst, src, length) in enumerate(todo):
                     copy = pltpu.make_async_copy(
-                        own.at[lane, pl.ds(src, length), :, :, :, pl.ds(start, a.shape[-1])],
+                        own.at[lane, pl.ds(src, length), :, :, :, pl.ds(start, samples)],
                         targets[target].at[pl.ds(dst, length), :, :, at],
                         sems.at[lane, i],
                     )
@@ -173,71 +175,77 @@
                 copy.wait()
 
 
-def run_gather(arrays, part, own, start, samples, plan, lanes):
+def run_gather(arrays, own, start, samples, plan, outs, lanes):
     senders, _, two, split, rows, _ = own.shape
     shape = (two, split, senders * rows, samples)
-    token = arrays["token"]
     any_spec = pl.BlockSpec(memory_space=pl.ANY)
-    vmem_spec = pl.BlockSpec(memory_space=pltpu.VMEM)
+    tokens = [arrays["token"]] if "token" in arrays else []
     most = max(len(todo) for todo in plan.values())
-    arrays["a0.%d" % part], arrays["b0.%d" % part], arrays["token"] = pl.pallas_call(
-        functools.partial(gather_kernel, plan, lanes, start),
-        out_shape=[jax.ShapeDtypeStruct((n,) + shape, own.dtype) for n in (len(UP), len(DOWN))]
-        + [jax.ShapeDtypeStruct(token.shape, token.dtype)],
-        in_specs=[any_spec] * 2,
-        out_specs=[vmem_spec] * 2 + [any_spec],
+    got = pl.pallas_call(
+        functools.partial(gather_kernel, plan, lanes, start, list(outs)),
+        out_shape=[jax.ShapeDtypeStruct((n,) + shape, own.dtype) for n in outs.values()]
+        + [jax.ShapeDtypeStruct((8, 128), jnp.int32)],
+        in_specs=[any_spec] * (1 + len(tokens)),
+        out_specs=[pl.BlockSpec(memory_space=pltpu.VMEM)] * len(outs) + [any_spec],
         scratch_shapes=[pltpu.SemaphoreType.DMA((senders, most))],
-        input_output_aliases={1: 2},
+        input_output_aliases={1: len(outs)} if tokens else {},
         compiler_params=pltpu.CompilerParams(vmem_limit_bytes=VMEM_BYTES),
         cost_estimate=pl.CostEstimate(flops=0, bytes_accessed=0, transcendentals=0),
         name="gather",
-    )(own, token)
+    )(own, *tokens)
+    for name, value in zip(list(outs) + ["token"], got):
+        arrays[name] = value
 
 
 def tiles_kernel(names, plan, lanes, scale, first, last, *refs):
     ins = dict(zip(names, refs[: len(names)]))
-    refs = refs[len(names) :]
-    flag = acc = None
-    if last:
-        flag, refs = refs[0], refs[1:]
+    refs = list(refs[len(names) :])
+    flag = refs.pop(0) if last else None
+    acc = None if first else refs.pop(0)
+    _, out, _, held, sums, sems, in_sems, out_sems = refs
+    me = my_kind(lanes)
+    tiles = held.shape[0]
+    for kind, todo in plan.items():
+
+        @pl.when(me == kind)
+        def _(todo=todo):
+            for slot, row, name, src in todo:
+                pltpu.make_async_copy(ins[name].at[src], held.at[slot, :, :, row], sems.at[slot, row]).start()
+
     if not first:
-        acc, refs = refs[0], refs[1:]
-    _, out, _, held, sems = refs
-    me = my_kind(lanes)
-    s = pl.program_id(0)
-
-    @pl.when(s == 0)
-    def _():
-        for kind, todo in plan.items():
-
-            @pl.when(me == kind)
-            def _(todo=todo):
-                for slot, row, name, src in todo:
-                    pltpu.make_async_copy(ins[name].at[src], held.at[slot, :, :, row], sems.at[slot, row]).start()
-
-    for row in range(NB):
-        pltpu.make_async_copy(held.at[s, :, :, row], held.at[s, :, :, row], sems.at[s, row]).wait()
+        for s in range(tiles):
+            pltpu.make_async_copy(acc.at[s], sums.at[s], in_sems.at[s]).start()
     rows = held.shape[2] * held.shape[3] * held.shape[4]
     samples = held.shape[5]
 
     def mul(a, b):
         return lax.dot_general(a, b, (((1,), (1,)), ((), ())), preferred_element_type=jnp.float32)
 
-    ar = held[s, 0].reshape(rows, samples)
-    ai = held[s, 1].reshape(rows, samples)
-    br = held[0, 0].reshape(rows, samples)
-    bi = held[0, 1].reshape(rows, samples)
-    real = (mul(ar, br) + mul(ai, bi)) * scale
-    imag = (mul(ar, bi) - mul(ai, br)) * scale
-    if not first:
-        real = real + acc[0, :, :rows]
-        imag = imag + acc[0, :, rows:]
-    if last:
-        keep = jnp.logical_or(s < HALF, flag[0] == 1)
-        real = jnp.where(keep, real, 0.0)
-        imag = jnp.where(keep, imag, 0.0)
-    out[0, :, :rows] = real
-    out[0, :, rows:] = imag
+    @pl.loop(0, tiles)
+    def _(s):
+        for row in range(NB):
+            pltpu.make_async_copy(held.at[s, :, :, row], held.at[s, :, :, row], sems.at[s, row]).wait()
+        if not first:
+            pltpu.make_async_copy(acc.at[s], sums.at[s], in_sems.at[s]).wait()
+        ar = held[s, 0].reshape(rows, samples)
+        ai = held[s, 1].reshape(rows, samples)
+        br = held[0, 0].reshape(rows, samples)
+        bi = held[0, 1].reshape(rows, samples)
+        real = (mul(ar, br) + mul(ai, bi)) * scale
+        imag = (mul(ar, bi) - mul(ai, br)) * scale
+        if not first:
+            real = real + sums[s, :, :rows]
+            imag = imag + sums[s, :, rows:]
+        if last:
+            keep = jnp.logical_or(s < tiles - 1, flag[0] == 1)
+            real = jnp.where(keep, real, 0.0)
+            imag = jnp.where(keep, imag, 0.0)
+        sums[s, :, :rows] = real
+        sums[s, :, rows:] = imag
+        pltpu.make_async_copy(sums.at[s], out.at[s], out_sems.at[s]).start()
+
+    for s in range(tiles):
+        pltpu.make_async_copy(sums.at[s], out.at[s], out_sems.at[s]).wait()
 
 
 def run_tiles(arrays, names, plan, lanes, scale, acc, flag):
@@ -245,8 +253,8 @@
     shape = arrays[names[0]].shape[1:]
     rows = shape[1] * shape[2] * NB
     samples = shape[3]
+    tiles = HALF + 1
     any_spec = pl.BlockSpec(memory_space=pl.ANY)
-    tile_spec = pl.BlockSpec((1, rows, 2 * rows), lambda s: (s, 0, 0))
     operands = [arrays[n] for n in names]
     in_specs = [any_spec] * len(names)
     aliases = {}
@@ -256,21 +264,25 @@
     if acc is not None:
         aliases = {len(operands): 0}
         operands.append(acc)
-        in_specs.append(tile_spec)
+        in_specs.append(any_spec)
     aliases[len(operands)] = 1
     operands.append(token)
     in_specs.append(any_spec)
-    held = (HALF + 1, 2, shape[1], NB, shape[2], samples)
     result, arrays["token"] = pl.pallas_call(
         functools.partial(tiles_kernel, names, plan, lanes, scale, acc is None, flag is not None),
-        grid=(HALF + 1,),
         out_shape=[
-            jax.ShapeDtypeStruct((HALF + 1, rows, 2 * rows), jnp.float32),
+            jax.ShapeDtypeStruct((tiles, rows, 2 * rows), jnp.float32),
             jax.ShapeDtypeStruct(token.shape, token.dtype),
         ],
         in_specs=in_specs,
-        out_specs=[tile_spec, any_spec],
-        scratch_shapes=[pltpu.VMEM(held, jnp.bfloat16), pltpu.SemaphoreType.DMA((HALF + 1, NB))],
+        out_specs=[any_spec, any_spec],
+        scratch_shapes=[
+            pltpu.VMEM((tiles, 2, shape[1], NB, shape[2], samples), jnp.bfloat16),
+            pltpu.VMEM((tiles, rows, 2 * rows), jnp.float32),
+            pltpu.SemaphoreType.DMA((tiles, NB)),
+            pltpu.SemaphoreType.DMA((tiles,)),
+            pltpu.SemaphoreType.DMA((tiles,)),
+        ],
         input_output_aliases=aliases,
         compiler_params=pltpu.CompilerParams(vmem_limit_bytes=VMEM_BYTES),
         cost_estimate=pl.CostEstimate(flops=0, bytes_accessed=0, transcendentals=0),
@@ -303,7 +315,7 @@
         self.owns, self.lanes = owns, lanes
         self.positions = lax.axis_size("tile")
         self.plan = Plan()
-        self.arrays = {"token": jnp.zeros((8, 128), jnp.int32)}
+        self.arrays = {}
         for part in range(len(owns)):
             self.plan.own("blocks.%d" % part, part, lambda parity: range(NB))
             self.plan.own("a0.%d" % part, part, lambda parity: DOWN if parity else UP)
@@ -317,16 +329,29 @@
         pairs = device_pairs(lambda kind: step(kind)[0], self.positions, self.lanes)
         self.arrays[target] = lax.ppermute(self.arrays[source], "tile", pairs)
 
-    def gather(self, part):
-        todo = {}
+    def gather(self, part, side=None):
+        todo, outs = {}, {"a0.%d" % part: len(UP), "b0.%d" % part: len(DOWN)}
+        if side is not None:
+            outs["side" + side] = HALF + 1
         for kind in KINDS:
             todo[kind] = []
-            for name in "ab":
-                blocks = [item[3] for item in self.plan.held["%s0.%d" % (name, part)][kind]]
+            for name in ("a0.%d" % part, "b0.%d" % part):
+                blocks = [item[3] for item in self.plan.held[name][kind]]
                 for d, _, src, length in runs([(i, "", b) for i, b in enumerate(blocks)]):
                     todo[kind].append((name, d, src, length))
-        run_gather(self.arrays, part, *self.owns[part], todo, self.lanes)
+            if side is not None:
+                items = [item for item, _ in self.choose(kind, HALF + 1, [part], ["blocks.%d" % part])]
+                self.plan.held.setdefault("side" + side, []).append(items)
+                for d, _, src, length in runs([(i, "", item[3]) for i, item in enumerate(items)]):
+                    todo[kind].append(("side" + side, d, src, length))
+        run_gather(self.arrays, *self.owns[part], todo, outs, self.lanes)
         self.here += ["a0.%d" % part, "b0.%d" % part]
+        if side is not None:
+            self.across(side)
+
+    def across(self, name):
+        self.move("side" + name, "got" + name, lambda kind: (kind ^ 2, True))
+        self.crossed.append("got" + name)
 
     def along(self, part, stage):
         for name in "ab":
@@ -337,21 +362,21 @@
         self.here += names
         return names
 
-    def choose(self, kind, most, parts):
+    def choose(self, kind, most, parts, names):
         wanted = []
         y = place(kind)[1]
         for part in parts:
             for source in range(DEPTH):
                 for b in needed(kind // 2 ^ 1):
                     item = (part, source, y, b)
-                    where = self.plan.find(kind, item, self.here)
+                    where = self.plan.find(kind, item, names)
                     if item not in self.sent[kind] and where and len(wanted) < most:
                         wanted.append((item, where))
         wanted.sort(key=lambda w: w[1])
         self.sent[kind].update(w[0] for w in wanted)
         return wanted
 
-    def prepare(self, part=None, stage=None, side=None, after=(), parts=None):
+    def prepare(self, part=None, stage=None, side=None, after=()):
         todo = {kind: [] for kind in KINDS}
         patched, outs = [], {}
         if part is not None:
@@ -369,7 +394,7 @@
                         self.plan.held[target][kind][dst : dst + len(items)] = items
         if side is not None:
             name, most = side
-            chosen = [self.choose(kind, most, range(len(self.owns)) if parts is None else parts) for kind in KINDS]
+            chosen = [self.choose(kind, most, range(len(self.owns)), self.here) for kind in KINDS]
             slots = max(len(c) for c in chosen)
             outs = {"side" + name: slots}
             for kind in KINDS:
@@ -383,8 +408,7 @@
         after = [n for n in after if n not in names]
         run_copies(self.arrays, names, after, todo, patched, outs, self.lanes)
         if side is not None:
-            self.move("side" + name, "got" + name, lambda kind: (kind ^ 2, True))
-            self.crossed.append("got" + name)
+            self.across(name)
 
     def tiles(self, part, scale, result, flag):
         names = [n for n in self.here if n.endswith(".%d" % part)] + self.crossed
@@ -422,14 +446,15 @@
     known = 0
     for n, (part, stage) in enumerate(STEPS):
         for fresh in GATHERS.get(n, ()):
-            turn.gather(fresh)
+            turn.gather(fresh, "0" if n == 0 else None)
         done = []
         while known < n and (known <= n - 2 or STEPS[known][0] == part):
             done += turn.arrived(STEPS[known][0], STEPS[known][1] + 1)
             known += 1
         if n >= 1:
             done = done + ["got%d" % max(n - 2, 0)]
-        turn.prepare(part, stage, side=(str(n), SIDE), after=done)
+        if n >= 1:
+            turn.prepare(part, stage, side=(str(n), SIDE), after=done)
         turn.along(part, stage)
         for ready in TILES.get(n, ()):
             result = turn.tiles(ready, scale, result, None)

time: 302 us -> 295 us (0.977)
  Pallas kernels: 93.5 us -> 86.9 us
    pallas_call x4, Pallas kernels: 50.3 us -> 44.8 us  [run_tiles(): pl.pallas_call(functools.partial(tiles_kernel, names, plan, lanes, scale,...]
    ppermute x38, waiting for transfers between devices: 113 us -> 109 us  [move(): self.arrays[target] = lax.ppermute(self.arrays[source], 'tile', pairs)]
    pallas_call x14 -> x13, Pallas kernels: 32.2 us -> 30.3 us  [run_copies(): pl.pallas_call(functools.partial(copies_kernel, names, len(after), plan,...]
  transfers between devices with their start and end apart: 40 -> 40, of which waited for: 20 -> 21; matrix products, arithmetic and copies ran while one was open for 2% -> 2% of each run, Pallas kernels for 26% -> 26%
where the time goes in v3:
time: 295 us; the launch traced here: 292 us
  waiting for transfers between devices  125 us (42%)
  Pallas kernels  86.9 us (29%)
  starting transfers between devices  54.3 us (18%)
  local copies, waits for them, and re-layouts  20.5 us (7%)
  other arithmetic  4.79 us (2%)
    ppermute x38, waiting for transfers between devices, move(): self.arrays[target] = lax.ppermute(self.arrays[source], 'tile', pairs)  109 us
    ppermute x38, starting transfers between devices, move(): self.arrays[target] = lax.ppermute(self.arrays[source], 'tile', pairs)  46.4 us
    pallas_call x4, Pallas kernels, run_tiles(): pl.pallas_call(functools.partial(tiles_kernel, names, plan, lanes, scale,...  44.8 us
    pallas_call x13, Pallas kernels, run_copies(): pl.pallas_call(functools.partial(copies_kernel, names, len(after), plan,...  30.3 us
    all_to_all x2, waiting for transfers between devices, exchange(): x = lax.all_to_all(x, 'tile', 0, 0, axis_index_groups=groups, tiled=True)  16 us
    unnamed x74, local copies, waits for them, and re-layouts  15.7 us
    pallas_call x4, Pallas kernels, run_gather(): pl.pallas_call(functools.partial(gather_kernel, plan, lanes, start, list(...  11.8 us
    all_to_all x2, starting transfers between devices, exchange(): x = lax.all_to_all(x, 'tile', 0, 0, axis_index_groups=groups, tiled=True)  7.93 us
  transfers between devices with their start and end apart: 40, of which 21 were waited for; matrix products, arithmetic and copies ran while one was open for 2% of the time, Pallas kernels for 26%

profile of v3, /device:TPU:0, one launch (start us, length us, event | category | flops | bytes accessed | tf_op | source)
XLA Modules:
  0.0 292.3 jit_solution(5239544660033775294)
XLA Ops:
  4.0 4.2 %all-to-all-start.1 = ((bf16[4,8,2,1,16,512]{5,4,3,2,1,0:T(8,128)(2,1)}), bf16[4,8,2,1,16,512]{5,4,3,2,1,0:T(8,128)(2,1)}, u32[]{:S(2)}, u32[]{:S(2)}) async-start(bf16[4,8,2,1,16,512]{5,4,3,2,1,0:T(8,128)(2,1)} %fusion.1), calls=%async_computation.1 | async-start | bytes 2097152 | tf_op jit(solution)/shard_map/all_to_all | solution.py:306
  10.7 2.6 fusion
  13.3 10.1 %all-to-all-done.1.own = bf16[4,8,2,1,16,512]{5,4,3,2,1,0:T(8,128)(2,1)} async-done(((bf16[4,8,2,1,16,512]{5,4,3,2,1,0:T(8,128)(2,1)}), bf16[4,8,2,1,16,512]{5,4,3,2,1,0:T(8,128)(2,1)}, u32[]{:S(2)}, u32[]{:S(2)}) %all-to-all-start.1) | async-done | bytes 1048608 | tf_op jit(solution)/shard_map/all_to_all | solution.py:306
  23.4 3.7 %all-to-all-start = ((bf16[4,8,2,1,16,1536]{5,4,3,2,1,0:T(8,128)(2,1)}), bf16[4,8,2,1,16,1536]{5,4,3,2,1,0:T(8,128)(2,1)S(1)}, u32[]{:S(2)}, u32[]{:S(2)}) async-start(bf16[4,8,2,1,16,1536]{5,4,3,2,1,0:T(8,128)(2,1)} %fusion), calls=%async_computation | async-start | bytes 6291456 | tf_op jit(solution)/shard_map/all_to_all | solution.py:306
  27.1 3.5 %gather.4 = (bf16[6,2,1,64,512]{4,3,2,1,0:T(8,128)(2,1)}, bf16[6,2,1,64,512]{4,3,2,1,0:T(8,128)(2,1)}, bf16[5,2,1,64,512]{4,3,2,1,0:T(8,128)(2,1)}, s32[8,128]{1,0:T(8,128)}) custom-call(bf16[4,8,2,1,16,512]{5,4,3,2,1,0:T(8,128)(2,1)} %all-to-all-done.1.own), custom_call_target="tpu_custom_call" | custom-call | tf_op jit(solution)/shard_map/gather/pallas_call | solution.py:184
  30.6 2.4 collective-permute-start
  34.5 15.5 %collective-permute-done.2.refs_5_.refs_8_ = bf16[5,2,1,64,512]{4,3,2,1,0:T(8,128)(2,1)S(1)} collective-permute-done((bf16[5,2,1,64,512]{4,3,2,1,0:T(8,128)(2,1)}, bf16[5,2,1,64,512]{4,3,2,1,0:T(8,128)(2,1)S(1)}, u32[]{:S(2)}, u32[]{:S(2)}) %collective-permute-start.2) | collective-permute-done | bytes 655392 | tf_op jit(solution)/shard_map/ppermute | solution.py:330
  52.1 2.8 pick.13
  58.1 5.9 %all-to-all-done.own = bf16[4,8,2,1,16,1536]{5,4,3,2,1,0:T(8,128)(2,1)S(1)} async-done(((bf16[4,8,2,1,16,1536]{5,4,3,2,1,0:T(8,128)(2,1)}), bf16[4,8,2,1,16,1536]{5,4,3,2,1,0:T(8,128)(2,1)S(1)}, u32[]{:S(2)}, u32[]{:S(2)}) %all-to-all-start) | async-done | bytes 3145760 | tf_op jit(solution)/shard_map/all_to_all | solution.py:306
  65.7 2.7 gather.5
  68.4 2.0 pick.14
  70.4 2.5 collective-permute-start.3
  73.0 2.3 collective-permute-start.8
  75.3 2.8 gather.6
  78.1 2.2 pick.15
  80.4 10.7 %collective-permute-done.3.refs_4_ = bf16[6,2,1,64,512]{4,3,2,1,0:T(8,128)(2,1)S(1)} collective-permute-done((bf16[6,2,1,64,512]{4,3,2,1,0:T(8,128)(2,1)}, bf16[6,2,1,64,512]{4,3,2,1,0:T(8,128)(2,1)S(1)}, u32[]{:S(2)}, u32[]{:S(2)}) %collective-permute-start.3) | collective-permute-done | bytes 786464 | tf_op jit(solution)/shard_map/ppermute | solution.py:330
  91.1 2.4 collective-permute-start.9
  93.5 2.8 gather.7
  97.4 2.9 pick.16
  101.1 6.2 %collective-permute-done.10.refs_5_.refs_7_ = bf16[6,2,1,64,512]{4,3,2,1,0:T(8,128)(2,1)S(1)} collective-permute-done((bf16[6,2,1,64,512]{4,3,2,1,0:T(8,128)(2,1)}, bf16[6,2,1,64,512]{4,3,2,1,0:T(8,128)(2,1)S(1)}, u32[]{:S(2)}, u32[]{:S(2)}) %collective-permute-start.10) | collective-permute-done | bytes 786464 | tf_op jit(solution)/shard_map/ppermute | solution.py:330
  112.7 2.1 pick.17
  114.9 2.4 collective-permute-start.12
  117.3 11.4 %collective-permute-done.14.refs_4_ = bf16[6,2,1,64,512]{4,3,2,1,0:T(8,128)(2,1)S(1)} collective-permute-done((bf16[6,2,1,64,512]{4,3,2,1,0:T(8,128)(2,1)}, bf16[6,2,1,64,512]{4,3,2,1,0:T(8,128)(2,1)S(1)}, u32[]{:S(2)}, u32[]{:S(2)}) %collective-permute-start.14) | collective-permute-done | bytes 786464 | tf_op jit(solution)/shard_map/ppermute | solution.py:330
  131.4 2.1 pick.18
  133.5 3.1 %collective-permute-start.20 = (bf16[6,2,1,64,512]{4,3,2,1,0:T(8,128)(2,1)}, bf16[6,2,1,64,512]{4,3,2,1,0:T(8,128)(2,1)S(1)}, u32[]{:S(2)}, u32[]{:S(2)}) collective-permute-start(bf16[6,2,1,64,512]{4,3,2,1,0:T(8,128)(2,1)} %get-tuple-element.109.refs_4_), channel_id=1, source_target_pairs={{0,8},{1,0},{2,10},{3,2},{4,12},{5,4},{6,14},{7,6},{8,16},{9,1},{1... | collective-permute-start | bytes 2359304 | tf_op jit(solution)/shard_map/ppermute | solution.py:330
  136.7 8.9 %collective-permute-done.12.refs_4_ = bf16[6,2,1,64,512]{4,3,2,1,0:T(8,128)(2,1)S(1)} collective-permute-done((bf16[6,2,1,64,512]{4,3,2,1,0:T(8,128)(2,1)}, bf16[6,2,1,64,512]{4,3,2,1,0:T(8,128)(2,1)S(1)}, u32[]{:S(2)}, u32[]{:S(2)}) %collective-permute-start.12) | collective-permute-done | bytes 786464 | tf_op jit(solution)/shard_map/ppermute | solution.py:330
  148.3 2.1 pick.19
  150.4 2.4 collective-permute-start.18
  152.8 9.6 %collective-permute-done.20.refs_6_ = bf16[6,2,1,64,512]{4,3,2,1,0:T(8,128)(2,1)S(1)} collective-permute-done((bf16[6,2,1,64,512]{4,3,2,1,0:T(8,128)(2,1)}, bf16[6,2,1,64,512]{4,3,2,1,0:T(8,128)(2,1)S(1)}, u32[]{:S(2)}, u32[]{:S(2)}) %collective-permute-start.20) | collective-permute-done | bytes 786464 | tf_op jit(solution)/shard_map/ppermute | solution.py:330
  163.9 9.5 %tiles.4 = (f32[5,512,1024]{2,1,0:T(8,128)}, s32[8,128]{1,0:T(8,128)}) custom-call(bf16[6,2,1,64,512]{4,3,2,1,0:T(8,128)(2,1)} %get-tuple-element.73.refs_0_, bf16[6,2,1,64,512]{4,3,2,1,0:T(8,128)(2,1)} %get-tuple-element.74.refs_1_, bf16[6,2,1,64,512]{4,3,2,1,0:T(8,128)(2,1)} %get-tuple-element.77.refs_0_.refs_2_, ...), custom_call_target="tpu_custom_call", output_to_operand_aliasing={{1}: (13, {})} | custom-call | tf_op jit(solution)/shard_map/tiles/pallas_call | solution.py:271
  174.7 2.9 pick.20
  181.3 2.8 pick.21
  186.0 9.2 %collective-permute-done.28.refs_12_.refs_9_.refs_13_.refs_8_ = bf16[6,2,1,64,512]{4,3,2,1,0:T(8,128)(2,1)S(1)} collective-permute-done((bf16[6,2,1,64,512]{4,3,2,1,0:T(8,128)(2,1)}, bf16[6,2,1,64,512]{4,3,2,1,0:T(8,128)(2,1)S(1)}, u32[]{:S(2)}, u32[]{:S(2)}) %collective-permute-start.28) | collective-permute-done | bytes 786464 | tf_op jit(solution)/shard_map/ppermute | solution.py:330
  197.0 11.6 %tiles.5 = (f32[5,512,1024]{2,1,0:T(8,128)}, s32[8,128]{1,0:T(8,128)}) custom-call(bf16[6,2,1,64,512]{4,3,2,1,0:T(8,128)(2,1)} %get-tuple-element.86.refs_0_, bf16[6,2,1,64,512]{4,3,2,1,0:T(8,128)(2,1)} %get-tuple-element.87.refs_1_, bf16[6,2,1,64,512]{4,3,2,1,0:T(8,128)(2,1)} %get-tuple-element.93.refs_2_, ...), custom_call_target="tpu_custom_call", output_to_operand_aliasing={{0}: (13, {}), {1}: (14, {})} | custom-call | tf_op jit(solution)/shard_map/tiles/pallas_call | solution.py:271
  209.7 2.1 pick.22
  212.8 3.0 %collective-permute-start.34 = (bf16[6,2,1,64,512]{4,3,2,1,0:T(8,128)(2,1)}, bf16[6,2,1,64,512]{4,3,2,1,0:T(8,128)(2,1)S(1)}, u32[]{:S(2)}, u32[]{:S(2)}) collective-permute-start(bf16[6,2,1,64,512]{4,3,2,1,0:T(8,128)(2,1)} %get-tuple-element.130.refs_4_), channel_id=1, source_target_pairs={{0,8},{1,0},{2,10},{3,2},{4,12},{5,4},{6,14},{7,6},{8,16},{9,1},{1... | collective-permute-start | bytes 2359304 | tf_op jit(solution)/shard_map/ppermute | solution.py:330
  217.2 2.1 pick.23
  219.3 2.5 collective-permute-start.30
  221.8 7.3 %collective-permute-done.32.refs_9_.refs_14_.refs_10_ = bf16[6,2,1,64,512]{4,3,2,1,0:T(8,128)(2,1)S(1)} collective-permute-done((bf16[6,2,1,64,512]{4,3,2,1,0:T(8,128)(2,1)}, bf16[6,2,1,64,512]{4,3,2,1,0:T(8,128)(2,1)S(1)}, u32[]{:S(2)}, u32[]{:S(2)}) %collective-permute-start.32) | collective-permute-done | bytes 786464 | tf_op jit(solution)/shard_map/ppermute | solution.py:330
  230.9 3.2 %collective-permute-done.34.refs_6_ = bf16[6,2,1,64,512]{4,3,2,1,0:T(8,128)(2,1)S(1)} collective-permute-done((bf16[6,2,1,64,512]{4,3,2,1,0:T(8,128)(2,1)}, bf16[6,2,1,64,512]{4,3,2,1,0:T(8,128)(2,1)S(1)}, u32[]{:S(2)}, u32[]{:S(2)}) %collective-permute-start.34) | collective-permute-done | bytes 786464 | tf_op jit(solution)/shard_map/ppermute | solution.py:330
  234.1 2.4 collective-permute-done.35.refs_7_
  237.3 2.1 pick.24
  240.7 7.0 %collective-permute-done.30.refs_4_.refs_6_ = bf16[6,2,1,64,512]{4,3,2,1,0:T(8,128)(2,1)S(1)} collective-permute-done((bf16[6,2,1,64,512]{4,3,2,1,0:T(8,128)(2,1)}, bf16[6,2,1,64,512]{4,3,2,1,0:T(8,128)(2,1)S(1)}, u32[]{:S(2)}, u32[]{:S(2)}) %collective-permute-start.30) | collective-permute-done | bytes 786464 | tf_op jit(solution)/shard_map/ppermute | solution.py:330
  247.7 2.1 collective-permute-done.33.refs_7_.refs_11_
  250.7 2.0 pick.25
  255.8 10.9 %collective-permute-done.36.refs_15_.refs_12_ = bf16[6,2,1,64,512]{4,3,2,1,0:T(8,128)(2,1)S(1)} collective-permute-done((bf16[6,2,1,64,512]{4,3,2,1,0:T(8,128)(2,1)}, bf16[6,2,1,64,512]{4,3,2,1,0:T(8,128)(2,1)S(1)}, u32[]{:S(2)}, u32[]{:S(2)}) %collective-permute-start.36) | collective-permute-done | bytes 786464 | tf_op jit(solution)/shard_map/ppermute | solution.py:330
  267.5 11.6 %tiles.6 = (f32[5,512,1024]{2,1,0:T(8,128)}, s32[8,128]{1,0:T(8,128)}) custom-call(bf16[6,2,1,64,512]{4,3,2,1,0:T(8,128)(2,1)} %get-tuple-element.99.refs_2_.refs_0_, bf16[6,2,1,64,512]{4,3,2,1,0:T(8,128)(2,1)} %get-tuple-element.100.refs_3_.refs_1_, ...), custom_call_target="tpu_custom_call", output_to_operand_aliasing={{0}: (16, {}), {1}: (17, {})} | custom-call | tf_op jit(solution)/shard_map/tiles/pallas_call | solution.py:271
  279.9 12.2 %tiles.7 = (f32[5,512,1024]{2,1,0:T(8,128)}, s32[8,128]{1,0:T(8,128)}) custom-call(bf16[6,2,1,64,512]{4,3,2,1,0:T(8,128)(2,1)} %get-tuple-element.107.refs_2_.refs_0_, bf16[6,2,1,64,512]{4,3,2,1,0:T(8,128)(2,1)} %get-tuple-element.108.refs_3_.refs_1_, ...), custom_call_target="tpu_custom_call", output_to_operand_aliasing={{0}: (15, {}), {1}: (16, {})} | custom-call | tf_op jit(solution)/shard_map/tiles/pallas_call | solution.py:271
  (145 shorter events, 50.9 us)
Async XLA Ops:
  0.0 2.4 slice-start
  4.0 19.4 %all-to-all-start.1 = ((bf16[4,8,2,1,16,512]{5,4,3,2,1,0:T(8,128)(2,1)}), bf16[4,8,2,1,16,512]{5,4,3,2,1,0:T(8,128)(2,1)}, u32[]{:S(2)}, u32[]{:S(2)}) async-start(bf16[4,8,2,1,16,512]{5,4,3,2,1,0:T(8,128)(2,1)} %fusion.1), calls=%async_computation.1 | async-start | bytes 2097152 | tf_op jit(solution)/shard_map/all_to_all | solution.py:306
  23.4 40.6 %all-to-all-start = ((bf16[4,8,2,1,16,1536]{5,4,3,2,1,0:T(8,128)(2,1)}), bf16[4,8,2,1,16,1536]{5,4,3,2,1,0:T(8,128)(2,1)S(1)}, u32[]{:S(2)}, u32[]{:S(2)}) async-start(bf16[4,8,2,1,16,1536]{5,4,3,2,1,0:T(8,128)(2,1)} %fusion), calls=%async_computation | async-start | bytes 6291456 | tf_op jit(solution)/shard_map/all_to_all | solution.py:306
  30.6 20.0 %collective-permute-start = (bf16[6,2,1,64,512]{4,3,2,1,0:T(8,128)(2,1)}, bf16[6,2,1,64,512]{4,3,2,1,0:T(8,128)(2,1)S(1)}, u32[]{:S(2)}, u32[]{:S(2)}) collective-permute-start(bf16[6,2,1,64,512]{4,3,2,1,0:T(8,128)(2,1)} %get-tuple-element.73.refs_0_), channel_id=1, source_target_pairs={{0,8},{1,0},{2,10},{3,2},{4,12},{5,4},{6,14},{7,6},{8,16},{9,1},{1... | collective-permute-start | bytes 2359304 | tf_op jit(solution)/shard_map/ppermute | solution.py:330
  33.0 18.2 %collective-permute-start.1 = (bf16[6,2,1,64,512]{4,3,2,1,0:T(8,128)(2,1)}, bf16[6,2,1,64,512]{4,3,2,1,0:T(8,128)(2,1)S(1)}, u32[]{:S(2)}, u32[]{:S(2)}) collective-permute-start(bf16[6,2,1,64,512]{4,3,2,1,0:T(8,128)(2,1)} %get-tuple-element.74.refs_1_), channel_id=1, source_target_pairs={{0,1},{1,9},{2,3},{3,11},{4,5},{5,13},{6,7},{7,15},{8,0},{9,17},{1... | collective-permute-start | bytes 2359304 | tf_op jit(solution)/shard_map/ppermute | solution.py:330
  33.0 17.0 %collective-permute-start.2 = (bf16[5,2,1,64,512]{4,3,2,1,0:T(8,128)(2,1)}, bf16[5,2,1,64,512]{4,3,2,1,0:T(8,128)(2,1)S(1)}, u32[]{:S(2)}, u32[]{:S(2)}) collective-permute-start(bf16[5,2,1,64,512]{4,3,2,1,0:T(8,128)(2,1)} %get-tuple-element.76), channel_id=1, source_target_pairs={{0,4},{1,5},{2,6},{3,7},{4,0},{5,1},{6,2},{7,3},{8,12},{9,13},{10,... | collective-permute-start | bytes 1966088 | tf_op jit(solution)/shard_map/ppermute | solution.py:330
  54.9 18.1 %collective-permute-start.5 = (bf16[6,2,1,64,512]{4,3,2,1,0:T(8,128)(2,1)}, bf16[6,2,1,64,512]{4,3,2,1,0:T(8,128)(2,1)}, u32[]{:S(2)}, u32[]{:S(2)}) collective-permute-start(bf16[6,2,1,64,512]{4,3,2,1,0:T(8,128)(2,1)} %get-tuple-element.77.refs_0_.refs_2_), channel_id=1, source_target_pairs={{0,8},{1,0},{2,10},{3,2},{4,12},{5,4},{6,14},{7,6},{8,16},{9,1},{1... | collective-permute-start | bytes 2359304 | tf_op jit(solution)/shard_map/ppermute | solution.py:330
  56.2 21.9 %collective-permute-start.6 = (bf16[6,2,1,64,512]{4,3,2,1,0:T(8,128)(2,1)}, bf16[6,2,1,64,512]{4,3,2,1,0:T(8,128)(2,1)}, u32[]{:S(2)}, u32[]{:S(2)}) collective-permute-start(bf16[6,2,1,64,512]{4,3,2,1,0:T(8,128)(2,1)} %get-tuple-element.78.refs_1_.refs_3_), channel_id=1, source_target_pairs={{0,1},{1,9},{2,3},{3,11},{4,5},{5,13},{6,7},{7,15},{8,0},{9,17},{1... | collective-permute-start | bytes 2359304 | tf_op jit(solution)/shard_map/ppermute | solution.py:330
  56.2 21.9 %collective-permute-start.7 = (bf16[6,2,1,64,512]{4,3,2,1,0:T(8,128)(2,1)}, bf16[6,2,1,64,512]{4,3,2,1,0:T(8,128)(2,1)}, u32[]{:S(2)}, u32[]{:S(2)}) collective-permute-start(bf16[6,2,1,64,512]{4,3,2,1,0:T(8,128)(2,1)} %get-tuple-element.89), channel_id=1, source_target_pairs={{0,4},{1,5},{2,6},{3,7},{4,0},{5,1},{6,2},{7,3},{8,12},{9,13},{10,... | collective-permute-start | bytes 2359304 | tf_op jit(solution)/shard_map/ppermute | solution.py:330
  70.4 20.7 %collective-permute-start.3 = (bf16[6,2,1,64,512]{4,3,2,1,0:T(8,128)(2,1)}, bf16[6,2,1,64,512]{4,3,2,1,0:T(8,128)(2,1)S(1)}, u32[]{:S(2)}, u32[]{:S(2)}) collective-permute-start(bf16[6,2,1,64,512]{4,3,2,1,0:T(8,128)(2,1)} %get-tuple-element.86.refs_0_), channel_id=1, source_target_pairs={{0,8},{1,0},{2,10},{3,2},{4,12},{5,4},{6,14},{7,6},{8,16},{9,1},{1... | collective-permute-start | bytes 2359304 | tf_op jit(solution)/shard_map/ppermute | solution.py:330
  72.9 23.4 %collective-permute-start.4 = (bf16[6,2,1,64,512]{4,3,2,1,0:T(8,128)(2,1)}, bf16[6,2,1,64,512]{4,3,2,1,0:T(8,128)(2,1)S(1)}, u32[]{:S(2)}, u32[]{:S(2)}) collective-permute-start(bf16[6,2,1,64,512]{4,3,2,1,0:T(8,128)(2,1)} %get-tuple-element.87.refs_1_), channel_id=1, source_target_pairs={{0,1},{1,9},{2,3},{3,11},{4,5},{5,13},{6,7},{7,15},{8,0},{9,17},{1... | collective-permute-start | bytes 2359304 | tf_op jit(solution)/shard_map/ppermute | solution.py:330
  73.0 23.3 %collective-permute-start.8 = (bf16[6,2,1,64,512]{4,3,2,1,0:T(8,128)(2,1)}, bf16[6,2,1,64,512]{4,3,2,1,0:T(8,128)(2,1)S(1)}, u32[]{:S(2)}, u32[]{:S(2)}) collective-permute-start(bf16[6,2,1,64,512]{4,3,2,1,0:T(8,128)(2,1)} %get-tuple-element.92), channel_id=1, source_target_pairs={{0,4},{1,5},{2,6},{3,7},{4,0},{5,1},{6,2},{7,3},{8,12},{9,13},{10,... | collective-permute-start | bytes 2359304 | tf_op jit(solution)/shard_map/ppermute | solution.py:330
  80.3 27.0 %collective-permute-start.10 = (bf16[6,2,1,64,512]{4,3,2,1,0:T(8,128)(2,1)}, bf16[6,2,1,64,512]{4,3,2,1,0:T(8,128)(2,1)S(1)}, u32[]{:S(2)}, u32[]{:S(2)}) collective-permute-start(bf16[6,2,1,64,512]{4,3,2,1,0:T(8,128)(2,1)} %get-tuple-element.96.refs_5_), channel_id=1, source_target_pairs={{0,1},{1,9},{2,3},{3,11},{4,5},{5,13},{6,7},{7,15},{8,0},{9,17},{1... | collective-permute-start | bytes 2359304 | tf_op jit(solution)/shard_map/ppermute | solution.py:330
  80.3 30.5 %collective-permute-start.11 = (bf16[6,2,1,64,512]{4,3,2,1,0:T(8,128)(2,1)}, bf16[6,2,1,64,512]{4,3,2,1,0:T(8,128)(2,1)S(1)}, u32[]{:S(2)}, u32[]{:S(2)}) collective-permute-start(bf16[6,2,1,64,512]{4,3,2,1,0:T(8,128)(2,1)} %get-tuple-element.98), channel_id=1, source_target_pairs={{0,4},{1,5},{2,6},{3,7},{4,0},{5,1},{6,2},{7,3},{8,12},{9,13},{10,... | collective-permute-start | bytes 2359304 | tf_op jit(solution)/shard_map/ppermute | solution.py:330
  91.1 5.2 %copy-start.14 = (bf16[6,2,1,64,512]{4,3,2,1,0:T(8,128)(2,1)}, bf16[6,2,1,64,512]{4,3,2,1,0:T(8,128)(2,1)S(1)}, u32[]{:S(2)}) copy-start(bf16[6,2,1,64,512]{4,3,2,1,0:T(8,128)(2,1)S(1)} %collective-permute-done.3.refs_4_) | copy-start | bytes 2359300
  91.1 20.7 %collective-permute-start.9 = (bf16[6,2,1,64,512]{4,3,2,1,0:T(8,128)(2,1)}, bf16[6,2,1,64,512]{4,3,2,1,0:T(8,128)(2,1)S(1)}, u32[]{:S(2)}, u32[]{:S(2)}) collective-permute-start(bf16[6,2,1,64,512]{4,3,2,1,0:T(8,128)(2,1)} %get-tuple-element.95.refs_4_), channel_id=1, source_target_pairs={{0,8},{1,0},{2,10},{3,2},{4,12},{5,4},{6,14},{7,6},{8,16},{9,1},{1... | collective-permute-start | bytes 2359304 | tf_op jit(solution)/shard_map/ppermute | solution.py:330
  100.3 28.4 %collective-permute-start.14 = (bf16[6,2,1,64,512]{4,3,2,1,0:T(8,128)(2,1)}, bf16[6,2,1,64,512]{4,3,2,1,0:T(8,128)(2,1)S(1)}, u32[]{:S(2)}, u32[]{:S(2)}) collective-permute-start(bf16[6,2,1,64,512]{4,3,2,1,0:T(8,128)(2,1)} %get-tuple-element.93.refs_2_), channel_id=1, source_target_pairs={{0,8},{1,0},{2,10},{3,2},{4,12},{5,4},{6,14},{7,6},{8,16},{9,1},{1... | collective-permute-start | bytes 2359304 | tf_op jit(solution)/shard_map/ppermute | solution.py:330
  101.1 29.1 %collective-permute-start.15 = (bf16[6,2,1,64,512]{4,3,2,1,0:T(8,128)(2,1)}, bf16[6,2,1,64,512]{4,3,2,1,0:T(8,128)(2,1)S(1)}, u32[]{:S(2)}, u32[]{:S(2)}) collective-permute-start(bf16[6,2,1,64,512]{4,3,2,1,0:T(8,128)(2,1)} %get-tuple-element.94.refs_3_), channel_id=1, source_target_pairs={{0,1},{1,9},{2,3},{3,11},{4,5},{5,13},{6,7},{7,15},{8,0},{9,17},{1... | collective-permute-start | bytes 2359304 | tf_op jit(solution)/shard_map/ppermute | solution.py:330
  107.3 4.5 %copy-start.33 = (bf16[6,2,1,64,512]{4,3,2,1,0:T(8,128)(2,1)}, bf16[6,2,1,64,512]{4,3,2,1,0:T(8,128)(2,1)S(1)}, u32[]{:S(2)}) copy-start(bf16[6,2,1,64,512]{4,3,2,1,0:T(8,128)(2,1)S(1)} %collective-permute-done.10.refs_5_.refs_7_) | copy-start | bytes 2359300
  107.3 23.0 %collective-permute-start.16 = (bf16[6,2,1,64,512]{4,3,2,1,0:T(8,128)(2,1)}, bf16[6,2,1,64,512]{4,3,2,1,0:T(8,128)(2,1)S(1)}, u32[]{:S(2)}, u32[]{:S(2)}) collective-permute-start(bf16[6,2,1,64,512]{4,3,2,1,0:T(8,128)(2,1)} %get-tuple-element.104), channel_id=1, source_target_pairs={{0,4},{1,5},{2,6},{3,7},{4,0},{5,1},{6,2},{7,3},{8,12},{9,13},{10,... | collective-permute-start | bytes 2359304 | tf_op jit(solution)/shard_map/ppermute | solution.py:330
  114.9 30.7 %collective-permute-start.12 = (bf16[6,2,1,64,512]{4,3,2,1,0:T(8,128)(2,1)}, bf16[6,2,1,64,512]{4,3,2,1,0:T(8,128)(2,1)S(1)}, u32[]{:S(2)}, u32[]{:S(2)}) collective-permute-start(bf16[6,2,1,64,512]{4,3,2,1,0:T(8,128)(2,1)} %get-tuple-element.99.refs_2_.refs_0_), channel_id=1, source_target_pairs={{0,8},{1,0},{2,10},{3,2},{4,12},{5,4},{6,14},{7,6},{8,16},{9,1},{1... | collective-permute-start | bytes 2359304 | tf_op jit(solution)/shard_map/ppermute | solution.py:330
  117.3 29.8 %collective-permute-start.13 = (bf16[6,2,1,64,512]{4,3,2,1,0:T(8,128)(2,1)}, bf16[6,2,1,64,512]{4,3,2,1,0:T(8,128)(2,1)S(1)}, u32[]{:S(2)}, u32[]{:S(2)}) collective-permute-start(bf16[6,2,1,64,512]{4,3,2,1,0:T(8,128)(2,1)} %get-tuple-element.100.refs_3_.refs_1_), channel_id=1, source_target_pairs={{0,1},{1,9},{2,3},{3,11},{4,5},{5,13},{6,7},{7,15},{8,0},{9,17},{1... | collective-permute-start | bytes 2359304 | tf_op jit(solution)/shard_map/ppermute | solution.py:330
  128.7 18.4 %collective-permute-start.17 = (bf16[6,2,1,64,512]{4,3,2,1,0:T(8,128)(2,1)}, bf16[6,2,1,64,512]{4,3,2,1,0:T(8,128)(2,1)S(1)}, u32[]{:S(2)}, u32[]{:S(2)}) collective-permute-start(bf16[6,2,1,64,512]{4,3,2,1,0:T(8,128)(2,1)} %get-tuple-element.106), channel_id=1, source_target_pairs={{0,4},{1,5},{2,6},{3,7},{4,0},{5,1},{6,2},{7,3},{8,12},{9,13},{10,... | collective-permute-start | bytes 2359304 | tf_op jit(solution)/shard_map/ppermute | solution.py:330
  133.5 28.8 %collective-permute-start.20 = (bf16[6,2,1,64,512]{4,3,2,1,0:T(8,128)(2,1)}, bf16[6,2,1,64,512]{4,3,2,1,0:T(8,128)(2,1)S(1)}, u32[]{:S(2)}, u32[]{:S(2)}) collective-permute-start(bf16[6,2,1,64,512]{4,3,2,1,0:T(8,128)(2,1)} %get-tuple-element.109.refs_4_), channel_id=1, source_target_pairs={{0,8},{1,0},{2,10},{3,2},{4,12},{5,4},{6,14},{7,6},{8,16},{9,1},{1... | collective-permute-start | bytes 2359304 | tf_op jit(solution)/shard_map/ppermute | solution.py:330
  136.7 36.8 %collective-permute-start.21 = (bf16[6,2,1,64,512]{4,3,2,1,0:T(8,128)(2,1)}, bf16[6,2,1,64,512]{4,3,2,1,0:T(8,128)(2,1)S(1)}, u32[]{:S(2)}, u32[]{:S(2)}) collective-permute-start(bf16[6,2,1,64,512]{4,3,2,1,0:T(8,128)(2,1)} %get-tuple-element.110.refs_5_), channel_id=1, source_target_pairs={{0,1},{1,9},{2,3},{3,11},{4,5},{5,13},{6,7},{7,15},{8,0},{9,17},{1... | collective-permute-start | bytes 2359304 | tf_op jit(solution)/shard_map/ppermute | solution.py:330
  145.5 28.0 %collective-permute-start.22 = (bf16[6,2,1,64,512]{4,3,2,1,0:T(8,128)(2,1)}, bf16[6,2,1,64,512]{4,3,2,1,0:T(8,128)(2,1)S(1)}, u32[]{:S(2)}, u32[]{:S(2)}) collective-permute-start(bf16[6,2,1,64,512]{4,3,2,1,0:T(8,128)(2,1)} %get-tuple-element.113), channel_id=1, source_target_pairs={{0,4},{1,5},{2,6},{3,7},{4,0},{5,1},{6,2},{7,3},{8,12},{9,13},{10,... | collective-permute-start | bytes 2359304 | tf_op jit(solution)/shard_map/ppermute | solution.py:330
  150.4 29.4 %collective-permute-start.18 = (bf16[6,2,1,64,512]{4,3,2,1,0:T(8,128)(2,1)}, bf16[6,2,1,64,512]{4,3,2,1,0:T(8,128)(2,1)S(1)}, u32[]{:S(2)}, u32[]{:S(2)}) collective-permute-start(bf16[6,2,1,64,512]{4,3,2,1,0:T(8,128)(2,1)} %get-tuple-element.107.refs_2_.refs_0_), channel_id=1, source_target_pairs={{0,8},{1,0},{2,10},{3,2},{4,12},{5,4},{6,14},{7,6},{8,16},{9,1},{1... | collective-permute-start | bytes 2359304 | tf_op jit(solution)/shard_map/ppermute | solution.py:330
  152.8 27.0 %collective-permute-start.19 = (bf16[6,2,1,64,512]{4,3,2,1,0:T(8,128)(2,1)}, bf16[6,2,1,64,512]{4,3,2,1,0:T(8,128)(2,1)S(1)}, u32[]{:S(2)}, u32[]{:S(2)}) collective-permute-start(bf16[6,2,1,64,512]{4,3,2,1,0:T(8,128)(2,1)} %get-tuple-element.108.refs_3_.refs_1_), channel_id=1, source_target_pairs={{0,1},{1,9},{2,3},{3,11},{4,5},{5,13},{6,7},{7,15},{8,0},{9,17},{1... | collective-permute-start | bytes 2359304 | tf_op jit(solution)/shard_map/ppermute | solution.py:330
  162.4 11.1 %copy-start.26 = (bf16[6,2,1,64,512]{4,3,2,1,0:T(8,128)(2,1)}, bf16[6,2,1,64,512]{4,3,2,1,0:T(8,128)(2,1)S(1)}, u32[]{:S(2)}) copy-start(bf16[6,2,1,64,512]{4,3,2,1,0:T(8,128)(2,1)S(1)} %collective-permute-done.20.refs_6_) | copy-start | bytes 2359300
  162.4 18.0 %collective-permute-start.23 = (bf16[6,2,1,64,512]{4,3,2,1,0:T(8,128)(2,1)}, bf16[6,2,1,64,512]{4,3,2,1,0:T(8,128)(2,1)S(1)}, u32[]{:S(2)}, u32[]{:S(2)}) collective-permute-start(bf16[6,2,1,64,512]{4,3,2,1,0:T(8,128)(2,1)} %get-tuple-element.115), channel_id=1, source_target_pairs={{0,4},{1,5},{2,6},{3,7},{4,0},{5,1},{6,2},{7,3},{8,12},{9,13},{10,... | collective-permute-start | bytes 2359304 | tf_op jit(solution)/shard_map/ppermute | solution.py:330
  177.7 17.5 %collective-permute-start.28 = (bf16[6,2,1,64,512]{4,3,2,1,0:T(8,128)(2,1)}, bf16[6,2,1,64,512]{4,3,2,1,0:T(8,128)(2,1)S(1)}, u32[]{:S(2)}, u32[]{:S(2)}) collective-permute-start(bf16[6,2,1,64,512]{4,3,2,1,0:T(8,128)(2,1)} %get-tuple-element.120), channel_id=1, source_target_pairs={{0,4},{1,5},{2,6},{3,7},{4,0},{5,1},{6,2},{7,3},{8,12},{9,13},{10,... | collective-permute-start | bytes 2359304 | tf_op jit(solution)/shard_map/ppermute | solution.py:330
  178.2 30.3 %collective-permute-start.26 = (bf16[6,2,1,64,512]{4,3,2,1,0:T(8,128)(2,1)}, bf16[6,2,1,64,512]{4,3,2,1,0:T(8,128)(2,1)S(1)}, u32[]{:S(2)}, u32[]{:S(2)}) collective-permute-start(bf16[6,2,1,64,512]{4,3,2,1,0:T(8,128)(2,1)} %get-tuple-element.118.refs_2_), channel_id=1, source_target_pairs={{0,8},{1,0},{2,10},{3,2},{4,12},{5,4},{6,14},{7,6},{8,16},{9,1},{1... | collective-permute-start | bytes 2359304 | tf_op jit(solution)/shard_map/ppermute | solution.py:330
  179.8 28.7 %collective-permute-start.27 = (bf16[6,2,1,64,512]{4,3,2,1,0:T(8,128)(2,1)}, bf16[6,2,1,64,512]{4,3,2,1,0:T(8,128)(2,1)S(1)}, u32[]{:S(2)}, u32[]{:S(2)}) collective-permute-start(bf16[6,2,1,64,512]{4,3,2,1,0:T(8,128)(2,1)} %get-tuple-element.119.refs_3_), channel_id=1, source_target_pairs={{0,1},{1,9},{2,3},{3,11},{4,5},{5,13},{6,7},{7,15},{8,0},{9,17},{1... | collective-permute-start | bytes 2359304 | tf_op jit(solution)/shard_map/ppermute | solution.py:330
  184.2 31.6 %collective-permute-start.24 = (bf16[6,2,1,64,512]{4,3,2,1,0:T(8,128)(2,1)}, bf16[6,2,1,64,512]{4,3,2,1,0:T(8,128)(2,1)S(1)}, u32[]{:S(2)}, u32[]{:S(2)}) collective-permute-start(bf16[6,2,1,64,512]{4,3,2,1,0:T(8,128)(2,1)} %get-tuple-element.116.refs_4_.refs_2_.refs_0_), channel_id=1, source_target_pairs={{0,8},{1,0},{2,10},{3,2},{4,12},{5,4},{6,14},{7,6},{8,16},{9,1},{1... | collective-permute-start | bytes 2359304 | tf_op jit(solution)/shard_map/ppermute | solution.py:330
  186.0 29.8 %collective-permute-start.25 = (bf16[6,2,1,64,512]{4,3,2,1,0:T(8,128)(2,1)}, bf16[6,2,1,64,512]{4,3,2,1,0:T(8,128)(2,1)S(1)}, u32[]{:S(2)}, u32[]{:S(2)}) collective-permute-start(bf16[6,2,1,64,512]{4,3,2,1,0:T(8,128)(2,1)} %get-tuple-element.117.refs_5_.refs_3_.refs_1_), channel_id=1, source_target_pairs={{0,1},{1,9},{2,3},{3,11},{4,5},{5,13},{6,7},{7,15},{8,0},{9,17},{1... | collective-permute-start | bytes 2359304 | tf_op jit(solution)/shard_map/ppermute | solution.py:330
  195.2 20.6 %collective-permute-start.29 = (bf16[6,2,1,64,512]{4,3,2,1,0:T(8,128)(2,1)}, bf16[6,2,1,64,512]{4,3,2,1,0:T(8,128)(2,1)S(1)}, u32[]{:S(2)}, u32[]{:S(2)}) collective-permute-start(bf16[6,2,1,64,512]{4,3,2,1,0:T(8,128)(2,1)} %get-tuple-element.125), channel_id=1, source_target_pairs={{0,4},{1,5},{2,6},{3,7},{4,0},{5,1},{6,2},{7,3},{8,12},{9,13},{10,... | collective-permute-start | bytes 2359304 | tf_op jit(solution)/shard_map/ppermute | solution.py:330
  211.8 17.3 %collective-permute-start.32 = (bf16[6,2,1,64,512]{4,3,2,1,0:T(8,128)(2,1)}, bf16[6,2,1,64,512]{4,3,2,1,0:T(8,128)(2,1)S(1)}, u32[]{:S(2)}, u32[]{:S(2)}) collective-permute-start(bf16[6,2,1,64,512]{4,3,2,1,0:T(8,128)(2,1)} %get-tuple-element.128), channel_id=1, source_target_pairs={{0,4},{1,5},{2,6},{3,7},{4,0},{5,1},{6,2},{7,3},{8,12},{9,13},{10,... | collective-permute-start | bytes 2359304 | tf_op jit(solution)/shard_map/ppermute | solution.py:330
  212.8 21.3 %collective-permute-start.34 = (bf16[6,2,1,64,512]{4,3,2,1,0:T(8,128)(2,1)}, bf16[6,2,1,64,512]{4,3,2,1,0:T(8,128)(2,1)S(1)}, u32[]{:S(2)}, u32[]{:S(2)}) collective-permute-start(bf16[6,2,1,64,512]{4,3,2,1,0:T(8,128)(2,1)} %get-tuple-element.130.refs_4_), channel_id=1, source_target_pairs={{0,8},{1,0},{2,10},{3,2},{4,12},{5,4},{6,14},{7,6},{8,16},{9,1},{1... | collective-permute-start | bytes 2359304 | tf_op jit(solution)/shard_map/ppermute | solution.py:330
  215.8 20.7 %collective-permute-start.35 = (bf16[6,2,1,64,512]{4,3,2,1,0:T(8,128)(2,1)}, bf16[6,2,1,64,512]{4,3,2,1,0:T(8,128)(2,1)S(1)}, u32[]{:S(2)}, u32[]{:S(2)}) collective-permute-start(bf16[6,2,1,64,512]{4,3,2,1,0:T(8,128)(2,1)} %get-tuple-element.131.refs_5_), channel_id=1, source_target_pairs={{0,1},{1,9},{2,3},{3,11},{4,5},{5,13},{6,7},{7,15},{8,0},{9,17},{1... | collective-permute-start | bytes 2359304 | tf_op jit(solution)/shard_map/ppermute | solution.py:330
  219.3 28.4 %collective-permute-start.30 = (bf16[6,2,1,64,512]{4,3,2,1,0:T(8,128)(2,1)}, bf16[6,2,1,64,512]{4,3,2,1,0:T(8,128)(2,1)S(1)}, u32[]{:S(2)}, u32[]{:S(2)}) collective-permute-start(bf16[6,2,1,64,512]{4,3,2,1,0:T(8,128)(2,1)} %get-tuple-element.126.refs_4_.refs_2_), channel_id=1, source_target_pairs={{0,8},{1,0},{2,10},{3,2},{4,12},{5,4},{6,14},{7,6},{8,16},{9,1},{1... | collective-permute-start | bytes 2359304 | tf_op jit(solution)/shard_map/ppermute | solution.py:330
  221.8 25.9 %collective-permute-start.31 = (bf16[6,2,1,64,512]{4,3,2,1,0:T(8,128)(2,1)}, bf16[6,2,1,64,512]{4,3,2,1,0:T(8,128)(2,1)S(1)}, u32[]{:S(2)}, u32[]{:S(2)}) collective-permute-start(bf16[6,2,1,64,512]{4,3,2,1,0:T(8,128)(2,1)} %get-tuple-element.127.refs_5_.refs_3_), channel_id=1, source_target_pairs={{0,1},{1,9},{2,3},{3,11},{4,5},{5,13},{6,7},{7,15},{8,0},{9,17},{1... | collective-permute-start | bytes 2359304 | tf_op jit(solution)/shard_map/ppermute | solution.py:330
  229.1 7.3 %copy-start.9 = (bf16[6,2,1,64,512]{4,3,2,1,0:T(8,128)(2,1)}, bf16[6,2,1,64,512]{4,3,2,1,0:T(8,128)(2,1)S(1)}, u32[]{:S(2)}) copy-start(bf16[6,2,1,64,512]{4,3,2,1,0:T(8,128)(2,1)S(1)} %collective-permute-done.32.refs_9_.refs_14_.refs_10_) | copy-start | bytes 2359300
  229.1 20.7 %collective-permute-start.33 = (bf16[6,2,1,64,512]{4,3,2,1,0:T(8,128)(2,1)}, bf16[6,2,1,64,512]{4,3,2,1,0:T(8,128)(2,1)S(1)}, u32[]{:S(2)}, u32[]{:S(2)}) collective-permute-start(bf16[6,2,1,64,512]{4,3,2,1,0:T(8,128)(2,1)} %get-tuple-element.129), channel_id=1, source_target_pairs={{0,4},{1,5},{2,6},{3,7},{4,0},{5,1},{6,2},{7,3},{8,12},{9,13},{10,... | collective-permute-start | bytes 2359304 | tf_op jit(solution)/shard_map/ppermute | solution.py:330
  234.1 2.4 copy-start.21
  239.4 27.2 %collective-permute-start.36 = (bf16[6,2,1,64,512]{4,3,2,1,0:T(8,128)(2,1)}, bf16[6,2,1,64,512]{4,3,2,1,0:T(8,128)(2,1)S(1)}, u32[]{:S(2)}, u32[]{:S(2)}) collective-permute-start(bf16[6,2,1,64,512]{4,3,2,1,0:T(8,128)(2,1)} %get-tuple-element.133), channel_id=1, source_target_pairs={{0,4},{1,5},{2,6},{3,7},{4,0},{5,1},{6,2},{7,3},{8,12},{9,13},{10,... | collective-permute-start | bytes 2359304 | tf_op jit(solution)/shard_map/ppermute | solution.py:330
  247.7 2.1 copy-start.23
  247.7 2.1 copy-start.24
  252.7 26.4 %collective-permute-start.37 = (bf16[5,2,1,64,512]{4,3,2,1,0:T(8,128)(2,1)}, bf16[5,2,1,64,512]{4,3,2,1,0:T(8,128)(2,1)S(1)}, u32[]{:S(2)}, u32[]{:S(2)}) collective-permute-start(bf16[5,2,1,64,512]{4,3,2,1,0:T(8,128)(2,1)} %get-tuple-element.135), channel_id=1, source_target_pairs={{0,4},{1,5},{2,6},{3,7},{4,0},{5,1},{6,2},{7,3},{8,12},{9,13},{10,... | collective-permute-start | bytes 1966088 | tf_op jit(solution)/shard_map/ppermute | solution.py:330
  (30 other events, 33.6 us)

commit v4 on v3

--- a/solution.py
+++ b/solution.py
@@ -22,7 +22,7 @@
 GATHERS = {0: (0,), 2: (1,), 3: (2,), 4: (3,)}
 TILES = {7: (0,), 9: (1,), 13: (2, 3)}
 SIDE = 6
-VMEM_BYTES = 56 * 1024 * 1024
+VMEM_BYTES = 62 * 1024 * 1024
 STEP_BYTES = 4_000_000
 
 KINDS = range(2 * NB)

time: 295 us -> 295 us (level)
  local copies, waits for them, and re-layouts: 20.5 us -> 14.6 us
  waiting for transfers between devices: 125 us -> 130 us
    unnamed x74 -> x34, local copies, waits for them, and re-layouts: 15.7 us -> 9.76 us
    ppermute x38, waiting for transfers between devices: 109 us -> 114 us  [move(): self.arrays[target] = lax.ppermute(self.arrays[source], 'tile', pairs)]
  transfers between devices with their start and end apart: 40 -> 40, of which waited for: 21 -> 21; matrix products, arithmetic and copies ran while one was open for 2% -> 2% of each run, Pallas kernels for 26% -> 25%
where the time goes in v4:
time: 295 us; the launch traced here: 294 us
  waiting for transfers between devices  130 us (44%)
  Pallas kernels  87.3 us (30%)
  starting transfers between devices  56.9 us (19%)
  local copies, waits for them, and re-layouts  14.6 us (5%)
  other arithmetic  4.81 us (2%)
    ppermute x38, waiting for transfers between devices, move(): self.arrays[target] = lax.ppermute(self.arrays[source], 'tile', pairs)  114 us
    ppermute x38, starting transfers between devices, move(): self.arrays[target] = lax.ppermute(self.arrays[source], 'tile', pairs)  48 us
    pallas_call x4, Pallas kernels, run_tiles(): pl.pallas_call(functools.partial(tiles_kernel, names, plan, lanes, scale,...  44.9 us
    pallas_call x13, Pallas kernels, run_copies(): pl.pallas_call(functools.partial(copies_kernel, names, len(after), plan,...  30.5 us
    all_to_all x2, waiting for transfers between devices, exchange(): x = lax.all_to_all(x, 'tile', 0, 0, axis_index_groups=groups, tiled=True)  15.9 us
    pallas_call x4, Pallas kernels, run_gather(): pl.pallas_call(functools.partial(gather_kernel, plan, lanes, start, list(...  11.9 us
    unnamed x34, local copies, waits for them, and re-layouts  9.76 us
    all_to_all x2, starting transfers between devices, exchange(): x = lax.all_to_all(x, 'tile', 0, 0, axis_index_groups=groups, tiled=True)  8.9 us
  transfers between devices with their start and end apart: 40, of which 21 were waited for; matrix products, arithmetic and copies ran while one was open for 2% of the time, Pallas kernels for 25%

profile of v4, /device:TPU:0, one launch (start us, length us, event | category | flops | bytes accessed | tf_op | source)
XLA Modules:
  0.0 294.5 jit_solution(15301341678615233980)
XLA Ops:
  4.0 4.2 %all-to-all-start.1 = ((bf16[4,8,2,1,16,512]{5,4,3,2,1,0:T(8,128)(2,1)}), bf16[4,8,2,1,16,512]{5,4,3,2,1,0:T(8,128)(2,1)}, u32[]{:S(2)}, u32[]{:S(2)}) async-start(bf16[4,8,2,1,16,512]{5,4,3,2,1,0:T(8,128)(2,1)} %fusion.1), calls=%async_computation.1 | async-start | bytes 2097152 | tf_op jit(solution)/shard_map/all_to_all | solution.py:306
  10.7 2.6 fusion
  13.3 10.1 %all-to-all-done.1.own = bf16[4,8,2,1,16,512]{5,4,3,2,1,0:T(8,128)(2,1)} async-done(((bf16[4,8,2,1,16,512]{5,4,3,2,1,0:T(8,128)(2,1)}), bf16[4,8,2,1,16,512]{5,4,3,2,1,0:T(8,128)(2,1)}, u32[]{:S(2)}, u32[]{:S(2)}) %all-to-all-start.1) | async-done | bytes 1048608 | tf_op jit(solution)/shard_map/all_to_all | solution.py:306
  23.4 4.7 %all-to-all-start = ((bf16[4,8,2,1,16,1536]{5,4,3,2,1,0:T(8,128)(2,1)}), bf16[4,8,2,1,16,1536]{5,4,3,2,1,0:T(8,128)(2,1)}, u32[]{:S(2)}, u32[]{:S(2)}) async-start(bf16[4,8,2,1,16,1536]{5,4,3,2,1,0:T(8,128)(2,1)} %fusion), calls=%async_computation | async-start | bytes 6291456 | tf_op jit(solution)/shard_map/all_to_all | solution.py:306
  28.1 3.8 %gather.4 = (bf16[6,2,1,64,512]{4,3,2,1,0:T(8,128)(2,1)}, bf16[6,2,1,64,512]{4,3,2,1,0:T(8,128)(2,1)}, bf16[5,2,1,64,512]{4,3,2,1,0:T(8,128)(2,1)}, s32[8,128]{1,0:T(8,128)}) custom-call(bf16[4,8,2,1,16,512]{5,4,3,2,1,0:T(8,128)(2,1)} %all-to-all-done.1.own), custom_call_target="tpu_custom_call" | custom-call | tf_op jit(solution)/shard_map/gather/pallas_call | solution.py:184
  31.9 2.4 collective-permute-start
  35.8 15.4 %collective-permute-done.2.refs_5_.refs_8_ = bf16[5,2,1,64,512]{4,3,2,1,0:T(8,128)(2,1)S(1)} collective-permute-done((bf16[5,2,1,64,512]{4,3,2,1,0:T(8,128)(2,1)}, bf16[5,2,1,64,512]{4,3,2,1,0:T(8,128)(2,1)S(1)}, u32[]{:S(2)}, u32[]{:S(2)}) %collective-permute-start.2) | collective-permute-done | bytes 655392 | tf_op jit(solution)/shard_map/ppermute | solution.py:330
  53.3 2.8 pick.13
  59.3 5.8 %all-to-all-done.own = bf16[4,8,2,1,16,1536]{5,4,3,2,1,0:T(8,128)(2,1)} async-done(((bf16[4,8,2,1,16,1536]{5,4,3,2,1,0:T(8,128)(2,1)}), bf16[4,8,2,1,16,1536]{5,4,3,2,1,0:T(8,128)(2,1)}, u32[]{:S(2)}, u32[]{:S(2)}) %all-to-all-start) | async-done | bytes 3145760 | tf_op jit(solution)/shard_map/all_to_all | solution.py:306
  65.1 2.7 gather.5
  69.8 2.4 collective-permute-start.3
  72.3 3.5 %collective-permute-done.5.refs_4_ = bf16[6,2,1,64,512]{4,3,2,1,0:T(8,128)(2,1)S(1)} collective-permute-done((bf16[6,2,1,64,512]{4,3,2,1,0:T(8,128)(2,1)}, bf16[6,2,1,64,512]{4,3,2,1,0:T(8,128)(2,1)S(1)}, u32[]{:S(2)}, u32[]{:S(2)}) %collective-permute-start.5) | collective-permute-done | bytes 786464 | tf_op jit(solution)/shard_map/ppermute | solution.py:330
  78.5 2.7 gather.6
  82.1 2.2 pick.15
  84.6 8.1 %collective-permute-done.3.refs_4_ = bf16[6,2,1,64,512]{4,3,2,1,0:T(8,128)(2,1)} collective-permute-done((bf16[6,2,1,64,512]{4,3,2,1,0:T(8,128)(2,1)}, bf16[6,2,1,64,512]{4,3,2,1,0:T(8,128)(2,1)}, u32[]{:S(2)}, u32[]{:S(2)}) %collective-permute-start.3) | collective-permute-done | bytes 786464 | tf_op jit(solution)/shard_map/ppermute | solution.py:330
  92.7 2.5 collective-permute-start.9
  95.1 2.7 gather.7
  98.8 2.9 pick.16
  102.8 4.4 %collective-permute-done.10.refs_5_.refs_7_ = bf16[6,2,1,64,512]{4,3,2,1,0:T(8,128)(2,1)} collective-permute-done((bf16[6,2,1,64,512]{4,3,2,1,0:T(8,128)(2,1)}, bf16[6,2,1,64,512]{4,3,2,1,0:T(8,128)(2,1)}, u32[]{:S(2)}, u32[]{:S(2)}) %collective-permute-start.10) | collective-permute-done | bytes 786464 | tf_op jit(solution)/shard_map/ppermute | solution.py:330
  107.1 2.6 collective-permute-start.16
  109.7 4.5 %collective-permute-done.11.refs_7_.refs_11_.refs_8_ = bf16[6,2,1,64,512]{4,3,2,1,0:T(8,128)(2,1)S(1)} collective-permute-done((bf16[6,2,1,64,512]{4,3,2,1,0:T(8,128)(2,1)}, bf16[6,2,1,64,512]{4,3,2,1,0:T(8,128)(2,1)S(1)}, u32[]{:S(2)}, u32[]{:S(2)}) %collective-permute-start.11) | collective-permute-done | bytes 786464 | tf_op jit(solution)/shard_map/ppermute | solution.py:330
  118.7 11.1 %collective-permute-done.14.refs_4_ = bf16[6,2,1,64,512]{4,3,2,1,0:T(8,128)(2,1)} collective-permute-done((bf16[6,2,1,64,512]{4,3,2,1,0:T(8,128)(2,1)}, bf16[6,2,1,64,512]{4,3,2,1,0:T(8,128)(2,1)}, u32[]{:S(2)}, u32[]{:S(2)}) %collective-permute-start.14) | collective-permute-done | bytes 786464 | tf_op jit(solution)/shard_map/ppermute | solution.py:330
  129.8 2.2 collective-permute-start.17
  132.9 2.2 pick.18
  135.1 3.2 %collective-permute-start.20 = (bf16[6,2,1,64,512]{4,3,2,1,0:T(8,128)(2,1)}, bf16[6,2,1,64,512]{4,3,2,1,0:T(8,128)(2,1)}, u32[]{:S(2)}, u32[]{:S(2)}) collective-permute-start(bf16[6,2,1,64,512]{4,3,2,1,0:T(8,128)(2,1)} %get-tuple-element.109.refs_4_), channel_id=1, source_target_pairs={{0,8},{1,0},{2,10},{3,2},{4,12},{5,4},{6,14},{7,6},{8,16},{9,1},{1... | collective-permute-start | bytes 2359304 | tf_op jit(solution)/shard_map/ppermute | solution.py:330
  138.4 8.3 %collective-permute-done.12.refs_4_ = bf16[6,2,1,64,512]{4,3,2,1,0:T(8,128)(2,1)} collective-permute-done((bf16[6,2,1,64,512]{4,3,2,1,0:T(8,128)(2,1)}, bf16[6,2,1,64,512]{4,3,2,1,0:T(8,128)(2,1)}, u32[]{:S(2)}, u32[]{:S(2)}) %collective-permute-start.12) | collective-permute-done | bytes 786464 | tf_op jit(solution)/shard_map/ppermute | solution.py:330
  146.7 2.2 collective-permute-start.22
  149.7 2.2 pick.19
  152.0 2.5 collective-permute-start.18
  154.5 9.1 %collective-permute-done.20.refs_6_ = bf16[6,2,1,64,512]{4,3,2,1,0:T(8,128)(2,1)} collective-permute-done((bf16[6,2,1,64,512]{4,3,2,1,0:T(8,128)(2,1)}, bf16[6,2,1,64,512]{4,3,2,1,0:T(8,128)(2,1)}, u32[]{:S(2)}, u32[]{:S(2)}) %collective-permute-start.20) | collective-permute-done | bytes 786464 | tf_op jit(solution)/shard_map/ppermute | solution.py:330
  163.5 2.2 collective-permute-start.23
  165.7 9.5 %tiles.4 = (f32[5,512,1024]{2,1,0:T(8,128)}, s32[8,128]{1,0:T(8,128)}) custom-call(bf16[6,2,1,64,512]{4,3,2,1,0:T(8,128)(2,1)} %get-tuple-element.73.refs_0_, bf16[6,2,1,64,512]{4,3,2,1,0:T(8,128)(2,1)} %get-tuple-element.74.refs_1_, bf16[6,2,1,64,512]{4,3,2,1,0:T(8,128)(2,1)} %get-tuple-element.77.refs_0_.refs_2_, ...), custom_call_target="tpu_custom_call", output_to_operand_aliasing={{1}: (13, {})} | custom-call | tf_op jit(solution)/shard_map/tiles/pallas_call | solution.py:271
  175.2 2.9 pick.20
  180.1 3.7 %collective-permute-done.23.refs_5_.refs_12_ = bf16[6,2,1,64,512]{4,3,2,1,0:T(8,128)(2,1)} collective-permute-done((bf16[6,2,1,64,512]{4,3,2,1,0:T(8,128)(2,1)}, bf16[6,2,1,64,512]{4,3,2,1,0:T(8,128)(2,1)}, u32[]{:S(2)}, u32[]{:S(2)}) %collective-permute-start.23) | collective-permute-done | bytes 786464 | tf_op jit(solution)/shard_map/ppermute | solution.py:330
  183.8 2.9 pick.21
  188.4 9.2 %collective-permute-done.28.refs_12_.refs_9_.refs_13_.refs_8_ = bf16[6,2,1,64,512]{4,3,2,1,0:T(8,128)(2,1)} collective-permute-done((bf16[6,2,1,64,512]{4,3,2,1,0:T(8,128)(2,1)}, bf16[6,2,1,64,512]{4,3,2,1,0:T(8,128)(2,1)}, u32[]{:S(2)}, u32[]{:S(2)}) %collective-permute-start.28) | collective-permute-done | bytes 786464 | tf_op jit(solution)/shard_map/ppermute | solution.py:330
  197.6 2.5 collective-permute-start.29
  200.0 11.6 %tiles.5 = (f32[5,512,1024]{2,1,0:T(8,128)}, s32[8,128]{1,0:T(8,128)}) custom-call(bf16[6,2,1,64,512]{4,3,2,1,0:T(8,128)(2,1)} %get-tuple-element.86.refs_0_, bf16[6,2,1,64,512]{4,3,2,1,0:T(8,128)(2,1)} %get-tuple-element.87.refs_1_, bf16[6,2,1,64,512]{4,3,2,1,0:T(8,128)(2,1)} %get-tuple-element.93.refs_2_, ...), custom_call_target="tpu_custom_call", output_to_operand_aliasing={{0}: (13, {}), {1}: (14, {})} | custom-call | tf_op jit(solution)/shard_map/tiles/pallas_call | solution.py:271
  213.9 3.2 %collective-permute-start.34 = (bf16[6,2,1,64,512]{4,3,2,1,0:T(8,128)(2,1)}, bf16[6,2,1,64,512]{4,3,2,1,0:T(8,128)(2,1)}, u32[]{:S(2)}, u32[]{:S(2)}) collective-permute-start(bf16[6,2,1,64,512]{4,3,2,1,0:T(8,128)(2,1)} %get-tuple-element.130.refs_4_), channel_id=1, source_target_pairs={{0,8},{1,0},{2,10},{3,2},{4,12},{5,4},{6,14},{7,6},{8,16},{9,1},{1... | collective-permute-start | bytes 2359304 | tf_op jit(solution)/shard_map/ppermute | solution.py:330
  220.3 2.5 collective-permute-start.30
  222.8 8.3 %collective-permute-done.32.refs_9_.refs_14_.refs_10_ = bf16[6,2,1,64,512]{4,3,2,1,0:T(8,128)(2,1)} collective-permute-done((bf16[6,2,1,64,512]{4,3,2,1,0:T(8,128)(2,1)}, bf16[6,2,1,64,512]{4,3,2,1,0:T(8,128)(2,1)}, u32[]{:S(2)}, u32[]{:S(2)}) %collective-permute-start.32) | collective-permute-done | bytes 786464 | tf_op jit(solution)/shard_map/ppermute | solution.py:330
  232.6 2.7 collective-permute-done.34.refs_6_
  235.3 2.5 collective-permute-done.35.refs_7_
  241.6 7.2 %collective-permute-done.30.refs_4_.refs_6_ = bf16[6,2,1,64,512]{4,3,2,1,0:T(8,128)(2,1)S(1)} collective-permute-done((bf16[6,2,1,64,512]{4,3,2,1,0:T(8,128)(2,1)}, bf16[6,2,1,64,512]{4,3,2,1,0:T(8,128)(2,1)S(1)}, u32[]{:S(2)}, u32[]{:S(2)}) %collective-permute-start.30) | collective-permute-done | bytes 786464 | tf_op jit(solution)/shard_map/ppermute | solution.py:330
  248.8 3.1 %collective-permute-done.33.refs_7_.refs_11_ = bf16[6,2,1,64,512]{4,3,2,1,0:T(8,128)(2,1)} collective-permute-done((bf16[6,2,1,64,512]{4,3,2,1,0:T(8,128)(2,1)}, bf16[6,2,1,64,512]{4,3,2,1,0:T(8,128)(2,1)}, u32[]{:S(2)}, u32[]{:S(2)}) %collective-permute-start.33) | collective-permute-done | bytes 786464 | tf_op jit(solution)/shard_map/ppermute | solution.py:330
  256.8 11.9 %collective-permute-done.36.refs_15_.refs_12_ = bf16[6,2,1,64,512]{4,3,2,1,0:T(8,128)(2,1)S(1)} collective-permute-done((bf16[6,2,1,64,512]{4,3,2,1,0:T(8,128)(2,1)}, bf16[6,2,1,64,512]{4,3,2,1,0:T(8,128)(2,1)S(1)}, u32[]{:S(2)}, u32[]{:S(2)}) %collective-permute-start.36) | collective-permute-done | bytes 786464 | tf_op jit(solution)/shard_map/ppermute | solution.py:330
  269.6 11.6 %tiles.6 = (f32[5,512,1024]{2,1,0:T(8,128)}, s32[8,128]{1,0:T(8,128)}) custom-call(bf16[6,2,1,64,512]{4,3,2,1,0:T(8,128)(2,1)} %get-tuple-element.99.refs_2_.refs_0_, bf16[6,2,1,64,512]{4,3,2,1,0:T(8,128)(2,1)} %get-tuple-element.100.refs_3_.refs_1_, ...), custom_call_target="tpu_custom_call", output_to_operand_aliasing={{0}: (16, {}), {1}: (17, {})} | custom-call | tf_op jit(solution)/shard_map/tiles/pallas_call | solution.py:271
  282.0 12.3 %tiles.7 = (f32[5,512,1024]{2,1,0:T(8,128)}, s32[8,128]{1,0:T(8,128)}) custom-call(bf16[6,2,1,64,512]{4,3,2,1,0:T(8,128)(2,1)} %get-tuple-element.107.refs_2_.refs_0_, bf16[6,2,1,64,512]{4,3,2,1,0:T(8,128)(2,1)} %get-tuple-element.108.refs_3_.refs_1_, ...), custom_call_target="tpu_custom_call", output_to_operand_aliasing={{0}: (15, {}), {1}: (16, {})} | custom-call | tf_op jit(solution)/shard_map/tiles/pallas_call | solution.py:271
  (105 shorter events, 48.4 us)
Async XLA Ops:
  0.0 2.4 slice-start
  4.0 19.4 %all-to-all-start.1 = ((bf16[4,8,2,1,16,512]{5,4,3,2,1,0:T(8,128)(2,1)}), bf16[4,8,2,1,16,512]{5,4,3,2,1,0:T(8,128)(2,1)}, u32[]{:S(2)}, u32[]{:S(2)}) async-start(bf16[4,8,2,1,16,512]{5,4,3,2,1,0:T(8,128)(2,1)} %fusion.1), calls=%async_computation.1 | async-start | bytes 2097152 | tf_op jit(solution)/shard_map/all_to_all | solution.py:306
  8.3 1.9 slice-start.1
  23.4 41.7 %all-to-all-start = ((bf16[4,8,2,1,16,1536]{5,4,3,2,1,0:T(8,128)(2,1)}), bf16[4,8,2,1,16,1536]{5,4,3,2,1,0:T(8,128)(2,1)}, u32[]{:S(2)}, u32[]{:S(2)}) async-start(bf16[4,8,2,1,16,1536]{5,4,3,2,1,0:T(8,128)(2,1)} %fusion), calls=%async_computation | async-start | bytes 6291456 | tf_op jit(solution)/shard_map/all_to_all | solution.py:306
  31.9 20.0 %collective-permute-start = (bf16[6,2,1,64,512]{4,3,2,1,0:T(8,128)(2,1)}, bf16[6,2,1,64,512]{4,3,2,1,0:T(8,128)(2,1)S(1)}, u32[]{:S(2)}, u32[]{:S(2)}) collective-permute-start(bf16[6,2,1,64,512]{4,3,2,1,0:T(8,128)(2,1)} %get-tuple-element.73.refs_0_), channel_id=1, source_target_pairs={{0,8},{1,0},{2,10},{3,2},{4,12},{5,4},{6,14},{7,6},{8,16},{9,1},{1... | collective-permute-start | bytes 2359304 | tf_op jit(solution)/shard_map/ppermute | solution.py:330
  34.3 18.2 %collective-permute-start.1 = (bf16[6,2,1,64,512]{4,3,2,1,0:T(8,128)(2,1)}, bf16[6,2,1,64,512]{4,3,2,1,0:T(8,128)(2,1)S(1)}, u32[]{:S(2)}, u32[]{:S(2)}) collective-permute-start(bf16[6,2,1,64,512]{4,3,2,1,0:T(8,128)(2,1)} %get-tuple-element.74.refs_1_), channel_id=1, source_target_pairs={{0,1},{1,9},{2,3},{3,11},{4,5},{5,13},{6,7},{7,15},{8,0},{9,17},{1... | collective-permute-start | bytes 2359304 | tf_op jit(solution)/shard_map/ppermute | solution.py:330
  34.3 16.9 %collective-permute-start.2 = (bf16[5,2,1,64,512]{4,3,2,1,0:T(8,128)(2,1)}, bf16[5,2,1,64,512]{4,3,2,1,0:T(8,128)(2,1)S(1)}, u32[]{:S(2)}, u32[]{:S(2)}) collective-permute-start(bf16[5,2,1,64,512]{4,3,2,1,0:T(8,128)(2,1)} %get-tuple-element.76), channel_id=1, source_target_pairs={{0,4},{1,5},{2,6},{3,7},{4,0},{5,1},{6,2},{7,3},{8,12},{9,13},{10,... | collective-permute-start | bytes 1966088 | tf_op jit(solution)/shard_map/ppermute | solution.py:330
  51.2 1.3 copy-start.10
  56.2 19.6 %collective-permute-start.5 = (bf16[6,2,1,64,512]{4,3,2,1,0:T(8,128)(2,1)}, bf16[6,2,1,64,512]{4,3,2,1,0:T(8,128)(2,1)S(1)}, u32[]{:S(2)}, u32[]{:S(2)}) collective-permute-start(bf16[6,2,1,64,512]{4,3,2,1,0:T(8,128)(2,1)} %get-tuple-element.77.refs_0_.refs_2_), channel_id=1, source_target_pairs={{0,8},{1,0},{2,10},{3,2},{4,12},{5,4},{6,14},{7,6},{8,16},{9,1},{1... | collective-permute-start | bytes 2359304 | tf_op jit(solution)/shard_map/ppermute | solution.py:330
  57.5 23.7 %collective-permute-start.6 = (bf16[6,2,1,64,512]{4,3,2,1,0:T(8,128)(2,1)}, bf16[6,2,1,64,512]{4,3,2,1,0:T(8,128)(2,1)}, u32[]{:S(2)}, u32[]{:S(2)}) collective-permute-start(bf16[6,2,1,64,512]{4,3,2,1,0:T(8,128)(2,1)} %get-tuple-element.78.refs_1_.refs_3_), channel_id=1, source_target_pairs={{0,1},{1,9},{2,3},{3,11},{4,5},{5,13},{6,7},{7,15},{8,0},{9,17},{1... | collective-permute-start | bytes 2359304 | tf_op jit(solution)/shard_map/ppermute | solution.py:330
  57.5 23.7 %collective-permute-start.7 = (bf16[6,2,1,64,512]{4,3,2,1,0:T(8,128)(2,1)}, bf16[6,2,1,64,512]{4,3,2,1,0:T(8,128)(2,1)S(1)}, u32[]{:S(2)}, u32[]{:S(2)}) collective-permute-start(bf16[6,2,1,64,512]{4,3,2,1,0:T(8,128)(2,1)} %get-tuple-element.89), channel_id=1, source_target_pairs={{0,4},{1,5},{2,6},{3,7},{4,0},{5,1},{6,2},{7,3},{8,12},{9,13},{10,... | collective-permute-start | bytes 2359304 | tf_op jit(solution)/shard_map/ppermute | solution.py:330
  69.8 22.8 %collective-permute-start.3 = (bf16[6,2,1,64,512]{4,3,2,1,0:T(8,128)(2,1)}, bf16[6,2,1,64,512]{4,3,2,1,0:T(8,128)(2,1)}, u32[]{:S(2)}, u32[]{:S(2)}) collective-permute-start(bf16[6,2,1,64,512]{4,3,2,1,0:T(8,128)(2,1)} %get-tuple-element.86.refs_0_), channel_id=1, source_target_pairs={{0,8},{1,0},{2,10},{3,2},{4,12},{5,4},{6,14},{7,6},{8,16},{9,1},{1... | collective-permute-start | bytes 2359304 | tf_op jit(solution)/shard_map/ppermute | solution.py:330
  72.3 25.6 %collective-permute-start.4 = (bf16[6,2,1,64,512]{4,3,2,1,0:T(8,128)(2,1)}, bf16[6,2,1,64,512]{4,3,2,1,0:T(8,128)(2,1)}, u32[]{:S(2)}, u32[]{:S(2)}) collective-permute-start(bf16[6,2,1,64,512]{4,3,2,1,0:T(8,128)(2,1)} %get-tuple-element.87.refs_1_), channel_id=1, source_target_pairs={{0,1},{1,9},{2,3},{3,11},{4,5},{5,13},{6,7},{7,15},{8,0},{9,17},{1... | collective-permute-start | bytes 2359304 | tf_op jit(solution)/shard_map/ppermute | solution.py:330
  76.7 21.2 %collective-permute-start.8 = (bf16[6,2,1,64,512]{4,3,2,1,0:T(8,128)(2,1)}, bf16[6,2,1,64,512]{4,3,2,1,0:T(8,128)(2,1)S(1)}, u32[]{:S(2)}, u32[]{:S(2)}) collective-permute-start(bf16[6,2,1,64,512]{4,3,2,1,0:T(8,128)(2,1)} %get-tuple-element.92), channel_id=1, source_target_pairs={{0,4},{1,5},{2,6},{3,7},{4,0},{5,1},{6,2},{7,3},{8,12},{9,13},{10,... | collective-permute-start | bytes 2359304 | tf_op jit(solution)/shard_map/ppermute | solution.py:330
  84.3 22.9 %collective-permute-start.10 = (bf16[6,2,1,64,512]{4,3,2,1,0:T(8,128)(2,1)}, bf16[6,2,1,64,512]{4,3,2,1,0:T(8,128)(2,1)}, u32[]{:S(2)}, u32[]{:S(2)}) collective-permute-start(bf16[6,2,1,64,512]{4,3,2,1,0:T(8,128)(2,1)} %get-tuple-element.96.refs_5_), channel_id=1, source_target_pairs={{0,1},{1,9},{2,3},{3,11},{4,5},{5,13},{6,7},{7,15},{8,0},{9,17},{1... | collective-permute-start | bytes 2359304 | tf_op jit(solution)/shard_map/ppermute | solution.py:330
  84.3 30.0 %collective-permute-start.11 = (bf16[6,2,1,64,512]{4,3,2,1,0:T(8,128)(2,1)}, bf16[6,2,1,64,512]{4,3,2,1,0:T(8,128)(2,1)S(1)}, u32[]{:S(2)}, u32[]{:S(2)}) collective-permute-start(bf16[6,2,1,64,512]{4,3,2,1,0:T(8,128)(2,1)} %get-tuple-element.98), channel_id=1, source_target_pairs={{0,4},{1,5},{2,6},{3,7},{4,0},{5,1},{6,2},{7,3},{8,12},{9,13},{10,... | collective-permute-start | bytes 2359304 | tf_op jit(solution)/shard_map/ppermute | solution.py:330
  92.7 21.6 %collective-permute-start.9 = (bf16[6,2,1,64,512]{4,3,2,1,0:T(8,128)(2,1)}, bf16[6,2,1,64,512]{4,3,2,1,0:T(8,128)(2,1)}, u32[]{:S(2)}, u32[]{:S(2)}) collective-permute-start(bf16[6,2,1,64,512]{4,3,2,1,0:T(8,128)(2,1)} %get-tuple-element.95.refs_4_), channel_id=1, source_target_pairs={{0,8},{1,0},{2,10},{3,2},{4,12},{5,4},{6,14},{7,6},{8,16},{9,1},{1... | collective-permute-start | bytes 2359304 | tf_op jit(solution)/shard_map/ppermute | solution.py:330
  101.7 28.1 %collective-permute-start.14 = (bf16[6,2,1,64,512]{4,3,2,1,0:T(8,128)(2,1)}, bf16[6,2,1,64,512]{4,3,2,1,0:T(8,128)(2,1)}, u32[]{:S(2)}, u32[]{:S(2)}) collective-permute-start(bf16[6,2,1,64,512]{4,3,2,1,0:T(8,128)(2,1)} %get-tuple-element.93.refs_2_), channel_id=1, source_target_pairs={{0,8},{1,0},{2,10},{3,2},{4,12},{5,4},{6,14},{7,6},{8,16},{9,1},{1... | collective-permute-start | bytes 2359304 | tf_op jit(solution)/shard_map/ppermute | solution.py:330
  102.8 29.2 %collective-permute-start.15 = (bf16[6,2,1,64,512]{4,3,2,1,0:T(8,128)(2,1)}, bf16[6,2,1,64,512]{4,3,2,1,0:T(8,128)(2,1)}, u32[]{:S(2)}, u32[]{:S(2)}) collective-permute-start(bf16[6,2,1,64,512]{4,3,2,1,0:T(8,128)(2,1)} %get-tuple-element.94.refs_3_), channel_id=1, source_target_pairs={{0,1},{1,9},{2,3},{3,11},{4,5},{5,13},{6,7},{7,15},{8,0},{9,17},{1... | collective-permute-start | bytes 2359304 | tf_op jit(solution)/shard_map/ppermute | solution.py:330
  107.1 24.9 %collective-permute-start.16 = (bf16[6,2,1,64,512]{4,3,2,1,0:T(8,128)(2,1)}, bf16[6,2,1,64,512]{4,3,2,1,0:T(8,128)(2,1)S(1)}, u32[]{:S(2)}, u32[]{:S(2)}) collective-permute-start(bf16[6,2,1,64,512]{4,3,2,1,0:T(8,128)(2,1)} %get-tuple-element.104), channel_id=1, source_target_pairs={{0,4},{1,5},{2,6},{3,7},{4,0},{5,1},{6,2},{7,3},{8,12},{9,13},{10,... | collective-permute-start | bytes 2359304 | tf_op jit(solution)/shard_map/ppermute | solution.py:330
  117.3 29.4 %collective-permute-start.12 = (bf16[6,2,1,64,512]{4,3,2,1,0:T(8,128)(2,1)}, bf16[6,2,1,64,512]{4,3,2,1,0:T(8,128)(2,1)}, u32[]{:S(2)}, u32[]{:S(2)}) collective-permute-start(bf16[6,2,1,64,512]{4,3,2,1,0:T(8,128)(2,1)} %get-tuple-element.99.refs_2_.refs_0_), channel_id=1, source_target_pairs={{0,8},{1,0},{2,10},{3,2},{4,12},{5,4},{6,14},{7,6},{8,16},{9,1},{1... | collective-permute-start | bytes 2359304 | tf_op jit(solution)/shard_map/ppermute | solution.py:330
  118.7 30.1 %collective-permute-start.13 = (bf16[6,2,1,64,512]{4,3,2,1,0:T(8,128)(2,1)}, bf16[6,2,1,64,512]{4,3,2,1,0:T(8,128)(2,1)}, u32[]{:S(2)}, u32[]{:S(2)}) collective-permute-start(bf16[6,2,1,64,512]{4,3,2,1,0:T(8,128)(2,1)} %get-tuple-element.100.refs_3_.refs_1_), channel_id=1, source_target_pairs={{0,1},{1,9},{2,3},{3,11},{4,5},{5,13},{6,7},{7,15},{8,0},{9,17},{1... | collective-permute-start | bytes 2359304 | tf_op jit(solution)/shard_map/ppermute | solution.py:330
  129.8 19.1 %collective-permute-start.17 = (bf16[6,2,1,64,512]{4,3,2,1,0:T(8,128)(2,1)}, bf16[6,2,1,64,512]{4,3,2,1,0:T(8,128)(2,1)S(1)}, u32[]{:S(2)}, u32[]{:S(2)}) collective-permute-start(bf16[6,2,1,64,512]{4,3,2,1,0:T(8,128)(2,1)} %get-tuple-element.106), channel_id=1, source_target_pairs={{0,4},{1,5},{2,6},{3,7},{4,0},{5,1},{6,2},{7,3},{8,12},{9,13},{10,... | collective-permute-start | bytes 2359304 | tf_op jit(solution)/shard_map/ppermute | solution.py:330
  132.0 0.9 copy-start.5
  135.1 28.4 %collective-permute-start.20 = (bf16[6,2,1,64,512]{4,3,2,1,0:T(8,128)(2,1)}, bf16[6,2,1,64,512]{4,3,2,1,0:T(8,128)(2,1)}, u32[]{:S(2)}, u32[]{:S(2)}) collective-permute-start(bf16[6,2,1,64,512]{4,3,2,1,0:T(8,128)(2,1)} %get-tuple-element.109.refs_4_), channel_id=1, source_target_pairs={{0,8},{1,0},{2,10},{3,2},{4,12},{5,4},{6,14},{7,6},{8,16},{9,1},{1... | collective-permute-start | bytes 2359304 | tf_op jit(solution)/shard_map/ppermute | solution.py:330
  138.4 36.9 %collective-permute-start.21 = (bf16[6,2,1,64,512]{4,3,2,1,0:T(8,128)(2,1)}, bf16[6,2,1,64,512]{4,3,2,1,0:T(8,128)(2,1)}, u32[]{:S(2)}, u32[]{:S(2)}) collective-permute-start(bf16[6,2,1,64,512]{4,3,2,1,0:T(8,128)(2,1)} %get-tuple-element.110.refs_5_), channel_id=1, source_target_pairs={{0,1},{1,9},{2,3},{3,11},{4,5},{5,13},{6,7},{7,15},{8,0},{9,17},{1... | collective-permute-start | bytes 2359304 | tf_op jit(solution)/shard_map/ppermute | solution.py:330
  146.7 28.6 %collective-permute-start.22 = (bf16[6,2,1,64,512]{4,3,2,1,0:T(8,128)(2,1)}, bf16[6,2,1,64,512]{4,3,2,1,0:T(8,128)(2,1)}, u32[]{:S(2)}, u32[]{:S(2)}) collective-permute-start(bf16[6,2,1,64,512]{4,3,2,1,0:T(8,128)(2,1)} %get-tuple-element.113), channel_id=1, source_target_pairs={{0,4},{1,5},{2,6},{3,7},{4,0},{5,1},{6,2},{7,3},{8,12},{9,13},{10,... | collective-permute-start | bytes 2359304 | tf_op jit(solution)/shard_map/ppermute | solution.py:330
  152.0 28.1 %collective-permute-start.18 = (bf16[6,2,1,64,512]{4,3,2,1,0:T(8,128)(2,1)}, bf16[6,2,1,64,512]{4,3,2,1,0:T(8,128)(2,1)S(1)}, u32[]{:S(2)}, u32[]{:S(2)}) collective-permute-start(bf16[6,2,1,64,512]{4,3,2,1,0:T(8,128)(2,1)} %get-tuple-element.107.refs_2_.refs_0_), channel_id=1, source_target_pairs={{0,8},{1,0},{2,10},{3,2},{4,12},{5,4},{6,14},{7,6},{8,16},{9,1},{1... | collective-permute-start | bytes 2359304 | tf_op jit(solution)/shard_map/ppermute | solution.py:330
  154.4 25.6 %collective-permute-start.19 = (bf16[6,2,1,64,512]{4,3,2,1,0:T(8,128)(2,1)}, bf16[6,2,1,64,512]{4,3,2,1,0:T(8,128)(2,1)S(1)}, u32[]{:S(2)}, u32[]{:S(2)}) collective-permute-start(bf16[6,2,1,64,512]{4,3,2,1,0:T(8,128)(2,1)} %get-tuple-element.108.refs_3_.refs_1_), channel_id=1, source_target_pairs={{0,1},{1,9},{2,3},{3,11},{4,5},{5,13},{6,7},{7,15},{8,0},{9,17},{1... | collective-permute-start | bytes 2359304 | tf_op jit(solution)/shard_map/ppermute | solution.py:330
  163.5 20.3 %collective-permute-start.23 = (bf16[6,2,1,64,512]{4,3,2,1,0:T(8,128)(2,1)}, bf16[6,2,1,64,512]{4,3,2,1,0:T(8,128)(2,1)}, u32[]{:S(2)}, u32[]{:S(2)}) collective-permute-start(bf16[6,2,1,64,512]{4,3,2,1,0:T(8,128)(2,1)} %get-tuple-element.115), channel_id=1, source_target_pairs={{0,4},{1,5},{2,6},{3,7},{4,0},{5,1},{6,2},{7,3},{8,12},{9,13},{10,... | collective-permute-start | bytes 2359304 | tf_op jit(solution)/shard_map/ppermute | solution.py:330
  178.2 19.4 %collective-permute-start.28 = (bf16[6,2,1,64,512]{4,3,2,1,0:T(8,128)(2,1)}, bf16[6,2,1,64,512]{4,3,2,1,0:T(8,128)(2,1)}, u32[]{:S(2)}, u32[]{:S(2)}) collective-permute-start(bf16[6,2,1,64,512]{4,3,2,1,0:T(8,128)(2,1)} %get-tuple-element.120), channel_id=1, source_target_pairs={{0,4},{1,5},{2,6},{3,7},{4,0},{5,1},{6,2},{7,3},{8,12},{9,13},{10,... | collective-permute-start | bytes 2359304 | tf_op jit(solution)/shard_map/ppermute | solution.py:330
  178.2 33.4 %collective-permute-start.26 = (bf16[6,2,1,64,512]{4,3,2,1,0:T(8,128)(2,1)}, bf16[6,2,1,64,512]{4,3,2,1,0:T(8,128)(2,1)}, u32[]{:S(2)}, u32[]{:S(2)}) collective-permute-start(bf16[6,2,1,64,512]{4,3,2,1,0:T(8,128)(2,1)} %get-tuple-element.118.refs_2_), channel_id=1, source_target_pairs={{0,8},{1,0},{2,10},{3,2},{4,12},{5,4},{6,14},{7,6},{8,16},{9,1},{1... | collective-permute-start | bytes 2359304 | tf_op jit(solution)/shard_map/ppermute | solution.py:330
  180.0 3.8 %copy-start = (bf16[6,2,1,64,512]{4,3,2,1,0:T(8,128)(2,1)}, bf16[6,2,1,64,512]{4,3,2,1,0:T(8,128)(2,1)S(1)}, u32[]{:S(2)}) copy-start(bf16[6,2,1,64,512]{4,3,2,1,0:T(8,128)(2,1)S(1)} %collective-permute-done.18.refs_2_) | copy-start | bytes 2359300
  180.0 31.6 %collective-permute-start.27 = (bf16[6,2,1,64,512]{4,3,2,1,0:T(8,128)(2,1)}, bf16[6,2,1,64,512]{4,3,2,1,0:T(8,128)(2,1)}, u32[]{:S(2)}, u32[]{:S(2)}) collective-permute-start(bf16[6,2,1,64,512]{4,3,2,1,0:T(8,128)(2,1)} %get-tuple-element.119.refs_3_), channel_id=1, source_target_pairs={{0,1},{1,9},{2,3},{3,11},{4,5},{5,13},{6,7},{7,15},{8,0},{9,17},{1... | collective-permute-start | bytes 2359304 | tf_op jit(solution)/shard_map/ppermute | solution.py:330
  180.0 3.8 %copy-start.1 = (bf16[6,2,1,64,512]{4,3,2,1,0:T(8,128)(2,1)}, bf16[6,2,1,64,512]{4,3,2,1,0:T(8,128)(2,1)S(1)}, u32[]{:S(2)}) copy-start(bf16[6,2,1,64,512]{4,3,2,1,0:T(8,128)(2,1)S(1)} %collective-permute-done.19.refs_3_) | copy-start | bytes 2359300
  186.7 30.4 %collective-permute-start.24 = (bf16[6,2,1,64,512]{4,3,2,1,0:T(8,128)(2,1)}, bf16[6,2,1,64,512]{4,3,2,1,0:T(8,128)(2,1)S(1)}, u32[]{:S(2)}, u32[]{:S(2)}) collective-permute-start(bf16[6,2,1,64,512]{4,3,2,1,0:T(8,128)(2,1)} %get-tuple-element.116.refs_4_.refs_2_.refs_0_), channel_id=1, source_target_pairs={{0,8},{1,0},{2,10},{3,2},{4,12},{5,4},{6,14},{7,6},{8,16},{9,1},{1... | collective-permute-start | bytes 2359304 | tf_op jit(solution)/shard_map/ppermute | solution.py:330
  188.4 28.7 %collective-permute-start.25 = (bf16[6,2,1,64,512]{4,3,2,1,0:T(8,128)(2,1)}, bf16[6,2,1,64,512]{4,3,2,1,0:T(8,128)(2,1)S(1)}, u32[]{:S(2)}, u32[]{:S(2)}) collective-permute-start(bf16[6,2,1,64,512]{4,3,2,1,0:T(8,128)(2,1)} %get-tuple-element.117.refs_5_.refs_3_.refs_1_), channel_id=1, source_target_pairs={{0,1},{1,9},{2,3},{3,11},{4,5},{5,13},{6,7},{7,15},{8,0},{9,17},{1... | collective-permute-start | bytes 2359304 | tf_op jit(solution)/shard_map/ppermute | solution.py:330
  197.6 19.7 %collective-permute-start.29 = (bf16[6,2,1,64,512]{4,3,2,1,0:T(8,128)(2,1)}, bf16[6,2,1,64,512]{4,3,2,1,0:T(8,128)(2,1)}, u32[]{:S(2)}, u32[]{:S(2)}) collective-permute-start(bf16[6,2,1,64,512]{4,3,2,1,0:T(8,128)(2,1)} %get-tuple-element.125), channel_id=1, source_target_pairs={{0,4},{1,5},{2,6},{3,7},{4,0},{5,1},{6,2},{7,3},{8,12},{9,13},{10,... | collective-permute-start | bytes 2359304 | tf_op jit(solution)/shard_map/ppermute | solution.py:330
  213.8 17.3 %collective-permute-start.32 = (bf16[6,2,1,64,512]{4,3,2,1,0:T(8,128)(2,1)}, bf16[6,2,1,64,512]{4,3,2,1,0:T(8,128)(2,1)}, u32[]{:S(2)}, u32[]{:S(2)}) collective-permute-start(bf16[6,2,1,64,512]{4,3,2,1,0:T(8,128)(2,1)} %get-tuple-element.128), channel_id=1, source_target_pairs={{0,4},{1,5},{2,6},{3,7},{4,0},{5,1},{6,2},{7,3},{8,12},{9,13},{10,... | collective-permute-start | bytes 2359304 | tf_op jit(solution)/shard_map/ppermute | solution.py:330
  213.9 21.5 %collective-permute-start.34 = (bf16[6,2,1,64,512]{4,3,2,1,0:T(8,128)(2,1)}, bf16[6,2,1,64,512]{4,3,2,1,0:T(8,128)(2,1)}, u32[]{:S(2)}, u32[]{:S(2)}) collective-permute-start(bf16[6,2,1,64,512]{4,3,2,1,0:T(8,128)(2,1)} %get-tuple-element.130.refs_4_), channel_id=1, source_target_pairs={{0,8},{1,0},{2,10},{3,2},{4,12},{5,4},{6,14},{7,6},{8,16},{9,1},{1... | collective-permute-start | bytes 2359304 | tf_op jit(solution)/shard_map/ppermute | solution.py:330
  217.0 20.8 %collective-permute-start.35 = (bf16[6,2,1,64,512]{4,3,2,1,0:T(8,128)(2,1)}, bf16[6,2,1,64,512]{4,3,2,1,0:T(8,128)(2,1)}, u32[]{:S(2)}, u32[]{:S(2)}) collective-permute-start(bf16[6,2,1,64,512]{4,3,2,1,0:T(8,128)(2,1)} %get-tuple-element.131.refs_5_), channel_id=1, source_target_pairs={{0,1},{1,9},{2,3},{3,11},{4,5},{5,13},{6,7},{7,15},{8,0},{9,17},{1... | collective-permute-start | bytes 2359304 | tf_op jit(solution)/shard_map/ppermute | solution.py:330
  217.0 1.2 copy-start.4
  220.3 28.5 %collective-permute-start.30 = (bf16[6,2,1,64,512]{4,3,2,1,0:T(8,128)(2,1)}, bf16[6,2,1,64,512]{4,3,2,1,0:T(8,128)(2,1)S(1)}, u32[]{:S(2)}, u32[]{:S(2)}) collective-permute-start(bf16[6,2,1,64,512]{4,3,2,1,0:T(8,128)(2,1)} %get-tuple-element.126.refs_4_.refs_2_), channel_id=1, source_target_pairs={{0,8},{1,0},{2,10},{3,2},{4,12},{5,4},{6,14},{7,6},{8,16},{9,1},{1... | collective-permute-start | bytes 2359304 | tf_op jit(solution)/shard_map/ppermute | solution.py:330
  222.8 26.0 %collective-permute-start.31 = (bf16[6,2,1,64,512]{4,3,2,1,0:T(8,128)(2,1)}, bf16[6,2,1,64,512]{4,3,2,1,0:T(8,128)(2,1)}, u32[]{:S(2)}, u32[]{:S(2)}) collective-permute-start(bf16[6,2,1,64,512]{4,3,2,1,0:T(8,128)(2,1)} %get-tuple-element.127.refs_5_.refs_3_), channel_id=1, source_target_pairs={{0,1},{1,9},{2,3},{3,11},{4,5},{5,13},{6,7},{7,15},{8,0},{9,17},{1... | collective-permute-start | bytes 2359304 | tf_op jit(solution)/shard_map/ppermute | solution.py:330
  231.1 20.8 %collective-permute-start.33 = (bf16[6,2,1,64,512]{4,3,2,1,0:T(8,128)(2,1)}, bf16[6,2,1,64,512]{4,3,2,1,0:T(8,128)(2,1)}, u32[]{:S(2)}, u32[]{:S(2)}) collective-permute-start(bf16[6,2,1,64,512]{4,3,2,1,0:T(8,128)(2,1)} %get-tuple-element.129), channel_id=1, source_target_pairs={{0,4},{1,5},{2,6},{3,7},{4,0},{5,1},{6,2},{7,3},{8,12},{9,13},{10,... | collective-permute-start | bytes 2359304 | tf_op jit(solution)/shard_map/ppermute | solution.py:330
  239.9 28.7 %collective-permute-start.36 = (bf16[6,2,1,64,512]{4,3,2,1,0:T(8,128)(2,1)}, bf16[6,2,1,64,512]{4,3,2,1,0:T(8,128)(2,1)S(1)}, u32[]{:S(2)}, u32[]{:S(2)}) collective-permute-start(bf16[6,2,1,64,512]{4,3,2,1,0:T(8,128)(2,1)} %get-tuple-element.133), channel_id=1, source_target_pairs={{0,4},{1,5},{2,6},{3,7},{4,0},{5,1},{6,2},{7,3},{8,12},{9,13},{10,... | collective-permute-start | bytes 2359304 | tf_op jit(solution)/shard_map/ppermute | solution.py:330
  248.8 3.1 %copy-start.12 = (bf16[6,2,1,64,512]{4,3,2,1,0:T(8,128)(2,1)}, bf16[6,2,1,64,512]{4,3,2,1,0:T(8,128)(2,1)S(1)}, u32[]{:S(2)}) copy-start(bf16[6,2,1,64,512]{4,3,2,1,0:T(8,128)(2,1)S(1)} %collective-permute-done.30.refs_4_.refs_6_) | copy-start | bytes 2359300
  253.9 27.2 %collective-permute-start.37 = (bf16[5,2,1,64,512]{4,3,2,1,0:T(8,128)(2,1)}, bf16[5,2,1,64,512]{4,3,2,1,0:T(8,128)(2,1)S(1)}, u32[]{:S(2)}, u32[]{:S(2)}) collective-permute-start(bf16[5,2,1,64,512]{4,3,2,1,0:T(8,128)(2,1)} %get-tuple-element.135), channel_id=1, source_target_pairs={{0,4},{1,5},{2,6},{3,7},{4,0},{5,1},{6,2},{7,3},{8,12},{9,13},{10,... | collective-permute-start | bytes 1966088 | tf_op jit(solution)/shard_map/ppermute | solution.py:330
  (10 other events, 9.0 us)
